TPU v7x, 32 devices: a whole 2x2x4 slice. The times are simulated.
32 devices in a mesh: grp: 4 (over y, x), seq: 8 (over z, core).
Axes of the slice: x: 2, y: 2, z: 4, core: 2. Of those that a mesh axis runs over, the one named last changes fastest.
Arguments:
- tokens: bfloat16 [12288, 1024], P(('grp', 'seq')), may hold values from -6 to 6
- valid: int32 [12288], P(('grp', 'seq')), may hold values from 0 to 1, as said below
- prompt_of: int32 [32], P(('grp', 'seq')), may hold values from 0 to 1, as said below
- teacher: bfloat16 [12288, 1024], P(('grp', 'seq')), may hold values from -8 to 8
- cotangent: bfloat16 [12288, 1024], P(('grp', 'seq')), may hold values from -6 to 6
- ln1_gain: bfloat16 [1024], P(('grp', 'seq')), may hold values from 0.25 to 1.75
- ln1_bias: bfloat16 [1024], P(('grp', 'seq')), may hold values from -1.75 to 1.75
- ln2_gain: bfloat16 [1024], P(('grp', 'seq')), may hold values from 0.25 to 1.75
- ln2_bias: bfloat16 [1024], P(('grp', 'seq')), may hold values from -1.75 to 1.75
- qkv_weight: bfloat16 [1024, 3072], P(('grp', 'seq')), may hold values from -0.25 to 0.25
- qkv_bias: bfloat16 [3072], P(('grp', 'seq')), may hold values from -1.75 to 1.75
- out_weight: bfloat16 [1024, 1024], P(('grp', 'seq')), may hold values from -1 to 1
- out_bias: bfloat16 [1024], P(('grp', 'seq')), may hold values from -1.75 to 1.75
- up_weight: bfloat16 [1024, 4096], P(('grp', 'seq')), may hold values from -0.1875 to 0.1875
- up_bias: bfloat16 [4096], P(('grp', 'seq')), may hold values from -1.75 to 1.75
- down_weight: bfloat16 [4096, 1024], P(('grp', 'seq')), may hold values from -0.1875 to 0.1875
- down_bias: bfloat16 [1024], P(('grp', 'seq')), may hold values from -1.75 to 1.75
Outputs:
- output: bfloat16 [12288, 1024], P(('grp', 'seq'))
- loss_value: float32 [], replicated
- input_grad: float32 [12288, 1024], P(('grp', 'seq'))
- ln1_gain_grad: float32 [1024], P(('grp', 'seq'))
- ln1_bias_grad: float32 [1024], P(('grp', 'seq'))
- ln2_gain_grad: float32 [1024], P(('grp', 'seq'))
- ln2_bias_grad: float32 [1024], P(('grp', 'seq'))
- qkv_weight_grad: float32 [1024, 3072], P(('grp', 'seq'))
- qkv_bias_grad: float32 [3072], P(('grp', 'seq'))
- out_weight_grad: float32 [1024, 1024], P(('grp', 'seq'))
- out_bias_grad: float32 [1024], P(('grp', 'seq'))
- up_weight_grad: float32 [1024, 4096], P(('grp', 'seq'))
- up_bias_grad: float32 [4096], P(('grp', 'seq'))
- down_weight_grad: float32 [4096, 1024], P(('grp', 'seq'))
- down_bias_grad: float32 [1024], P(('grp', 'seq'))
Inputs may be any that keep to these rules, and one draw needn't show every extreme that they name: Prompt tokens are all valid; the valid tokens of a continuation are a prefix of 1 to 512 tokens, and in each group one continuation is valid throughout. `prompt_of`: entries 2 * i and 2 * i + 1 of each group's 8 entries are equal; each group uses both prompts.
All inputs are finite; a program needn't handle non-finite values.
Results may differ from a plain program's by a relative error of at most 0.012.
The roundings to bfloat16 on the way count: a program that leaves them out, or rounds other values in their place, can miss the bound.
Values may be sent and summed in bfloat16 or wider, within the bound.
A program may use at most 320 MiB of HBM per device.

v0:
```python
import jax
import jax.numpy as jnp
from jax import lax
from jax.sharding import PartitionSpec as P

D = 1024
H = 16
HD = 64
ROT = 16
PSH = 64
CONT = 512


EPSILON = 1e-05
NEGATIVE = -1e30
SCALE = 0.125


def shifted(x, axis, by):
    length = lax.axis_size(axis)
    pairs = [(i, i + by) for i in range(length) if 0 <= i + by < length]
    return lax.ppermute(x, axis, pairs)


def normalize(values):
    center = values - jnp.mean(values, axis=-1, keepdims=True)
    inverse_dev = lax.rsqrt(jnp.mean(center * center, axis=-1, keepdims=True) + EPSILON)
    return (center * inverse_dev, inverse_dev)


def norm_back(incoming, normed, inverse_dev, scales):
    scaled = incoming * scales
    return inverse_dev * (
        scaled
        - jnp.mean(scaled, axis=-1, keepdims=True)
        - normed * jnp.mean(scaled * normed, axis=-1, keepdims=True)
    )


def rotate_heads(values, places, direction):
    halfrot = ROT // 2
    inverse = 10000.0 ** (-jnp.arange(halfrot, dtype=jnp.float32) / halfrot)
    angles = places.astype(jnp.float32)[..., None] * inverse
    cosine = jnp.cos(angles)[..., None, :]
    sine_part = direction * jnp.sin(angles)[..., None, :]
    leading = values[..., :halfrot]
    trailing = values[..., halfrot:ROT]
    return jnp.concatenate(
        [
            leading * cosine - trailing * sine_part,
            trailing * cosine + leading * sine_part,
            values[..., ROT:],
        ],
        axis=-1,
    )


def gelu_slope(values):
    return (
        0.5 * (1.0 + lax.erf(values * 0.7071067811865476))
        + values * jnp.exp(-0.5 * values * values) * 0.3989422804014327
    )


def prompt_scores(query_part, key_part, allowed):
    scores = (
        jnp.einsum("pqd,pkd->pqk", query_part, key_part, preferred_element_type=jnp.float32) * SCALE
    )
    return jnp.where(allowed[None], scores, NEGATIVE)


def cont_scores(query_part, chosen_keys, own_keys, allowed):
    far_scores = jnp.dot(query_part, chosen_keys.T, preferred_element_type=jnp.float32) * SCALE
    near_scores = jnp.dot(query_part, own_keys.T, preferred_element_type=jnp.float32) * SCALE
    return (far_scores, jnp.where(allowed, near_scores, NEGATIVE))


def body(
    tokens,
    valid,
    prompt_of,
    teacher,
    cotangent,
    ln1_gain,
    ln1_bias,
    ln2_gain,
    ln2_bias,
    qkv_weight,
    qkv_bias,
    out_weight,
    out_bias,
    up_weight,
    up_bias,
    down_weight,
    down_bias,
):
    gathered = (
        lax.all_gather(ln1_gain, ("grp", "seq"), axis=0, tiled=True),
        lax.all_gather(ln1_bias, ("grp", "seq"), axis=0, tiled=True),
        lax.all_gather(ln2_gain, ("grp", "seq"), axis=0, tiled=True),
        lax.all_gather(ln2_bias, ("grp", "seq"), axis=0, tiled=True),
        lax.all_gather(qkv_weight, ("grp", "seq"), axis=0, tiled=True),
        lax.all_gather(qkv_bias, ("grp", "seq"), axis=0, tiled=True),
        lax.all_gather(out_weight, ("grp", "seq"), axis=0, tiled=True),
        lax.all_gather(out_bias, ("grp", "seq"), axis=0, tiled=True),
        lax.all_gather(up_weight, ("grp", "seq"), axis=0, tiled=True),
        lax.all_gather(up_bias, ("grp", "seq"), axis=0, tiled=True),
        lax.all_gather(down_weight, ("grp", "seq"), axis=0, tiled=True),
        lax.all_gather(down_bias, ("grp", "seq"), axis=0, tiled=True),
    )
    (
        ln1_scale,
        ln1_offset,
        ln2_scale,
        ln2_offset,
        qkv_matrix,
        qkv_offset,
        out_matrix,
        out_offset,
        up_matrix,
        up_offset,
        down_matrix,
        down_offset,
    ) = gathered
    seats = lax.axis_size("seq")
    seat = lax.axis_index("seq")
    parity = seat % 2
    halfcont = CONT // 2
    prompt_len = PSH * seats
    row_count = tokens.shape[0]
    row_ids = jnp.arange(row_count, dtype=jnp.int32)
    places = jnp.where(
        row_ids < 2 * PSH,
        seat * PSH + row_ids % PSH,
        prompt_len + parity * halfcont + row_ids - 2 * PSH,
    )
    inputs = tokens.astype(jnp.float32)
    normed, inverse_dev = normalize(inputs)
    first_in = (normed * ln1_scale.astype(jnp.float32) + ln1_offset.astype(jnp.float32)).astype(
        jnp.bfloat16
    )
    second_in = (normed * ln2_scale.astype(jnp.float32) + ln2_offset.astype(jnp.float32)).astype(
        jnp.bfloat16
    )
    projected = jnp.dot(
        first_in, qkv_matrix, preferred_element_type=jnp.float32
    ) + qkv_offset.astype(jnp.float32)
    projected = projected.reshape(row_count, 3, H, HD)
    queries = rotate_heads(projected[:, 0], places, 1.0).astype(jnp.bfloat16)
    keys_now = rotate_heads(projected[:, 1], places, 1.0).astype(jnp.bfloat16)
    values_now = projected[:, 2].astype(jnp.bfloat16)
    pair_now = jnp.stack([keys_now, values_now], axis=1).reshape(row_count, 2 * D)
    prompt_pairs = lax.all_gather(pair_now[: 2 * PSH], "seq", axis=0, tiled=True)
    partner_pairs, partner_valid = shifted((pair_now[2 * PSH :], valid[2 * PSH :]), "seq", 1)
    prompt_heads = (
        prompt_pairs.reshape(seats, 2, PSH, 2, H, HD)
        .transpose(4, 3, 1, 0, 2, 5)
        .reshape(H, 2, 2, prompt_len, HD)
    )
    cont_pairs = jnp.concatenate([partner_pairs, pair_now[2 * PSH :]], axis=0)
    cont_heads = cont_pairs.reshape(2 * halfcont, 2, H, HD).transpose(2, 1, 0, 3)
    query_heads = queries.transpose(1, 0, 2)
    query_place = seat * PSH + jnp.arange(PSH)
    prompt_mask = jnp.arange(prompt_len)[None, :] <= query_place[:, None]
    cont_step = parity * halfcont + jnp.arange(halfcont)
    own_mask = (cont_step[None, :] <= cont_step[:, None]) & (valid[2 * PSH :] > 0)[None, :]
    partner_mask = jnp.broadcast_to(
        ((partner_valid > 0) & (parity == 1))[None, :], (halfcont, halfcont)
    )
    cont_mask = jnp.concatenate([partner_mask, own_mask], axis=1)
    chosen = prompt_of[0]
    pick_weight = (jnp.arange(2) == chosen).astype(jnp.float32)[:, None, None]

    def head_forward(operands):
        query_head, prompt_head, cont_head = operands
        prompt_query = query_head[: 2 * PSH].reshape(2, PSH, HD)
        scores = prompt_scores(prompt_query, prompt_head[0], prompt_mask)
        largest = jnp.max(scores, axis=-1, keepdims=True)
        weights = jnp.exp(scores - largest)
        totals = jnp.sum(weights, axis=-1, keepdims=True)
        probs = (weights / totals).astype(jnp.bfloat16)
        prompt_out = jnp.einsum(
            "pqk,pkd->pqd", probs, prompt_head[1], preferred_element_type=jnp.float32
        )
        prompt_lse = (largest + jnp.log(totals))[..., 0]
        chosen_pair = lax.dynamic_index_in_dim(prompt_head, chosen, 1, keepdims=False)
        cont_query = query_head[2 * PSH :]
        far_scores, near_scores = cont_scores(cont_query, chosen_pair[0], cont_head[0], cont_mask)
        cont_largest = jnp.maximum(
            jnp.max(far_scores, axis=-1, keepdims=True),
            jnp.max(near_scores, axis=-1, keepdims=True),
        )
        far_weights = jnp.exp(far_scores - cont_largest)
        near_weights = jnp.exp(near_scores - cont_largest)
        cont_totals = jnp.sum(far_weights, axis=-1, keepdims=True) + jnp.sum(
            near_weights, axis=-1, keepdims=True
        )
        cont_out = jnp.dot(
            (far_weights / cont_totals).astype(jnp.bfloat16),
            chosen_pair[1],
            preferred_element_type=jnp.float32,
        )
        cont_out = cont_out + jnp.dot(
            (near_weights / cont_totals).astype(jnp.bfloat16),
            cont_head[1],
            preferred_element_type=jnp.float32,
        )
        cont_lse = (cont_largest + jnp.log(cont_totals))[:, 0]
        return (
            jnp.concatenate([prompt_out.reshape(2 * PSH, HD), cont_out], axis=0),
            prompt_lse,
            cont_lse,
        )

    attn_heads, prompt_lse_all, cont_lse_all = lax.map(
        head_forward, (query_heads, prompt_heads, cont_heads)
    )
    attended = attn_heads.transpose(1, 0, 2).reshape(row_count, D).astype(jnp.bfloat16)
    attn_branch = jnp.dot(
        attended, out_matrix, preferred_element_type=jnp.float32
    ) + out_offset.astype(jnp.float32)
    hidden_pre = jnp.dot(
        second_in, up_matrix, preferred_element_type=jnp.float32
    ) + up_offset.astype(jnp.float32)
    activated = jax.nn.gelu(hidden_pre, approximate=False).astype(jnp.bfloat16)
    mlp_branch = jnp.dot(
        activated, down_matrix, preferred_element_type=jnp.float32
    ) + down_offset.astype(jnp.float32)
    output = inputs + attn_branch + mlp_branch
    live_rows = (valid > 0).astype(jnp.float32)[:, None]
    missed = output - teacher.astype(jnp.float32)
    count_all, squared_all = lax.psum(
        (jnp.sum(live_rows), jnp.sum(live_rows * missed * missed)), ("grp", "seq")
    )
    loss_value = squared_all / (count_all * D)
    out_grad = cotangent.astype(jnp.float32) + 2.0 / (count_all * D) * live_rows * missed
    out_low = out_grad.astype(jnp.bfloat16)
    back_weights = (
        lax.all_gather(ln1_gain, ("grp", "seq"), axis=0, tiled=True),
        lax.all_gather(ln1_bias, ("grp", "seq"), axis=0, tiled=True),
        lax.all_gather(ln2_gain, ("grp", "seq"), axis=0, tiled=True),
        lax.all_gather(ln2_bias, ("grp", "seq"), axis=0, tiled=True),
        lax.all_gather(qkv_weight, ("grp", "seq"), axis=0, tiled=True),
        lax.all_gather(qkv_bias, ("grp", "seq"), axis=0, tiled=True),
        lax.all_gather(out_weight, ("grp", "seq"), axis=0, tiled=True),
        lax.all_gather(out_bias, ("grp", "seq"), axis=0, tiled=True),
        lax.all_gather(up_weight, ("grp", "seq"), axis=0, tiled=True),
        lax.all_gather(up_bias, ("grp", "seq"), axis=0, tiled=True),
        lax.all_gather(down_weight, ("grp", "seq"), axis=0, tiled=True),
        lax.all_gather(down_bias, ("grp", "seq"), axis=0, tiled=True),
    )
    (
        ln1_back,
        unused_one,
        ln2_back,
        unused_two,
        qkv_back,
        unused_three,
        out_back,
        unused_four,
        up_back,
        unused_five,
        down_back,
        unused_six,
    ) = back_weights
    branch_bias_grad = jnp.sum(out_low.astype(jnp.float32), axis=0)
    out_matrix_grad = jnp.dot(attended.T, out_low, preferred_element_type=jnp.float32)
    down_matrix_grad = jnp.dot(activated.T, out_low, preferred_element_type=jnp.float32)
    attended_grad = jnp.dot(out_low, out_back.T, preferred_element_type=jnp.float32).astype(
        jnp.bfloat16
    )
    activated_grad = jnp.dot(out_low, down_back.T, preferred_element_type=jnp.float32)
    hidden_grad = (activated_grad * gelu_slope(hidden_pre)).astype(jnp.bfloat16)
    up_matrix_grad = jnp.dot(second_in.T, hidden_grad, preferred_element_type=jnp.float32)
    up_bias_grad = jnp.sum(hidden_grad.astype(jnp.float32), axis=0)
    second_grad = jnp.dot(hidden_grad, up_back.T, preferred_element_type=jnp.float32)

    def head_backward(operands):
        query_head, prompt_head, cont_head, grad_head, prompt_lse, cont_lse = operands
        prompt_query = query_head[: 2 * PSH].reshape(2, PSH, HD)
        prompt_grad = grad_head[: 2 * PSH].reshape(2, PSH, HD)
        scores = prompt_scores(prompt_query, prompt_head[0], prompt_mask)
        probs = jnp.exp(scores - prompt_lse[..., None])
        prob_grad = jnp.einsum(
            "pqd,pkd->pqk", prompt_grad, prompt_head[1], preferred_element_type=jnp.float32
        )
        inner = jnp.sum(probs * prob_grad, axis=-1, keepdims=True)
        score_grad = (probs * (prob_grad - inner)).astype(jnp.bfloat16)
        prompt_query_grad = (
            jnp.einsum(
                "pqk,pkd->pqd", score_grad, prompt_head[0], preferred_element_type=jnp.float32
            )
            * SCALE
        )
        prompt_key_grad = (
            jnp.einsum("pqk,pqd->pkd", score_grad, prompt_query, preferred_element_type=jnp.float32)
            * SCALE
        )
        prompt_value_grad = jnp.einsum(
            "pqk,pqd->pkd",
            probs.astype(jnp.bfloat16),
            prompt_grad,
            preferred_element_type=jnp.float32,
        )
        chosen_pair = lax.dynamic_index_in_dim(prompt_head, chosen, 1, keepdims=False)
        cont_query = query_head[2 * PSH :]
        cont_grad = grad_head[2 * PSH :]
        far_scores, near_scores = cont_scores(cont_query, chosen_pair[0], cont_head[0], cont_mask)
        far_probs = jnp.exp(far_scores - cont_lse[:, None])
        near_probs = jnp.exp(near_scores - cont_lse[:, None])
        far_prob_grad = jnp.dot(cont_grad, chosen_pair[1].T, preferred_element_type=jnp.float32)
        near_prob_grad = jnp.dot(cont_grad, cont_head[1].T, preferred_element_type=jnp.float32)
        cont_inner = jnp.sum(far_probs * far_prob_grad, axis=-1, keepdims=True) + jnp.sum(
            near_probs * near_prob_grad, axis=-1, keepdims=True
        )
        far_score_grad = (far_probs * (far_prob_grad - cont_inner)).astype(jnp.bfloat16)
        near_score_grad = (near_probs * (near_prob_grad - cont_inner)).astype(jnp.bfloat16)
        cont_query_grad = jnp.dot(
            far_score_grad, chosen_pair[0], preferred_element_type=jnp.float32
        )
        cont_query_grad = (
            cont_query_grad
            + jnp.dot(near_score_grad, cont_head[0], preferred_element_type=jnp.float32)
        ) * SCALE
        far_key_grad = (
            jnp.dot(far_score_grad.T, cont_query, preferred_element_type=jnp.float32) * SCALE
        )
        far_value_grad = jnp.dot(
            far_probs.astype(jnp.bfloat16).T, cont_grad, preferred_element_type=jnp.float32
        )
        near_key_grad = (
            jnp.dot(near_score_grad.T, cont_query, preferred_element_type=jnp.float32) * SCALE
        )
        near_value_grad = jnp.dot(
            near_probs.astype(jnp.bfloat16).T, cont_grad, preferred_element_type=jnp.float32
        )
        prompt_pair_grad = jnp.stack(
            [
                prompt_key_grad + pick_weight * far_key_grad[None],
                prompt_value_grad + pick_weight * far_value_grad[None],
            ]
        )
        cont_pair_grad = jnp.stack([near_key_grad, near_value_grad])
        query_grad = jnp.concatenate(
            [prompt_query_grad.reshape(2 * PSH, HD), cont_query_grad], axis=0
        )
        return (query_grad, prompt_pair_grad, cont_pair_grad)

    grad_heads = attended_grad.reshape(row_count, H, HD).transpose(1, 0, 2)
    query_grads, prompt_pair_grads, cont_pair_grads = lax.map(
        head_backward,
        (query_heads, prompt_heads, cont_heads, grad_heads, prompt_lse_all, cont_lse_all),
    )
    prompt_rows_grad = (
        prompt_pair_grads.reshape(H, 2, 2, seats, PSH, HD)
        .transpose(3, 2, 4, 1, 0, 5)
        .reshape(seats * 2 * PSH, 2 * D)
    )
    own_prompt_grad = lax.psum_scatter(
        prompt_rows_grad.astype(jnp.bfloat16), "seq", scatter_dimension=0, tiled=True
    ).astype(jnp.float32)
    cont_rows_grad = cont_pair_grads.transpose(2, 1, 0, 3).reshape(2 * halfcont, 2 * D)
    returned = shifted(cont_rows_grad[:halfcont].astype(jnp.bfloat16), "seq", -1).astype(
        jnp.float32
    )
    own_cont_grad = cont_rows_grad[halfcont:] + returned
    pair_grad = jnp.concatenate([own_prompt_grad, own_cont_grad], axis=0).reshape(
        row_count, 2, H, HD
    )
    query_grad = query_grads.transpose(1, 0, 2)
    projected_grad = jnp.stack(
        [
            rotate_heads(query_grad, places, -1.0),
            rotate_heads(pair_grad[:, 0], places, -1.0),
            pair_grad[:, 1],
        ],
        axis=1,
    )
    projected_grad = projected_grad.reshape(row_count, 3 * D).astype(jnp.bfloat16)
    qkv_matrix_grad = jnp.dot(first_in.T, projected_grad, preferred_element_type=jnp.float32)
    qkv_bias_grad = jnp.sum(projected_grad.astype(jnp.float32), axis=0)
    first_grad = jnp.dot(projected_grad, qkv_back.T, preferred_element_type=jnp.float32)
    input_grad = (
        out_grad
        + norm_back(first_grad, normed, inverse_dev, ln1_back.astype(jnp.float32))
        + norm_back(second_grad, normed, inverse_dev, ln2_back.astype(jnp.float32))
    )
    ln1_scale_grad = jnp.sum(first_grad * normed, axis=0)
    ln1_offset_grad = jnp.sum(first_grad, axis=0)
    ln2_scale_grad = jnp.sum(second_grad * normed, axis=0)
    ln2_offset_grad = jnp.sum(second_grad, axis=0)
    shares = (
        lax.psum_scatter(ln1_scale_grad, ("grp", "seq"), scatter_dimension=0, tiled=True),
        lax.psum_scatter(ln1_offset_grad, ("grp", "seq"), scatter_dimension=0, tiled=True),
        lax.psum_scatter(ln2_scale_grad, ("grp", "seq"), scatter_dimension=0, tiled=True),
        lax.psum_scatter(ln2_offset_grad, ("grp", "seq"), scatter_dimension=0, tiled=True),
        lax.psum_scatter(qkv_matrix_grad, ("grp", "seq"), scatter_dimension=0, tiled=True),
        lax.psum_scatter(qkv_bias_grad, ("grp", "seq"), scatter_dimension=0, tiled=True),
        lax.psum_scatter(out_matrix_grad, ("grp", "seq"), scatter_dimension=0, tiled=True),
        lax.psum_scatter(branch_bias_grad, ("grp", "seq"), scatter_dimension=0, tiled=True),
        lax.psum_scatter(up_matrix_grad, ("grp", "seq"), scatter_dimension=0, tiled=True),
        lax.psum_scatter(up_bias_grad, ("grp", "seq"), scatter_dimension=0, tiled=True),
        lax.psum_scatter(down_matrix_grad, ("grp", "seq"), scatter_dimension=0, tiled=True),
        lax.psum_scatter(branch_bias_grad, ("grp", "seq"), scatter_dimension=0, tiled=True),
    )
    return (
        output.astype(jnp.bfloat16),
        loss_value,
        input_grad,
        shares[0],
        shares[1],
        shares[2],
        shares[3],
        shares[4],
        shares[5],
        shares[6],
        shares[7],
        shares[8],
        shares[9],
        shares[10],
        shares[11],
    )


def solution(mesh):
    in_specs = (
        P(("grp", "seq"), None),
        P(("grp", "seq")),
        P(("grp", "seq")),
        P(("grp", "seq"), None),
        P(("grp", "seq"), None),
        P(("grp", "seq")),
        P(("grp", "seq")),
        P(("grp", "seq")),
        P(("grp", "seq")),
        P(("grp", "seq"), None),
        P(("grp", "seq")),
        P(("grp", "seq"), None),
        P(("grp", "seq")),
        P(("grp", "seq"), None),
        P(("grp", "seq")),
        P(("grp", "seq"), None),
        P(("grp", "seq")),
    )
    out_specs = (
        P(("grp", "seq"), None),
        P(),
        P(("grp", "seq"), None),
        P(("grp", "seq")),
        P(("grp", "seq")),
        P(("grp", "seq")),
        P(("grp", "seq")),
        P(("grp", "seq"), None),
        P(("grp", "seq")),
        P(("grp", "seq"), None),
        P(("grp", "seq")),
        P(("grp", "seq"), None),
        P(("grp", "seq")),
        P(("grp", "seq"), None),
        P(("grp", "seq")),
    )
    return jax.shard_map(body, mesh=mesh, in_specs=in_specs, out_specs=out_specs, check_vma=False)
```

profile of v0, /device:TPU:29, one launch (start us, length us, event | category | flops | bytes accessed | tf_op | source)
XLA Modules:
  0.0 1569.4 jit_solution(16576321543388665161)
XLA Ops:
  15.3 39.0 %all-reduce.15 = (bf16[1024]{0:T(1024)(128)(2,1)S(1)}, bf16[1024]{0:T(1024)(128)(2,1)S(1)}, bf16[3072]{0:T(1024)(128)(2,1)S(1)}, bf16[1024]{0:T(1024)(128)(2,1)S...) all-reduce(bf16[1024]{0:T(1024)(128)(2,1)S(1)} %dynamic-update-slic, ...), channel_id=1, replica_groups=mesh['grp'=4,'seq'=8] {'grp','seq'}, use_global_device_ids=true, to_apply=%add.5 | all-reduce | flops 9216 | bytes 36864
  57.4 23.3 %all-gather.7.cloned.1.call-done = bf16[1024,3072]{1,0:T(8,128)(2,1)} async-done(((bf16[32,3072]{1,0:T(8,128)(2,1)}), bf16[1024,3072]{1,0:T(8,128)(2,1)}) %all-gather.7.cloned.1.call-update) | async-done | bytes 6291472 | tf_op jit(solution)/shard_map/all_gather | solution.py:102
  80.6 7.9 convolution_add_fusion.3
  88.6 6.1 copy.64
  105.1 45.5 %psum.15 = f32[]{:T(128)} all-reduce(f32[]{:T(128)} %get-tuple-element.626), channel_id=1, replica_groups=mesh['grp'=4,'seq'=8] {'grp','seq'}, use_global_device_ids=true, to_apply=%region_13.14 | all-reduce | flops 1 | bytes 8 | tf_op jit(solution)/shard_map/psum | solution.py:232
  151.3 34.5 %all-gather = bf16[32,1,128]{2,1,0:T(2,128)(2,1)S(1)} all-gather(bf16[1,1,128]{2,1,0:T(2,128)(2,1)S(1)} %bitcast.399), channel_id=1, replica_groups=mesh['grp'=4,'seq'=8] {'grp','seq'}, dimensions={0}, use_global_device_ids=true | all-gather | bytes 8448 | tf_op jit(solution)/shard_map/all_gather | solution.py:107
  195.2 21.1 %fusion.61 = (bf16[384,4096]{1,0:T(8,128)(2,1)}, f32[384,4096]{1,0:T(8,128)}) fusion(f32[4096]{0:T(1024)S(1)} %bitcast.397, bf16[1024,4096]{1,0:T(8,128)(2,1)} %all-gather.13.cloned.1.call-done, bf16[384,1024]{1,0:T(8,128)(2,1)S(1)} %copy-done, f32[1024]{0:T(1024)S(1)} %convert_element_type.212, f32[1024]{0:T(1024)S(1)} %convert_element_type.211, ...), kind=kOutput, calls=%fused_computation.116 | convolution fusion | flops 3327393792 | bytes 18639872 | tf_op jit(solution)/shard_map/dot_general | solution.py:222
  216.3 25.1 %all-gather.15.cloned.1.call-done = bf16[4096,1024]{1,0:T(8,128)(2,1)} async-done(((bf16[128,1024]{1,0:T(8,128)(2,1)}), bf16[4096,1024]{1,0:T(8,128)(2,1)}) %all-gather.15.cloned.1.call-update) | async-done | bytes 8388624 | tf_op jit(solution)/shard_map/all_gather | solution.py:108
  241.4 8.9 fusion.123
  250.3 38.2 %all-gather.9.cloned.1.call-done = bf16[1024,2048]{0,1:T(8,128)(2,1)} async-done(((bf16[128,2048]{0,1:T(8,128)(2,1)}), bf16[1024,2048]{0,1:T(8,128)(2,1)}) %all-gather.9.cloned.1.call-update) | async-done | bytes 4194320 | tf_op jit(solution)/shard_map/all_gather | solution.py:153
  288.5 16.0 %reshape.471 = bf16[8,2,64,2,16,64]{2,1,0,5,4,3:T(2,128)(2,1)} reshape(bf16[1024,2048]{0,1:T(8,128)(2,1)} %all-gather.9.cloned.1.call-done) | data formatting | bytes 8388608 | tf_op jit(solution)/shard_map/reshape | solution.py:156
  304.5 8.8 copy.98
  313.3 11.9 reshape.472
  325.2 139.4 %while.38 = (s32[]{:T(128)}, bf16[16,384,64]{1,2,0:T(8,128)(2,1)S(1)}, f32[16,2,64]{2,1,0:T(2,128)S(1)}, f32[16,256]{1,0:T(8,128)S(1)}, bf16[16,384,64]{2,1,0:T(...) while((s32[]{:T(128)}, ...), condition=%wide.region_9.10_spmd.clone.clone, body=%wide.region_2.9_spmd.clone.sunk.clone | while | flops 86539904 | bytes 5303757 | solution.py:215
  464.7 5.3 convert_reduce_fusion.3
  473.1 314.6 %while.39 = (s32[]{:T(128)}, f32[16,384,64]{1,2,0:T(8,128)}, bf16[16,2,2,512,64]{3,4,2,1,0:T(8,128)(2,1)}, f32[16,2,512,64]{2,3,0,1:T(8,128)}, bf16[16,384,64]{2...) while((s32[]{:T(128)}, f32[16,384,64]{1,2,0:T(8,128)}, ...), condition=%wide.region_18.19_spmd.clone.clone, body=%wide.region_14.18_spmd.clone.sunk.clone | while | flops 213745280 | bytes 14174273 | solution.py:350
  787.8 11.2 convert_element_type.225
  799.0 11.8 copy.72
  810.8 12.5 convert_element_type.227
  824.7 3.3 fusion.125
  835.5 47.3 %reduce-scatter.6.cloned.1.call-done = bf16[128,2048]{1,0:T(8,128)(2,1)} async-done(((bf16[1024,2048]{1,0:T(8,128)(2,1)}), bf16[128,2048]{1,0:T(8,128)(2,1)}) %reduce-scatter.6.cloned.1.call-update) | async-done | bytes 524304 | tf_op jit(solution)/shard_map/reduce_scatter | solution.py:359
  890.1 6.8 fusion.116
  898.0 8.6 convert_reduce_fusion
  908.3 8.3 fusion.112
  916.6 10.4 fusion.126
  927.7 6.8 fusion.124
  934.6 6.6 fusion.97
  944.6 40.3 %all-reduce.14 = (f32[]{:T(128)}, f32[1024]{0:T(1024)S(1)}, f32[1024]{0:T(1024)S(1)}, f32[1024]{0:T(1024)S(1)}, f32[1024]{0:T(1024)S(1)}, /*index=5*/f32[3072]{0:T(1024)S(1)}, f32[1024]{0:T(1024)S(1)}, f32[4096]{0:T(1024)S(1)}) all-reduce(f32[]{:T(128)} %get-tuple-element.645, ...), channel_id=1, replica_groups=mesh['grp'=4,'seq'=8] {'grp','seq'}, use_global_device_ids=true, to_apply=%region_11.12 | all-reduce | flops 12289 | bytes 98312 | tf_op jit(solution)/shard_map/psum | solution.py:232
  989.1 24.2 %reduce-scatter.10.cloned.1.call-done = f32[32,1024]{1,0:T(8,128)} async-done(((f32[1024,1024]{1,0:T(8,128)}), f32[32,1024]{1,0:T(8,128)}) %reduce-scatter.10.cloned.1.call-update) | async-done | bytes 131088 | tf_op jit(solution)/shard_map/reduce_scatter | solution.py:399
  1013.3 171.7 %reduce-scatter.8.cloned.1.call-done = f32[32,3072]{1,0:T(8,128)} async-done(((f32[1024,3072]{1,0:T(8,128)}), f32[32,3072]{1,0:T(8,128)}) %reduce-scatter.8.cloned.1.call-update) | async-done | bytes 393232 | tf_op jit(solution)/shard_map/reduce_scatter | solution.py:397
  1185.0 188.2 %reduce-scatter.12.cloned.1.call-done = f32[32,4096]{1,0:T(8,128)} async-done(((f32[1024,4096]{1,0:T(8,128)}), f32[32,4096]{1,0:T(8,128)}) %reduce-scatter.12.cloned.1.call-update) | async-done | bytes 524304 | tf_op jit(solution)/shard_map/reduce_scatter | solution.py:401
  1373.3 187.2 %reduce-scatter.14.cloned.1.call-done = f32[128,1024]{1,0:T(8,128)} async-done(((f32[4096,1024]{1,0:T(8,128)}), f32[128,1024]{1,0:T(8,128)}) %reduce-scatter.14.cloned.1.call-update) | async-done | bytes 524304 | tf_op jit(solution)/shard_map/reduce_scatter | solution.py:403
  (873 shorter events, 511.3 us)
Async XLA Ops:
  7.2 73.5 %all-gather.7.cloned.1.call-start = ((), (), s32[]{:S(2)}) async-start(), calls=%async_computation.5 | async-start | bytes 6488064 | tf_op jit(solution)/shard_map/all_gather | solution.py:102
  7.9 187.3 %all-gather.13.cloned.1.call-start = ((), (), s32[]{:S(2)}) async-start(), calls=%async_computation.8 | async-start | bytes 8650752 | tf_op jit(solution)/shard_map/all_gather | solution.py:106
  8.7 232.7 %all-gather.15.cloned.1.call-start = ((), (), s32[]{:S(2)}) async-start(), calls=%async_computation.9 | async-start | bytes 8650752 | tf_op jit(solution)/shard_map/all_gather | solution.py:108
  9.4 279.1 %all-gather.9.cloned.1.call-start = ((), (), s32[]{:S(2)}) async-start(), calls=%async_computation.6 | async-start | bytes 4718592 | tf_op jit(solution)/shard_map/all_gather | solution.py:153
  98.3 1.1 copy-start.6
  98.3 2.3 copy-start.14
  99.6 51.7 %copy-start.17 = (bf16[128]{0:T(256)(128)(2,1)S(1)}, bf16[128]{0:T(256)(128)(2,1)}, u32[]{:S(2)}) copy-start(bf16[128]{0:T(256)(128)(2,1)} %param.35) | copy-start | bytes 772
  100.6 364.1 %all-gather.11.cloned.1.call-start = ((), (), s32[]{:S(2)}) async-start(), calls=%async_computation.7 | async-start | bytes 2162688 | tf_op jit(solution)/shard_map/all_gather | solution.py:104
  100.6 86.1 %collective-permute-start.1 = (s32[256]{0:T(256)S(1)}, s32[256]{0:T(256)S(1)}, u32[]{:S(2)}, u32[]{:S(2)}) collective-permute-start(s32[256]{0:T(256)S(1)} %slice.248), channel_id=1, source_target_pairs={{0,1},{1,2},{2,3},{3,4},{4,5},{5,6},{6,7},{8,9},{9,10},{10,11},{11... | collective-permute-start | bytes 3080 | tf_op jit(solution)/shard_map/ppermute | solution.py:22
  102.0 780.8 %reduce-scatter.6.cloned.1.call-start = ((), (), s32[]{:S(2)}) async-start(), calls=%async_computation.10 | async-start | bytes 4718592 | tf_op jit(solution)/shard_map/reduce_scatter | solution.py:359
  102.6 83.2 %copy-start.15 = (pred[384]{0:T(512)(128)(4,1)}, pred[384]{0:T(512)(128)(4,1)S(1)}, u32[]{:S(2)}) copy-start(pred[384]{0:T(512)(128)(4,1)S(1)} %get-tuple-element.627) | copy-start | bytes 1156
  103.7 86.5 %copy-start.5 = (bf16[256,2,16,64]{0,3,2,1:T(8,128)(2,1)}, bf16[256,2,16,64]{0,3,2,1:T(8,128)(2,1)S(1)}, u32[]{:S(2)}) copy-start(bf16[256,2,16,64]{0,3,2,1:T(8,128)(2,1)S(1)} %pad_maximum_fusion.1) | copy-start | bytes 3145732
  103.7 86.5 %collective-permute-start = (bf16[256,2048]{0,1:T(8,128)(2,1)S(1)}, bf16[256,2048]{0,1:T(8,128)(2,1)}, u32[]{:S(2)}, u32[]{:S(2)}) collective-permute-start(bf16[256,2048]{0,1:T(8,128)(2,1)S(1)} %bitcast.385), channel_id=1, source_target_pairs={{0,1},{1,2},{2,3},{3,4},{4,5},{5,6},{6,7},{8,9},{9,10},{10,11},{11... | collective-permute-start | bytes 3145736 | tf_op jit(solution)/shard_map/ppermute | solution.py:22
  192.0 3.2 copy-start
  313.3 11.9 copy-start.2
  464.6 5.4 copy-start.3
  464.7 6.2 copy-start.18
  470.0 0.9 copy-start.7
  823.3 1.1 copy-start.4
  823.3 1.4 copy-start.8
  823.4 190.0 %reduce-scatter.10.cloned.1.call-start = ((), (), s32[]{:S(2)}) async-start(), calls=%async_computation.12 | async-start | bytes 4325376 | tf_op jit(solution)/shard_map/reduce_scatter | solution.py:399
  828.1 357.0 %reduce-scatter.8.cloned.1.call-start = ((), (), s32[]{:S(2)}) async-start(), calls=%async_computation.11 | async-start | bytes 12976128 | tf_op jit(solution)/shard_map/reduce_scatter | solution.py:397
  829.8 5.4 collective-permute-start.2
  888.7 1.4 copy-start.1
  896.9 1.1 copy-start.9
  896.9 476.4 %reduce-scatter.12.cloned.1.call-start = ((), (), s32[]{:S(2)}) async-start(), calls=%async_computation.13 | async-start | bytes 17301504 | tf_op jit(solution)/shard_map/reduce_scatter | solution.py:401
  906.6 1.7 copy-start.10
  916.6 644.0 %reduce-scatter.14.cloned.1.call-start = ((), (), s32[]{:S(2)}) async-start(), calls=%async_computation.14 | async-start | bytes 17301504 | tf_op jit(solution)/shard_map/reduce_scatter | solution.py:403
  934.6 6.7 copy-start.11
  934.6 6.7 copy-start.12
  934.6 6.7 copy-start.13
  987.9 573.1 %copy-start.19 = (f32[32]{0:T(128)}, f32[32]{0:T(128)S(1)}, u32[]{:S(2)}) copy-start(f32[32]{0:T(128)S(1)} %dynamic-slice.17) | copy-start | bytes 388
  (1 other events, 0.7 us)
Sparse Core Ops, SparseCore 0:
  11.0 69.5 all-gather.6
  83.6 78.5 all-gather.12
  165.2 76.1 all-gather.14
  243.4 45.0 all-gather.8
  291.3 56.4 all-gather.10
  823.5 59.2 reduce-scatter.5
  885.6 127.6 reduce-scatter.9
  1019.9 165.0 reduce-scatter.7
  1188.0 185.2 reduce-scatter.11
  1376.1 184.3 reduce-scatter.13
where the time goes:
time: 1600 us; the launch traced here: 1570 us
  waiting for transfers between devices  708 us (44%)
  matrix products  445 us (28%)
  blocking collectives  159 us (10%)
  local copies, waits for them, and re-layouts  157 us (10%)
  other arithmetic  75 us (5%)
  between operations  18.3 us (1%)
    reduce_scatter x1, waiting for transfers between devices, body(): lax.psum_scatter(up_matrix_grad, ('grp', 'seq'), scatter_dimension=0, til...  188 us
    reduce_scatter x1, waiting for transfers between devices, body(): lax.psum_scatter(down_matrix_grad, ('grp', 'seq'), scatter_dimension=0, t...  187 us
    reduce_scatter x1, waiting for transfers between devices, body(): lax.psum_scatter(qkv_matrix_grad, ('grp', 'seq'), scatter_dimension=0, ti...  172 us
    psum x2, blocking collectives, body(): lax.psum((jnp.sum(live_rows), jnp.sum(live_rows * missed * missed)), ('gr...  85.8 us
    reduce_scatter x1, waiting for transfers between devices, body(): lax.psum_scatter(prompt_rows_grad.astype(jnp.bfloat16), 'seq', scatter_di...  47.3 us
    dot_general x32, matrix products, cont_scores(): jnp.dot(query_part, own_keys.T, preferred_element_type=jnp.float32) * SCALE  41.8 us
    unnamed x1, blocking collectives  39 us
    all_gather x1, waiting for transfers between devices, body(): prompt_pairs = lax.all_gather(pair_now[:2 * PSH], 'seq', axis=0, tiled=True)  38.2 us
  transfers between devices with their start and end apart: 13, of which 8 were waited for; matrix products, arithmetic and copies ran while one was open for 20% of the time, Pallas kernels for 0%

commit v1 on v0

v1 whole, which is shorter than its diff:
```python
import functools

import jax
import jax.numpy as jnp
import numpy as np
from jax import lax
from jax.experimental import pallas as pl
from jax.experimental.pallas import tpu as pltpu
from jax.sharding import Mesh
from jax.sharding import PartitionSpec as P

D = 1024
H = 16
HD = 64
ROT = 16
FF = 4096
PSH = 64
CONT = 512
HALF = CONT // 2
HC = H // 2 * HD
EPSILON = 1e-05
NEGATIVE = -1e30
SCALE = 0.125
BF = jnp.bfloat16
F32 = jnp.float32
ALL = ("grp", "chip", "core")
CHIPS = ("grp", "chip")


def swap_cores(x):
    return lax.ppermute(x, "core", [(0, 1), (1, 0)])


def pair_rows(own):
    both = lax.all_gather(own, "core", axis=0)
    prompts = both[:, : 2 * PSH].reshape((2, 2, PSH) + own.shape[1:])
    prompts = prompts.swapaxes(0, 1).reshape((4 * PSH,) + own.shape[1:])
    return jnp.concatenate([prompts, both[:, 2 * PSH :].reshape((CONT,) + own.shape[1:])], axis=0)


def split_rows(rows):
    prompts = rows[: 4 * PSH].reshape((2, 2, PSH) + rows.shape[1:]).swapaxes(0, 1)
    prompts = prompts.reshape((2, 2 * PSH) + rows.shape[1:])
    return jnp.concatenate([prompts, rows[4 * PSH :].reshape((2, HALF) + rows.shape[1:])], axis=1)


def normalize(values):
    center = values - jnp.mean(values, axis=-1, keepdims=True)
    inverse_dev = lax.rsqrt(jnp.mean(center * center, axis=-1, keepdims=True) + EPSILON)
    return (center * inverse_dev, inverse_dev)


def rotate_heads(values, places, direction):
    halfrot = ROT // 2
    inverse = 10000.0 ** (-jnp.arange(halfrot, dtype=F32) / halfrot)
    angles = places.astype(F32)[..., None] * inverse
    cosine = jnp.cos(angles)[..., None, :]
    sine_part = direction * jnp.sin(angles)[..., None, :]
    leading = values[..., :halfrot]
    trailing = values[..., halfrot:ROT]
    return jnp.concatenate(
        [
            leading * cosine - trailing * sine_part,
            trailing * cosine + leading * sine_part,
            values[..., ROT:],
        ],
        axis=-1,
    )


def gelu_slope(values):
    return (
        0.5 * (1.0 + lax.erf(values * 0.7071067811865476))
        + values * jnp.exp(-0.5 * values * values) * 0.3989422804014327
    )


def dot(a, b, contract):
    return lax.dot_general(a, b, ((contract[:1], contract[1:]), ((), ())), preferred_element_type=F32)


def g_weights(c, qkv_weight, out_weight, up_weight, down_weight):
    r = qkv_weight.shape[0]
    mine = functools.partial(lax.dynamic_index_in_dim, index=c, keepdims=False)
    both = lambda w: lax.all_gather(w, "core", axis=0, tiled=True)
    qkv = mine(both(qkv_weight).reshape(2 * r, 3, 2, HC), axis=2).reshape(2 * r, 3 * HC)
    qkv = lax.all_gather(qkv, CHIPS, axis=0, tiled=True)
    rd = down_weight.shape[0]
    up = mine(both(up_weight).reshape(2 * r, FF // (2 * rd), 2, rd), axis=2).reshape(2 * r, FF // 2)
    up = lax.all_gather(up, CHIPS, axis=0, tiled=True)
    down = lax.all_gather(down_weight, CHIPS, axis=0, tiled=True)
    out = lax.all_gather(out_weight, ALL, axis=0, tiled=True)
    out = mine(out.reshape(2, HC, D), axis=0)
    return qkv, out, up, down


def g_small(c, rd, ln1_gain, ln1_bias, ln2_gain, ln2_bias, qkv_bias, out_bias, up_bias, down_bias):
    sizes = [v.shape[0] for v in (ln1_gain, ln1_bias, ln2_gain, ln2_bias, out_bias, down_bias, qkv_bias, up_bias)]
    packed = jnp.concatenate([ln1_gain, ln1_bias, ln2_gain, ln2_bias, out_bias, down_bias, qkv_bias, up_bias])
    rows = lax.all_gather(packed, ALL, axis=0)
    parts, at = [], 0
    for size in sizes:
        parts.append(rows[:, at : at + size].reshape(-1).astype(F32))
        at += size
    qb = lax.dynamic_index_in_dim(parts[6].reshape(3, 2, HC), c, axis=1, keepdims=False).reshape(-1)
    ub = lax.dynamic_index_in_dim(parts[7].reshape(-1, 2, rd), c, axis=1, keepdims=False).reshape(-1)
    return parts[:6] + [qb, ub]


def places_of(z, chips):
    prompt = z * 2 * PSH + jnp.arange(2 * PSH)
    return jnp.concatenate([prompt, prompt, chips * 2 * PSH + jnp.arange(CONT)])


def masks_of(z, chips, cont_valid):
    length = chips * 2 * PSH
    prompt = jnp.arange(length)[None, :] <= z * 2 * PSH + jnp.arange(2 * PSH)[:, None]
    own = jnp.arange(CONT)[None, :] <= jnp.arange(CONT)[:, None]
    own = own & (cont_valid > 0)[None, :]
    return prompt, jnp.concatenate([jnp.ones((CONT, length), bool), own], axis=1)


def g_attention(q, prompt_kv, kv, chosen, masks):
    nh = HC // HD
    chips = prompt_kv.shape[0]
    pk = prompt_kv.reshape(chips, 2, 2 * PSH, 2, nh, HD).transpose(3, 4, 1, 0, 2, 5)
    pk = pk.reshape(2, nh, 2, chips * 2 * PSH, HD)
    qh = q.reshape(-1, nh, HD).swapaxes(0, 1)
    pq = qh[:, : 4 * PSH].reshape(nh, 2, 2 * PSH, HD)
    scores = jnp.einsum("hpqd,hpkd->hpqk", pq, pk[0], preferred_element_type=F32) * SCALE
    scores = jnp.where(masks[0], scores, NEGATIVE)
    top = jnp.max(scores, axis=-1, keepdims=True)
    weights = jnp.exp(scores - top)
    total = jnp.sum(weights, axis=-1, keepdims=True)
    p_out = jnp.einsum("hpqk,hpkd->hpqd", (weights / total).astype(BF), pk[1], preferred_element_type=F32)
    p_lse = (top + jnp.log(total))[..., 0].reshape(nh, 4 * PSH)
    far = lax.dynamic_index_in_dim(pk, chosen, axis=2, keepdims=False)
    near = kv[4 * PSH :].reshape(CONT, 2, nh, HD).transpose(1, 2, 0, 3)
    ck = jnp.concatenate([far, near], axis=2)
    cq = qh[:, 4 * PSH :]
    scores = jnp.einsum("hqd,hkd->hqk", cq, ck[0], preferred_element_type=F32) * SCALE
    scores = jnp.where(masks[1], scores, NEGATIVE)
    top = jnp.max(scores, axis=-1, keepdims=True)
    weights = jnp.exp(scores - top)
    total = jnp.sum(weights, axis=-1, keepdims=True)
    c_out = jnp.einsum("hqk,hkd->hqd", (weights / total).astype(BF), ck[1], preferred_element_type=F32)
    c_lse = (top + jnp.log(total))[..., 0]
    att = jnp.concatenate([p_out.reshape(nh, 4 * PSH, HD), c_out], axis=1)
    return att.swapaxes(0, 1).reshape(-1, HC).astype(BF), jnp.concatenate([p_lse, c_lse], axis=1)


def g_attention_back(q, prompt_kv, kv, att_grad, lse, chosen, masks):
    nh = HC // HD
    chips = prompt_kv.shape[0]
    pk = prompt_kv.reshape(chips, 2, 2 * PSH, 2, nh, HD).transpose(3, 4, 1, 0, 2, 5)
    pk = pk.reshape(2, nh, 2, chips * 2 * PSH, HD)
    qh = q.reshape(-1, nh, HD).swapaxes(0, 1)
    gh = att_grad.reshape(-1, nh, HD).swapaxes(0, 1)
    pq = qh[:, : 4 * PSH].reshape(nh, 2, 2 * PSH, HD)
    pg = gh[:, : 4 * PSH].reshape(nh, 2, 2 * PSH, HD)
    ein = functools.partial(jnp.einsum, preferred_element_type=F32)

    def back(eq, ek, query, key, value, grad, mask, lse_rows):
        scores = jnp.where(mask, ein(f"{eq},{ek}->{eq[:-1]}k", query, key) * SCALE, NEGATIVE)
        probs = jnp.exp(scores - lse_rows[..., None])
        prob_grad = ein(f"{eq},{ek}->{eq[:-1]}k", grad, value)
        inner = jnp.sum(probs * prob_grad, axis=-1, keepdims=True)
        score_grad = (probs * (prob_grad - inner)).astype(BF)
        es = eq[:-1] + "k"
        dq = ein(f"{es},{ek}->{eq}", score_grad, key) * SCALE
        dk = ein(f"{es},{eq}->{ek}", score_grad, query) * SCALE
        dv = ein(f"{es},{eq}->{ek}", probs.astype(BF), grad)
        return dq, dk, dv

    dq_p, dk_p, dv_p = back("hpqd", "hpkd", pq, pk[0], pk[1], pg, masks[0], lse[:, : 4 * PSH].reshape(nh, 2, 2 * PSH))
    far = lax.dynamic_index_in_dim(pk, chosen, axis=2, keepdims=False)
    near = kv[4 * PSH :].reshape(CONT, 2, nh, HD).transpose(1, 2, 0, 3)
    ck = jnp.concatenate([far, near], axis=2)
    dq_c, dk_c, dv_c = back("hqd", "hkd", qh[:, 4 * PSH :], ck[0], ck[1], gh[:, 4 * PSH :], masks[1], lse[:, 4 * PSH :])
    length = chips * 2 * PSH
    pick = (jnp.arange(2) == chosen).astype(F32)[None, :, None, None]
    dk_p = dk_p + pick * dk_c[:, None, :length]
    dv_p = dv_p + pick * dv_c[:, None, :length]
    dq = jnp.concatenate([dq_p.reshape(nh, 4 * PSH, HD), dq_c], axis=1).swapaxes(0, 1).reshape(-1, HC)
    pair = jnp.stack([dk_p, dv_p])
    pair = pair.reshape(2, nh, 2, chips, 2 * PSH, HD).transpose(3, 2, 4, 0, 1, 5).reshape(chips * 4 * PSH, 2 * HC)
    near_grad = jnp.stack([dk_c[:, length:], dv_c[:, length:]]).transpose(2, 0, 1, 3).reshape(CONT, 2 * HC)
    return dq, pair, near_grad


def generic_body(
    tokens, valid, prompt_of, teacher, cotangent,
    ln1_gain, ln1_bias, ln2_gain, ln2_bias, qkv_weight, qkv_bias, out_weight, out_bias,
    up_weight, up_bias, down_weight, down_bias, stop=None,
):
    c = lax.axis_index("core")
    z = lax.axis_index("chip")
    chips = lax.axis_size("chip")
    nh = HC // HD
    rd = down_weight.shape[0]
    device = lax.axis_index(ALL)
    w_qkv, w_out, w_up, w_down = g_weights(c, qkv_weight, out_weight, up_weight, down_weight)
    gain1, bias1, gain2, bias2, b_out, b_down, b_qkv, b_up = g_small(
        c, rd, ln1_gain, ln1_bias, ln2_gain, ln2_bias, qkv_bias, out_bias, up_bias, down_bias
    )
    x = pair_rows(tokens).astype(F32)
    normed, rstd = normalize(x)
    first_in = (normed * gain1 + bias1).astype(BF)
    second_in = (normed * gain2 + bias2).astype(BF)
    projected = dot(first_in, w_qkv, (1, 0)) + b_qkv
    places = places_of(z, chips)
    turn = lambda v, d: rotate_heads(v.reshape(-1, nh, HD), places, d).reshape(-1, HC)
    q = turn(projected[:, :HC], 1.0).astype(BF)
    k = turn(projected[:, HC : 2 * HC], 1.0).astype(BF)
    kv = jnp.concatenate([k, projected[:, 2 * HC :].astype(BF)], axis=1)
    prompt_kv = lax.all_gather(kv[: 4 * PSH].reshape(2, 2 * PSH, 2 * HC), "chip", axis=0)
    cont_valid = lax.all_gather(valid[2 * PSH :], "core", axis=0, tiled=True)
    masks = masks_of(z, chips, cont_valid)
    chosen = prompt_of[0]
    attended, lse = g_attention(q, prompt_kv, kv, chosen, masks)
    hidden_pre = dot(second_in, w_up, (1, 0)) + b_up
    activated = jax.nn.gelu(hidden_pre, approximate=False).astype(BF)
    partial = dot(attended, w_out, (1, 0)) + dot(activated, w_down, (1, 0))
    halves = split_rows(partial)
    take = lambda a: lax.dynamic_index_in_dim(a, c, axis=0, keepdims=False)
    give = lambda a: lax.dynamic_index_in_dim(a, 1 - c, axis=0, keepdims=False)
    output = tokens.astype(F32) + take(halves) + swap_cores(give(halves)) + b_out + b_down
    live = (valid > 0).astype(F32)[:, None]
    missed = output - teacher.astype(F32)
    count_all, squared_all = lax.psum((jnp.sum(live), jnp.sum(live * missed * missed)), ALL)
    loss_value = squared_all / (count_all * D)
    out_grad = cotangent.astype(F32) + 2.0 / (count_all * D) * live * missed
    out_low = pair_rows(out_grad.astype(BF))
    if stop == "fwd":
        return output, out_grad, out_low, attended, lse, activated, q, kv, first_in, second_in
    out_bias_grad = jnp.sum(out_grad.astype(BF).astype(F32), axis=0)
    dw_out = dot(attended, out_low, (0, 0))
    dw_down = dot(activated, out_low, (0, 0))
    att_grad = dot(out_low, w_out, (1, 1)).astype(BF)
    hidden_grad = (dot(out_low, w_down, (1, 1)) * gelu_slope(hidden_pre)).astype(BF)
    dw_up = dot(second_in, hidden_grad, (0, 0))
    db_up = jnp.sum(hidden_grad.astype(F32), axis=0)
    second_grad = dot(hidden_grad, w_up, (1, 1))
    dq, pair, near = g_attention_back(q, prompt_kv, kv, att_grad, lse, chosen, masks)
    own_pair = lax.psum_scatter(pair.astype(BF), "chip", scatter_dimension=0, tiled=True).astype(F32)
    pair = jnp.concatenate([own_pair, near], axis=0)
    projected_grad = jnp.concatenate([turn(dq, -1.0), turn(pair[:, :HC], -1.0), pair[:, HC:]], axis=1).astype(BF)
    dw_qkv = dot(first_in, projected_grad, (0, 0))
    db_qkv = jnp.sum(projected_grad.astype(F32), axis=0)
    first_grad = dot(projected_grad, w_qkv, (1, 1))
    if stop == "bwd":
        return dw_out, dw_down, dw_up, dw_qkv, second_grad, first_grad, projected_grad, hidden_grad, att_grad
    joint = first_grad * gain1 + second_grad * gain2
    halves = split_rows(joint)
    joint = take(halves) + swap_cores(give(halves))
    own_normed = take(split_rows(normed))
    own_rstd = take(split_rows(rstd))
    input_grad = out_grad + own_rstd * (
        joint
        - jnp.mean(joint, axis=-1, keepdims=True)
        - own_normed * jnp.mean(joint * own_normed, axis=-1, keepdims=True)
    )
    wide = lambda v, n: jnp.zeros((v.shape[0], 2, v.shape[1]), F32).at[:, c].set(v).reshape(-1)
    small = jnp.concatenate(
        [
            jnp.sum(first_grad * normed, axis=0),
            jnp.sum(first_grad, axis=0),
            jnp.sum(second_grad * normed, axis=0),
            jnp.sum(second_grad, axis=0),
            out_bias_grad,
            wide(db_qkv.reshape(3, HC), 3),
            wide(db_up.reshape(-1, rd), 16),
        ]
    )
    small = lax.psum(small, ALL)
    shares, at = [], 0
    for size in (D, D, D, D, D, 3 * D, FF):
        own = size // lax.axis_size(ALL)
        shares.append(lax.dynamic_slice_in_dim(small, at + device * own, own))
        at += size
    rs = lambda v: lax.psum_scatter(v.astype(BF), CHIPS, scatter_dimension=0, tiled=True).astype(F32)
    r = qkv_weight.shape[0]
    s_qkv = rs(dw_qkv).reshape(2, r, 3, HC)
    s_up = rs(dw_up).reshape(2, r, FF // (2 * rd), rd)
    s_down = rs(dw_down)
    pairs = lambda own, other, axis: jnp.where(c == 0, jnp.stack([own, other], axis), jnp.stack([other, own], axis))
    s_qkv = pairs(take(s_qkv), swap_cores(give(s_qkv)), 2).reshape(r, 3 * D)
    s_up = pairs(take(s_up), swap_cores(give(s_up)), 2).reshape(r, FF)
    o = dw_out.reshape(H // 2, -1, 2, r, D)
    o_own = lax.dynamic_index_in_dim(o, c, axis=2, keepdims=False)
    o_other = swap_cores(lax.dynamic_index_in_dim(o, 1 - c, axis=2, keepdims=False))
    s_out = rs(pairs(o_own, o_other, 0).reshape(-1, D))
    return (
        output.astype(BF), loss_value, input_grad, shares[0], shares[1], shares[2], shares[3],
        s_qkv, shares[5], s_out, shares[4], s_up, shares[6], s_down, shares[4],
    )


def solution(mesh):
    groups, seats = mesh.shape["grp"], mesh.shape["seq"]
    fine = Mesh(mesh.devices.reshape(groups, seats // 2, 2), ALL)
    rows, row = P(ALL, None), P(ALL)
    in_specs = (rows, row, row, rows, rows) + (row,) * 4 + (rows, row) * 4
    out_specs = (rows, P(), rows) + (row,) * 4 + (rows, row) * 4
    return jax.shard_map(generic_body, mesh=fine, in_specs=in_specs, out_specs=out_specs, check_vma=False)
```

time: 1600 us -> 965 us (0.60)
  matrix products: 445 us -> 128 us
  waiting for transfers between devices: 708 us -> 522 us
  local copies, waits for them, and re-layouts: 157 us -> 92.5 us
  blocking collectives: 159 us -> 122 us
    dot_general x348 -> x24, matrix products: 445 us -> 128 us  [the longest x12 81.4 us: dot(): lax.dot_general(a, b, ((contract[:1], contract[1:]), ((), ())), preferred...]
    reduce_scatter x5, waiting for transfers between devices: 619 us -> 314 us  [the longest x4 308 us: generic_body(): lax.psum_scatter(v.astype(BF), CHIPS, scatter_dimension=0, tiled=True)]
    all_gather x5 -> x7, waiting for transfers between devices: 86.6 us -> 204 us  [the longest x1 55.2 us: g_weights(): down = lax.all_gather(down_weight, CHIPS, axis=0, tiled=True)]
    dynamic_update_slice x80 -> x0, other arithmetic: 34.4 us -> none  [the longest x32 23.2 us: body(): lax.map(head_backward, (query_heads, prompt_heads, cont_heads, grad_heads...]
    reshape x35 -> x11, local copies, waits for them, and re-layouts: 39.1 us -> 6.82 us  [the longest x1 4.59 us: g_attention(): pk = pk.reshape(2, nh, 2, chips * 2 * PSH, HD)]
    convert_element_type x5 -> x10, local copies, waits for them, and re-layouts: 38.9 us -> 9.79 us  [the longest x2 8.99 us: generic_body(): pair.astype(BF)]
    all_gather x1 -> x3, blocking collectives: 34.5 us -> 7.28 us  [the longest x2 4.92 us: g_weights(): both = lambda w: lax.all_gather(w, 'core', axis=0, tiled=True)]
    convert_element_type x42 -> x14, other arithmetic: 4.34 us -> 24.5 us  [the longest x2 12.8 us: back(): score_grad = (probs * (prob_grad - inner)).astype(BF)]
  transfers between devices with their start and end apart: 13 -> 17, of which waited for: 8 -> 12; matrix products, arithmetic and copies ran while one was open for 20% -> 20% of each run, Pallas kernels for 0% -> 0%
where the time goes in v1:
time: 965 us; the launch traced here: 950 us
  waiting for transfers between devices  522 us (54%)
  matrix products  128 us (13%)
  blocking collectives  122 us (13%)
  local copies, waits for them, and re-layouts  92.5 us (10%)
  other arithmetic  60.3 us (6%)
  between operations  19.2 us (2%)
    reduce_scatter x4, waiting for transfers between devices, generic_body(): lax.psum_scatter(v.astype(BF), CHIPS, scatter_dimension=0, tiled=True)  308 us
    dot_general x12, matrix products, dot(): lax.dot_general(a, b, ((contract[:1], contract[1:]), ((), ())), preferred...  81.4 us
    psum x2, blocking collectives, generic_body(): lax.psum((jnp.sum(live), jnp.sum(live * missed * missed)), ALL)  76.6 us
    all_gather x1, waiting for transfers between devices, g_weights(): down = lax.all_gather(down_weight, CHIPS, axis=0, tiled=True)  55.2 us
    all_gather x1, waiting for transfers between devices, g_weights(): up = lax.all_gather(up, CHIPS, axis=0, tiled=True)  50.4 us
    unnamed x1, blocking collectives  38.4 us
    all_gather x1, waiting for transfers between devices, generic_body(): lax.all_gather(kv[:4 * PSH].reshape(2, 2 * PSH, 2 * HC), 'chip', axis=0)  37.8 us
    all_gather x1, waiting for transfers between devices, g_weights(): qkv = lax.all_gather(qkv, CHIPS, axis=0, tiled=True)  29.6 us
  transfers between devices with their start and end apart: 17, of which 12 were waited for; matrix products, arithmetic and copies ran while one was open for 20% of the time, Pallas kernels for 0%

profile of v1, /device:TPU:29, one launch (start us, length us, event | category | flops | bytes accessed | tf_op | source)
XLA Modules:
  0.0 949.9 jit_solution(4237720769104675188)
XLA Ops:
  19.1 38.4 %all-reduce.1 = bf16[13312]{0:T(1024)(128)(2,1)S(1)} all-reduce(bf16[13312]{0:T(1024)(128)(2,1)S(1)} %dynamic-update-slice.6), channel_id=3, replica_groups=mesh['grp'=4,'chip'=4,'core'=2] {'grp','chip','core'}, use_global_device_ids=true, to_apply=%add.1 | all-reduce | flops 13312 | bytes 53248
  62.9 29.6 %all-gather.12.cloned.1.call-done = bf16[1024,1536]{1,0:T(8,128)(2,1)} async-done(((bf16[64,1536]{1,0:T(8,128)(2,1)}), bf16[1024,1536]{1,0:T(8,128)(2,1)}) %all-gather.12.cloned.1.call-update) | async-done | bytes 3145744 | tf_op jit(solution)/shard_map/all_gather | solution.py:87
  92.4 4.6 convolution_add_fusion
  120.0 50.4 %all-gather.18.cloned.1.call-done = bf16[1024,2048]{1,0:T(8,128)(2,1)} async-done(((bf16[64,2048]{1,0:T(8,128)(2,1)}), bf16[1024,2048]{1,0:T(8,128)(2,1)}) %all-gather.18.cloned.1.call-update) | async-done | bytes 4194320 | tf_op jit(solution)/shard_map/all_gather | solution.py:90
  170.4 21.9 %fusion.8 = (bf16[768,2048]{1,0:T(8,128)(2,1)}, f32[768,2048]{1,0:T(8,128)}) fusion(f32[2048]{0:T(1024)S(1)} %bitcast.328, bf16[1024,2048]{1,0:T(8,128)(2,1)} %all-gather.18.cloned.1.call-done, f32[1024]{0:T(1024)S(1)} %reshape.613, f32[1024]{0:T(1024)S(1)} %reshape.612, f32[768]{0:T(1024)S(1)} %add_rsqrt_fusion, f32[768]{0:T(1024)S(1)} %broadcast_multiply_fusion.1, ...), kind=kOutput, calls=%fused_computation.15 | convolution fusion | flops 3332112384 | bytes 15226880 | tf_op jit(solution)/shard_map/dot_general | solution.py:79
  192.3 55.2 %all-gather.20.cloned.1.call-done = bf16[2048,1024]{1,0:T(8,128)(2,1)} async-done(((bf16[128,1024]{1,0:T(8,128)(2,1)}), bf16[2048,1024]{1,0:T(8,128)(2,1)}) %all-gather.20.cloned.1.call-update) | async-done | bytes 4194320 | tf_op jit(solution)/shard_map/all_gather | solution.py:91
  247.5 8.2 fusion.104
  255.8 37.8 %all-gather.14.cloned.1.call-done = bf16[4,2,128,1024]{3,2,1,0:T(8,128)(2,1)} async-done(((bf16[1,2,128,1024]{3,2,1,0:T(8,128)(2,1)}), bf16[4,2,128,1024]{3,2,1,0:T(8,128)(2,1)}) %all-gather.14.cloned.1.call-update) | async-done | bytes 2097168 | tf_op jit(solution)/shard_map/all_gather | solution.py:216
  301.5 4.6 reshape.573
  333.3 19.6 %all-gather.16.cloned.1.call-done = bf16[1024,1024]{1,0:T(8,128)(2,1)} async-done(((bf16[32,1024]{1,0:T(8,128)(2,1)}), bf16[1024,1024]{1,0:T(8,128)(2,1)}) %all-gather.16.cloned.1.call-update) | async-done | bytes 2097168 | tf_op jit(solution)/shard_map/all_gather | solution.py:92
  359.7 38.0 %psum.22 = f32[]{:T(128)} all-reduce(f32[]{:T(128)} %get-tuple-element.51), channel_id=1, replica_groups=mesh['grp'=4,'chip'=4,'core'=2] {'grp','chip','core'}, use_global_device_ids=true, to_apply=%region_9.10 | all-reduce | flops 1 | bytes 8 | tf_op jit(solution)/shard_map/psum | solution.py:230
  398.6 5.1 convert_reduce_fusion.3
  404.9 11.7 %all-gather.24.cloned.1.call-done = bf16[768,1024]{1,0:T(8,128)(2,1)} async-done(((bf16[384,1024]{1,0:T(8,128)(2,1)}), bf16[768,1024]{1,0:T(8,128)(2,1)}) %all-gather.24.cloned.1.call-update) | async-done | bytes 1572880 | tf_op jit(solution)/shard_map/all_gather | solution.py:35
  421.1 8.8 fusion.2
  429.9 10.0 %multiply_reduce_fusion = (f32[8,512]{1,0:T(8,128)}, f32[8,512,1024]{2,1,0:T(8,128)}) fusion(f32[8,512,1024]{2,1,0:T(8,128)S(1)} %bitcast.232, f32[8,512]{1,0:T(8,128)} %log_add_fusion, bf16[2,8,512,64]{2,3,1,0:T(8,128)(2,1)} %bitcast.265, bf16[2,8,512,64]{2,3,1,0:T(8,128)(2,1)} %copy-done.21, bf16[8,768,64]{1,2,0:T(8,128)(2,1)} %bitcast.280), kind=kOutput, calls=%fused_computation.1 | convolution fusion | flops 551546880 | bytes 36208640 | tf_op jit(solution)/shard_map/hqd,hkd->hqk/dot_general | solution.py:166
  442.8 4.7 multiply_reduce_fusion.1
  450.7 11.8 %multiply_convert_fusion = bf16[8,512,1024]{2,1,0:T(8,128)(2,1)S(1)} fusion(f32[8,512,1024]{2,1,0:T(8,128)} %get-tuple-element.107, f32[8,512,1024]{2,1,0:T(8,128)} %copy-done, f32[8,512]{1,0:T(8,128)S(1)} %copy-done.48, f32[8,512]{1,0:T(8,128)S(1)} %copy-done.44), kind=kLoop, calls=%fused_computation | loop fusion | flops 16777216 | bytes 41975808 | tf_op jit(solution)/shard_map/convert_element_type | solution.py:168
  477.5 4.6 copy.118
  495.4 9.1 convert_reduce_fusion
  506.3 5.7 convolution_convert_fusion.2
  514.8 6.1 convolution_multiply_fusion.1
  523.4 6.0 reduce-scatter.6.cloned.1.call-done
  532.7 4.7 convolution_convert_fusion
  537.6 7.8 convolution_convert_fusion.1
  545.5 6.4 fusion.105
  552.0 6.1 fusion.92
  562.4 29.4 %reduce-scatter.10.cloned.1.call-done = bf16[32,1024]{1,0:T(8,128)(2,1)} async-done(((bf16[512,1024]{1,0:T(8,128)(2,1)}), bf16[32,1024]{1,0:T(8,128)(2,1)}) %reduce-scatter.10.cloned.1.call-update) | async-done | bytes 65552 | tf_op jit(solution)/shard_map/reduce_scatter | solution.py:281
  603.5 99.4 %reduce-scatter.12.cloned.1.call-done = bf16[64,2048]{1,0:T(8,128)(2,1)} async-done(((bf16[1024,2048]{1,0:T(8,128)(2,1)}), bf16[64,2048]{1,0:T(8,128)(2,1)}) %reduce-scatter.12.cloned.1.call-update) | async-done | bytes 262160 | tf_op jit(solution)/shard_map/reduce_scatter | solution.py:281
  706.0 4.7 multiply_add_fusion.1
  710.7 38.6 %all-reduce.2 = (f32[]{:T(128)}, f32[12288]{0:T(1024)S(1)}) all-reduce(f32[]{:T(128)} %get-tuple-element.59, f32[12288]{0:T(1024)S(1)} %constant_dynamic-update-slice_fusion), channel_id=1, replica_groups=mesh['grp'=4,'chip'=4,'core'=2] {'grp','chip','core'}, use_global_device_ids=true, to_apply=%region_7.8 | all-reduce | flops 12289 | bytes 98312 | tf_op jit(solution)/shard_map/psum | solution.py:230
  751.2 87.0 %reduce-scatter.8.cloned.1.call-done = bf16[64,1536]{1,0:T(8,128)(2,1)} async-done(((bf16[1024,1536]{1,0:T(8,128)(2,1)}), bf16[64,1536]{1,0:T(8,128)(2,1)}) %reduce-scatter.8.cloned.1.call-update) | async-done | bytes 196624 | tf_op jit(solution)/shard_map/reduce_scatter | solution.py:281
  842.6 92.2 %reduce-scatter.14.cloned.1.call-done = bf16[128,1024]{1,0:T(8,128)(2,1)} async-done(((bf16[2048,1024]{1,0:T(8,128)(2,1)}), bf16[128,1024]{1,0:T(8,128)(2,1)}) %reduce-scatter.14.cloned.1.call-update) | async-done | bytes 262160 | tf_op jit(solution)/shard_map/reduce_scatter | solution.py:281
  (389 shorter events, 162.8 us)
Async XLA Ops:
  7.2 52.4 %all-gather.22.cloned.1.call-start = ((), (), s32[]{:S(2)}) async-start(), calls=%async_computation.15 | async-start | bytes 2359296 | tf_op jit(solution)/shard_map/all_gather | solution.py:35
  7.9 84.5 %all-gather.12.cloned.1.call-start = ((), (), s32[]{:S(2)}) async-start(), calls=%async_computation.5 | async-start | bytes 3342336 | tf_op jit(solution)/shard_map/all_gather | solution.py:87
  13.1 157.3 %all-gather.18.cloned.1.call-start = ((), (), s32[]{:S(2)}) async-start(), calls=%async_computation.8 | async-start | bytes 4456448 | tf_op jit(solution)/shard_map/all_gather | solution.py:90
  18.1 229.5 %all-gather.20.cloned.1.call-start = ((), (), s32[]{:S(2)}) async-start(), calls=%async_computation.9 | async-start | bytes 4456448 | tf_op jit(solution)/shard_map/all_gather | solution.py:91
  18.6 274.9 %all-gather.14.cloned.1.call-start = ((), (), s32[]{:S(2)}) async-start(), calls=%async_computation.6 | async-start | bytes 2621440 | tf_op jit(solution)/shard_map/all_gather | solution.py:216
  58.6 33.8 %copy-start.64 = (f32[1024]{0:T(1024)}, f32[1024]{0:T(1024)S(1)}, u32[]{:S(2)}) copy-start(f32[1024]{0:T(1024)S(1)} %reshape.609) | copy-start | bytes 12292
  58.7 33.7 %copy-start.66 = (f32[1024]{0:T(1024)}, f32[1024]{0:T(1024)S(1)}, u32[]{:S(2)}) copy-start(f32[1024]{0:T(1024)S(1)} %reshape.610) | copy-start | bytes 12292
  62.0 30.5 %copy-start.16 = (bf16[2,2,64,1024]{3,2,0,1:T(8,128)(2,1)}, bf16[2,2,64,1024]{3,2,0,1:T(8,128)(2,1)S(1)}, u32[]{:S(2)}) copy-start(bf16[2,2,64,1024]{3,2,0,1:T(8,128)(2,1)S(1)} %copy.98) | copy-start | bytes 1572868
  62.3 108.1 %copy-start.53 = (f32[768]{0:T(1024)}, f32[768]{0:T(1024)S(1)}, u32[]{:S(2)}) copy-start(f32[768]{0:T(1024)S(1)} %broadcast_multiply_fusion.1) | copy-start | bytes 9220
  62.9 107.5 %copy-start.56 = (f32[768]{0:T(1024)}, f32[768]{0:T(1024)S(1)}, u32[]{:S(2)}) copy-start(f32[768]{0:T(1024)S(1)} %add_rsqrt_fusion) | copy-start | bytes 9220
  111.5 58.9 %copy-start.17 = (bf16[2,2,64,1024]{3,2,0,1:T(8,128)(2,1)S(1)}, bf16[2,2,64,1024]{3,2,0,1:T(8,128)(2,1)}, u32[]{:S(2)}) copy-start(bf16[2,2,64,1024]{3,2,0,1:T(8,128)(2,1)} %copy-done.16) | copy-start | bytes 1572868
  111.5 241.4 %all-gather.16.cloned.1.call-start = ((), (), s32[]{:S(2)}) async-start(), calls=%async_computation.7 | async-start | bytes 2162688 | tf_op jit(solution)/shard_map/all_gather | solution.py:92
  112.1 304.4 %all-gather.24.cloned.1.call-start = ((), (), s32[]{:S(2)}) async-start(), calls=%async_computation.16 | async-start | bytes 2359296 | tf_op jit(solution)/shard_map/all_gather | solution.py:35
  115.4 76.9 %copy-start.58 = (f32[16,1,128]{2,1,0:T(1,128)}, f32[16,1,128]{2,1,0:T(1,128)S(1)}, u32[]{:S(2)}) copy-start(f32[16,1,128]{2,1,0:T(1,128)S(1)} %dynamic-slice_convert_fusion) | copy-start | bytes 24580
  115.5 76.8 %copy-start.68 = (f32[1024]{0:T(1024)}, f32[1024]{0:T(1024)S(1)}, u32[]{:S(2)}) copy-start(f32[1024]{0:T(1024)S(1)} %reshape.612) | copy-start | bytes 12292
  115.6 76.7 %copy-start.71 = (f32[1024]{0:T(1024)}, f32[1024]{0:T(1024)S(1)}, u32[]{:S(2)}) copy-start(f32[1024]{0:T(1024)S(1)} %reshape.613) | copy-start | bytes 12292
  333.3 22.8 %copy-start.13 = (bf16[8,768,64]{1,2,0:T(8,128)(2,1)}, bf16[8,768,64]{1,2,0:T(8,128)(2,1)S(1)}, u32[]{:S(2)}) copy-start(bf16[8,768,64]{1,2,0:T(8,128)(2,1)S(1)} %maximum_convert_fusion) | copy-start | bytes 2359300
  356.5 41.2 %copy-start.50 = (f32[32,32]{1,0:T(8,128)S(1)}, f32[32,32]{1,0:T(8,128)}, u32[]{:S(2)}) copy-start(f32[32,32]{1,0:T(8,128)} %get-tuple-element.92) | copy-start | bytes 12292
  356.5 41.3 %copy-start.49 = (f32[32,32]{1,0:T(8,128)S(1)}, f32[32,32]{1,0:T(8,128)}, u32[]{:S(2)}) copy-start(f32[32,32]{1,0:T(8,128)} %get-tuple-element.93) | copy-start | bytes 12292
  358.9 39.7 %collective-permute-start = (f32[384,1024]{1,0:T(8,128)}, f32[384,1024]{1,0:T(8,128)}, u32[]{:S(2)}, u32[]{:S(2)}) collective-permute-start(f32[384,1024]{1,0:T(8,128)} %fusion.42), channel_id=1, source_target_pairs={{0,1},{1,0},{2,3},{3,2},{4,5},{5,4},{6,7},{7,6},{8,9},{9,8},{10,11... | collective-permute-start | bytes 4718600 | tf_op jit(solution)/shard_map/ppermute | solution.py:31
  359.7 43.9 %copy-start.62 = (pred[384]{0:T(512)(128)(4,1)}, pred[384]{0:T(512)(128)(4,1)S(1)}, u32[]{:S(2)}) copy-start(pred[384]{0:T(512)(128)(4,1)S(1)} %get-tuple-element.52) | copy-start | bytes 1156
  403.7 125.7 %reduce-scatter.6.cloned.1.call-start = ((), (), s32[]{:S(2)}) async-start(), calls=%async_computation.10 | async-start | bytes 2621440 | tf_op jit(solution)/shard_map/reduce_scatter | solution.py:245
  486.5 105.2 %reduce-scatter.10.cloned.1.call-start = ((), (), s32[]{:S(2)}) async-start(), calls=%async_computation.12 | async-start | bytes 1114112 | tf_op jit(solution)/shard_map/reduce_scatter | solution.py:281
  490.2 2.3 collective-permute-start.3
  495.3 207.6 %reduce-scatter.12.cloned.1.call-start = ((), (), s32[]{:S(2)}) async-start(), calls=%async_computation.13 | async-start | bytes 4456448 | tf_op jit(solution)/shard_map/reduce_scatter | solution.py:281
  512.0 326.2 %reduce-scatter.8.cloned.1.call-start = ((), (), s32[]{:S(2)}) async-start(), calls=%async_computation.11 | async-start | bytes 3342336 | tf_op jit(solution)/shard_map/reduce_scatter | solution.py:281
  537.4 397.4 %reduce-scatter.14.cloned.1.call-start = ((), (), s32[]{:S(2)}) async-start(), calls=%async_computation.14 | async-start | bytes 4456448 | tf_op jit(solution)/shard_map/reduce_scatter | solution.py:281
  560.1 40.3 %collective-permute-start.1 = (f32[384,1024]{1,0:T(8,128)}, f32[384,1024]{1,0:T(8,128)}, u32[]{:S(2)}, u32[]{:S(2)}) collective-permute-start(f32[384,1024]{1,0:T(8,128)} %fusion.37), channel_id=1, source_target_pairs={{0,1},{1,0},{2,3},{3,2},{4,5},{5,4},{6,7},{7,6},{8,9},{9,8},{10,11... | collective-permute-start | bytes 4718600 | tf_op jit(solution)/shard_map/ppermute | solution.py:31
  603.5 102.5 %copy-start.9 = (f32[2,2,64,1024]{3,2,1,0:T(8,128)S(1)}, f32[2,2,64,1024]{3,2,1,0:T(8,128)}, u32[]{:S(2)}) copy-start(f32[2,2,64,1024]{3,2,1,0:T(8,128)} %copy-done.8) | copy-start | bytes 3145732
  704.8 231.8 %collective-permute-start.4 = (f32[32,16,128]{2,1,0:T(8,128)}, f32[32,16,128]{2,1,0:T(8,128)}, u32[]{:S(2)}, u32[]{:S(2)}) collective-permute-start(f32[32,16,128]{2,1,0:T(8,128)} %get-tuple-element.79), channel_id=1, source_target_pairs={{0,1},{1,0},{2,3},{3,2},{4,5},{5,4},{6,7},{7,6},{8,9},{9,8},{10,11... | collective-permute-start | bytes 786440 | tf_op jit(solution)/shard_map/ppermute | solution.py:31
  839.7 100.1 %collective-permute-start.2 = (f32[32,3,512]{2,0,1:T(8,128)S(1)}, f32[32,3,512]{2,0,1:T(8,128)S(1)}, u32[]{:S(2)}, u32[]{:S(2)}) collective-permute-start(f32[32,3,512]{2,0,1:T(8,128)S(1)} %bitcast.316), channel_id=1, source_target_pairs={{0,1},{1,0},{2,3},{3,2},{4,5},{5,4},{6,7},{7,6},{8,9},{9,8},{10,11... | collective-permute-start | bytes 589832 | tf_op jit(solution)/shard_map/ppermute | solution.py:31
  842.6 99.0 %copy-start.87 = (f32[32]{0:T(128)}, f32[32]{0:T(128)S(1)}, u32[]{:S(2)}) copy-start(f32[32]{0:T(128)S(1)} %get-tuple-element.143) | copy-start | bytes 388
  (80 other events, 442.0 us)
Sparse Core Ops, SparseCore 0:
  9.6 11.4 all-gather.21
  24.5 67.9 all-gather.11
  95.8 74.5 all-gather.17
  173.0 74.5 all-gather.19
  249.5 43.9 all-gather.13
  296.4 56.4 all-gather.15
  403.8 12.6 all-gather.23
  486.6 42.6 reduce-scatter.5
  531.7 59.9 reduce-scatter.9
  593.9 108.9 reduce-scatter.11
  707.9 130.2 reduce-scatter.7
  840.3 94.4 reduce-scatter.13

commit v2 on v1

--- a/solution.py
+++ b/solution.py
@@ -296,10 +296,701 @@
     )
 
 
+MESH_ID = pl.DeviceIdType.MESH
+RANKS = 4
+
+
+class Net:
+    def __init__(self, send, recv):
+        self.g, self.z, self.c = (lax.axis_index(a) for a in ALL)
+        self.y, self.x = self.g // 2, self.g % 2
+        self.send, self.recv, self.used = send, recv, 0
+        self.chip = self.g * RANKS + self.z
+        self.core = {"grp": self.g, "chip": self.z, "core": 1 - self.c}
+        self.right = {"grp": self.y * 2 + 1 - self.x, "chip": self.z, "core": self.c}
+        self.up = {"grp": (1 - self.y) * 2 + self.x, "chip": self.z, "core": self.c}
+        self.line = [{"grp": self.g, "chip": (self.z + j) % RANKS, "core": self.c} for j in (1, 2, 3)]
+        self.sent = []
+
+    def enter(self):
+        barrier = pltpu.get_barrier_semaphore()
+        for peer in [self.core, self.right, self.up] + self.line:
+            pl.semaphore_signal(barrier, inc=1, device_id=peer, device_id_type=MESH_ID)
+        pl.semaphore_wait(barrier, 6)
+
+    def copy(self, src, dst, peer):
+        i = self.used
+        self.used += 1
+        made = pltpu.make_async_remote_copy(
+            src_ref=src, dst_ref=dst, send_sem=self.send.at[i], recv_sem=self.recv.at[i],
+            device_id=peer, device_id_type=MESH_ID,
+        )
+        made.start()
+        self.sent.append(made)
+        return made
+
+    def same(self, view, peer):
+        return self.copy(view, view, peer)
+
+    def settle(self, made):
+        made.wait_recv()
+        made.wait_send()
+        self.sent = [m for m in self.sent if m is not made]
+
+    def leave(self):
+        for made in self.sent:
+            made.wait_send()
+        self.sent = []
+
+
+def gather_steps(net, dst, rb, col, width, before):
+    a, b, both = pl.ds(col, width // 2), pl.ds(col + width // 2, width // 2), pl.ds(col, width)
+    quad = 4 * rb
+    held = {}
+
+    def line():
+        for made in before:
+            made.wait_recv()
+        view = dst.at[pl.ds(net.chip * rb, rb), both]
+        held[0] = [net.same(view, peer) for peer in net.line]
+
+    def first():
+        for made in held[0]:
+            made.wait_recv()
+        rows = pl.ds(net.g * quad, quad)
+        held[1] = [net.same(dst.at[rows, a], net.right), net.same(dst.at[rows, b], net.up)]
+
+    def second():
+        for made in held[1]:
+            made.wait_recv()
+        held[2] = [net.same(dst.at[pl.ds(net.y * 2 * quad, 2 * quad), a], net.up)]
+        for y in range(2):
+            held[2].append(net.same(dst.at[pl.ds((y * 2 + net.x) * quad, quad), b], net.right))
+
+    def last():
+        for made in held[2]:
+            made.wait_recv()
+
+    return [line, first, second, last]
+
+
+def small_steps(net, rows):
+    held = {}
+
+    def pair():
+        held[0] = [net.same(rows.at[net.chip * 2 + net.c], net.core)]
+
+    def line():
+        held[0][0].wait_recv()
+        held[1] = [net.same(rows.at[pl.ds(net.chip * 2, 2)], peer) for peer in net.line]
+
+    def first():
+        for made in held[1]:
+            made.wait_recv()
+        held[2] = [net.same(rows.at[pl.ds(net.g * 8, 8)], net.right)]
+
+    def second():
+        held[2][0].wait_recv()
+        held[3] = [net.same(rows.at[pl.ds(net.y * 16, 16)], net.up)]
+
+    def last():
+        held[3][0].wait_recv()
+
+    return [pair, line, first, second, last]
+
+
+def run_diagonal(tasks):
+    longest = max(len(steps) + t for t, steps in enumerate(tasks))
+    for time in range(longest):
+        for t, steps in enumerate(tasks):
+            if 0 <= time - t < len(steps):
+                steps[time - t]()
+
+
+def add_rows(dst, dst_rows, cols, src, src_rows, count, tile=64):
+    @pl.loop(0, count // tile)
+    def _(i):
+        to = pl.ds(pl.multiple_of(dst_rows + i * tile, tile), tile)
+        total = dst[to, cols].astype(F32) + src[pl.ds(pl.multiple_of(src_rows + i * tile, tile), tile), :].astype(F32)
+        dst[to, cols] = total.astype(dst.dtype)
+
+
+def scatter_steps(net, src, rb, got_a, got_b, got_z, total):
+    cols = src.shape[1]
+    a, b = pl.ds(0, cols // 2), pl.ds(cols // 2, cols // 2)
+    tile = min(64, rb)
+    quad = 4 * rb
+    at = lambda y, x: pl.ds((y * 2 + x) * quad, quad)
+    held = {}
+
+    def first():
+        rows = pl.ds((1 - net.y) * 2 * quad, 2 * quad)
+        held[0] = [net.copy(src.at[rows, a], got_a.at[pl.ds(0, 2 * quad)], net.up)]
+        for y in range(2):
+            held[0].append(net.copy(src.at[at(y, 1 - net.x), b], got_b.at[pl.ds(y * quad, quad)], net.right))
+
+    def second():
+        for made in held[0]:
+            made.wait_recv()
+        add_rows(src, (net.y * 2 + 1 - net.x) * quad, a, got_a, (1 - net.x) * quad, quad, tile)
+        add_rows(src, ((1 - net.y) * 2 + net.x) * quad, b, got_b, (1 - net.y) * quad, quad, tile)
+        held[1] = [
+            net.copy(src.at[at(net.y, 1 - net.x), a], got_a.at[pl.ds(2 * quad, quad)], net.right),
+            net.copy(src.at[at(1 - net.y, net.x), b], got_b.at[pl.ds(2 * quad, quad)], net.up),
+        ]
+        add_rows(src, (net.y * 2 + net.x) * quad, a, got_a, net.x * quad, quad, tile)
+        add_rows(src, (net.y * 2 + net.x) * quad, b, got_b, net.y * quad, quad, tile)
+
+    def third():
+        for made in held[1]:
+            made.wait_recv()
+        line = (net.y * 2 + net.x) * quad
+        add_rows(src, line, a, got_a, 2 * quad, quad, tile)
+        add_rows(src, line, b, got_b, 2 * quad, quad, tile)
+        held[2] = [
+            net.copy(src.at[pl.ds(line + (net.z + j) % 4 * rb, rb)], got_z.at[j - 1], net.line[j - 1])
+            for j in (1, 2, 3)
+        ]
+
+    def last():
+        for made in held[2]:
+            made.wait_recv()
+        line = (net.y * 2 + net.x) * quad + net.z * rb
+
+        @pl.loop(0, rb // tile)
+        def _(i):
+            rows = pl.ds(pl.multiple_of(i * tile, tile), tile)
+            value = src[pl.ds(pl.multiple_of(line + i * tile, tile), tile), :].astype(F32)
+            for j in range(3):
+                value = value + got_z[j, rows, :].astype(F32)
+            total[rows, :] = value
+
+    return [first, second, third, last]
+
+
+def sum_steps(net, value, got):
+    held = {}
+    peers = [net.core, net.right, net.up]
+
+    def make(i):
+        def step():
+            if i > 0:
+                held[i - 1].wait_recv()
+                held[i - 1].wait_send()
+                net.sent = [m for m in net.sent if m is not held[i - 1]]
+                value[...] = value[...] + got[i - 1]
+            if i < 3:
+                held[i] = net.copy(value, got.at[i], peers[i])
+            else:
+                held[3] = [net.copy(value, got.at[3 + net.z], peer) for peer in net.line]
+                got[3 + net.z] = value[...]
+
+        return step
+
+    def last():
+        for made in held[3]:
+            made.wait_recv()
+            made.wait_send()
+            net.sent = [m for m in net.sent if m is not made]
+        value[...] = (got[3] + got[4]) + (got[5] + got[6])
+
+    return [make(i) for i in range(4)] + [last]
+
+
+VM = pl.BlockSpec(memory_space=pltpu.VMEM)
+PROMPT = RANKS * 2 * PSH
+KEYS = 2 * PROMPT + CONT
+ROWS = 4 * PSH + CONT
+
+
+def nt(a, b):
+    return lax.dot_general(a, b, (((1,), (1,)), ((), ())), preferred_element_type=F32)
+
+
+def nn(a, b):
+    return lax.dot_general(a, b, (((1,), (0,)), ((), ())), preferred_element_type=F32)
+
+
+def tn(a, b):
+    return lax.dot_general(a, b, (((0,), (0,)), ((), ())), preferred_element_type=F32)
+
+
+def tile_at(i, size):
+    return pl.ds(pl.multiple_of(i * size, size), size)
+
+
+def move_rows(dst, to, src, at, count, tile=32):
+    @pl.loop(0, count // tile)
+    def _(i):
+        step = pl.multiple_of(i * tile, tile)
+        dst[pl.ds(pl.multiple_of(to + step, tile), tile), :] = src[pl.ds(pl.multiple_of(at + step, tile), tile), :]
+
+
+def spread_row(rows, field, index, owner, lane, size):
+    table = rows[:, field, :].astype(BF)
+    lanes = lax.broadcasted_iota(jnp.int32, (128, size), 0)
+    pick = (lanes == index[lane : lane + 1, :size]).astype(F32).astype(BF)
+    wide = nn(table, pick)
+    owners = lax.broadcasted_iota(jnp.int32, (rows.shape[0], size), 0)
+    return jnp.sum(jnp.where(owners == index[owner : owner + 1, :size], wide, 0.0), axis=0, keepdims=True)
+
+
+def norm_rows(x):
+    x = x.astype(F32)
+    center = x - jnp.mean(x, axis=-1, keepdims=True)
+    return center * lax.rsqrt(jnp.mean(center * center, axis=-1, keepdims=True) + EPSILON)
+
+
+def turn(value, table, sign):
+    cos, low_sin, high_sin = (table[:, 128 * i : 128 * i + 128] for i in range(3))
+    out = []
+    for j in range(value.shape[1] // 128):
+        v = value[:, 128 * j : 128 * j + 128]
+        other = pltpu.roll(v, 120, 1) * low_sin + pltpu.roll(v, 8, 1) * high_sin
+        out.append(v * cos + sign * other)
+    return out[0] if len(out) == 1 else jnp.concatenate(out, axis=1)
+
+
+def rotary_table(length):
+    half = ROT // 2
+    inverse = (10000.0 ** (-np.arange(half, dtype=np.float32) / half)).astype(np.float32)
+    angles = (np.arange(length, dtype=np.float32)[:, None] * inverse).astype(np.float64)
+    cos, sin = np.cos(angles), np.sin(angles)
+    table = np.zeros((length, 3, 2, HD), np.float32)
+    table[:, 0] = 1.0
+    for head in range(2):
+        table[:, 0, head, :half] = cos
+        table[:, 0, head, half:ROT] = cos
+        table[:, 1, head, :half] = -sin
+        table[:, 2, head, half:ROT] = sin
+    return table.reshape(length, 384)
+
+
+def index_table(rd):
+    n = np.arange(2048)
+    table = np.zeros((2, 16, 2048), np.int32)
+    for c in range(2):
+        col = np.minimum(n // HC, 2) * D + c * HC + n % HC
+        table[c, 0], table[c, 1] = col // 96, col % 96
+        unit = n // rd * (2 * rd) + c * rd + n % rd
+        table[c, 2], table[c, 3] = unit // rd, unit % rd
+        table[c, 4] = n // 32 % 32
+        for i in range(4):
+            table[c, 8 + i] = n % 32 + 32 * i
+    return table
+
+
+def seen(keys_at, queries_at, shape, length=None):
+    keys = lax.broadcasted_iota(jnp.int32, shape, 0) + keys_at
+    queries = lax.broadcasted_iota(jnp.int32, shape, 1) + queries_at
+    mask = keys <= queries
+    return mask if length is None else mask & (keys < length)
+
+
+def head_lanes(rows):
+    return lax.broadcasted_iota(jnp.int32, (rows, 128), 1) < HD
+
+
+def attend(query, keys, values, masks, head):
+    lanes = head_lanes(query.shape[0])
+    own = jnp.where(lanes if head == 0 else ~lanes, query.astype(F32) * SCALE, 0.0).astype(BF)
+    scores = [nt(k, own) for k in keys]
+    scores = [s if m is None else jnp.where(m, s, NEGATIVE) for s, m in zip(scores, masks)]
+    top = functools.reduce(jnp.maximum, [jnp.max(s, axis=0, keepdims=True) for s in scores])
+    weights = [jnp.exp(s - top) for s in scores]
+    total = sum(jnp.sum(w, axis=0, keepdims=True) for w in weights)
+    share = 1.0 / total
+    out = sum(tn(v, (w * share).astype(BF)) for v, w in zip(values, weights))
+    return out[head * HD : head * HD + HD], top + jnp.log(total)
+
+
+def forward_kernel(
+    tokens, small, qkv, out, up, down, rotary, index,
+    rows, w_qkv, w_out, w_up, w_down, x_all, first_in, second_in, q, kv, attended, lse, activated, slope,
+    spread, swapped, send, recv,
+):
+    net = Net(send, recv)
+    c, z, chip = net.c, net.z, net.chip
+    net.enter()
+    for p in range(2):
+        move_rows(x_all, p * PROMPT + z * 2 * PSH + c * PSH, tokens, p * PSH, PSH)
+    move_rows(x_all, 2 * PROMPT + c * HALF, tokens, 2 * PSH, HALF)
+    rows[chip * 2 + c] = small[...]
+    pieces = [pl.ds(p * PROMPT + z * 2 * PSH + c * PSH, PSH) for p in range(2)]
+    smalls = small_steps(net, rows)
+    smalls[0]()
+    own_tokens = [net.same(x_all.at[piece], peer) for peer in net.line for piece in pieces]
+    mates = [net.same(x_all.at[piece], net.core) for piece in pieces + [pl.ds(2 * PROMPT + c * HALF, HALF)]]
+    half_rows = pl.ds(pl.multiple_of(chip * 64 + c * 32, 32), 32)
+    given = pl.ds(0, 32)
+    w_qkv[half_rows, :] = qkv[c]
+    swapped[given, : 3 * HC] = qkv[1 - c]
+    from_core = {}
+    from_core["qkv"] = net.copy(swapped.at[given, pl.ds(0, 3 * HC)], w_qkv.at[half_rows], net.core)
+    w_up[half_rows, :] = up[c]
+    given = pl.ds(32, 32)
+    swapped[given, : FF // 2] = up[1 - c]
+    from_core["up"] = net.copy(swapped.at[given, pl.ds(0, FF // 2)], w_up.at[half_rows], net.core)
+    w_down[pl.ds(pl.multiple_of(chip * 128, 128), 128), :] = down[...]
+    spread[pl.ds(pl.multiple_of(chip * 32, 32), 32), :] = out[...]
+    none = []
+    tasks = [
+        gather_steps(net, w_qkv, 64, 0, 768, [from_core["qkv"]]),
+        gather_steps(net, w_qkv, 64, 768, 768, none),
+        gather_steps(net, w_up, 64, 0, 1024, [from_core["up"]]),
+        gather_steps(net, w_up, 64, 1024, 1024, none),
+        gather_steps(net, spread, 32, 0, 1024, none),
+        gather_steps(net, w_down, 128, 0, 512, none),
+        gather_steps(net, w_down, 128, 512, 512, none),
+    ]
+    clock = [0]
+
+    def advance(until):
+        while clock[0] < until:
+            for t, steps in enumerate(tasks):
+                if (clock[0] - t) % 2 == 0 and 0 <= (clock[0] - t) // 2 < len(steps):
+                    steps[(clock[0] - t) // 2]()
+            clock[0] += 1
+
+    advance(1)
+    smalls[1]()
+    for made in own_tokens:
+        made.wait_recv()
+    relays = []
+    for j in (1, 2, 3):
+        for p in range(2):
+            piece = pl.ds(p * PROMPT + (z + j) % RANKS * 2 * PSH + c * PSH, PSH)
+            relays.append(net.same(x_all.at[piece], net.core))
+    advance(2)
+    smalls[2]()
+    smalls[3]()
+    smalls[4]()
+    advance(3)
+    for made in mates + relays:
+        made.wait_recv()
+    places = index.at[c]
+    gain1, bias1, gain2, bias2 = (spread_row(rows, 0, places, 4, 8 + i, D) for i in range(4))
+
+    @pl.loop(0, KEYS // 64)
+    def _(i):
+        at = tile_at(i, 64)
+        first_in[at, :] = (norm_rows(x_all[at, :]) * gain1 + bias1).astype(BF)
+
+    advance(4)
+
+    def own_at(i):
+        prompt = (i // 2) * PROMPT + z * 2 * PSH + (i % 2) * 64
+        return pl.multiple_of(jnp.where(i < 4, prompt, 2 * PROMPT + (i - 4) * 64), 64)
+
+    @pl.loop(0, ROWS // 64)
+    def _(i):
+        second_in[tile_at(i, 64), :] = (norm_rows(x_all[pl.ds(own_at(i), 64), :]) * gain2 + bias2).astype(BF)
+
+    b_qkv = spread_row(rows, 2, places, 0, 1, 3 * HC)
+    b_up = spread_row(rows, 3, places, 2, 3, FF // 2)
+    advance(8)
+
+    @pl.loop(0, KEYS // 256)
+    def _(i):
+        at = tile_at(i, 256)
+        here = first_in[at, :]
+        place = pl.multiple_of(jnp.where(i < 4, (i % 2) * 256, PROMPT + (i - 4) * 256), 256)
+        table = rotary[pl.ds(place, 256), :]
+        for j in range(4):
+            cols = slice(HC + 256 * j, HC + 256 * j + 256)
+            value = nn(here, w_qkv[:, cols]) + b_qkv[:, cols]
+            kv[at, 256 * j : 256 * j + 256] = (turn(value, table, 1.0) if j < 2 else value).astype(BF)
+
+    @pl.loop(0, ROWS // 128)
+    def _(i):
+        prompt = i * PROMPT + z * 2 * PSH
+        source = pl.multiple_of(jnp.where(i < 2, prompt, 2 * PROMPT + (i - 2) * 128), 128)
+        place = pl.multiple_of(jnp.where(i < 2, z * 2 * PSH, PROMPT + (i - 2) * 128), 128)
+        here = first_in[pl.ds(source, 128), :]
+        table = rotary[pl.ds(place, 128), :]
+        for j in range(2):
+            cols = slice(256 * j, 256 * j + 256)
+            q[tile_at(i, 128), cols] = turn(nn(here, w_qkv[:, cols]) + b_qkv[:, cols], table, 1.0).astype(BF)
+
+    advance(9)
+    length = jnp.sum(jnp.sum(rows[pl.ds(chip * 2, 2), 5:7, :], axis=0), keepdims=True).astype(jnp.int32)
+    second = jnp.broadcast_to(small[7:8, :], (PROMPT, 128)) > 0.5
+
+    def attend_pair(pair):
+        k_at, v_at = pl.ds(128 * pair, 128), pl.ds(HC + 128 * pair, 128)
+        prompts = [(kv[p * PROMPT : (p + 1) * PROMPT, k_at], kv[p * PROMPT : (p + 1) * PROMPT, v_at]) for p in range(2)]
+
+        def put(row, size, key_list, value_list, masks):
+            outs = []
+            for head in range(2):
+                o, stat = attend(q[row : row + size, k_at], key_list, value_list, masks, head)
+                outs.append(o)
+                lse[2 * pair + head, :, row : row + size] = stat
+            attended[row : row + size, k_at] = jnp.concatenate(outs, axis=0).T.astype(BF)
+
+        for p in range(2):
+            put(p * 128, 128, [prompts[p][0]], [prompts[p][1]], [seen(0, z * 2 * PSH, (PROMPT, 128))])
+        chosen = [jnp.where(second, b.astype(F32), a.astype(F32)).astype(BF) for a, b in zip(*prompts)]
+        for i in range(CONT // 128):
+            near = 128 * i + 128
+            put(
+                256 + 128 * i, 128,
+                [chosen[0], kv[2 * PROMPT : 2 * PROMPT + near, k_at]],
+                [chosen[1], kv[2 * PROMPT : 2 * PROMPT + near, v_at]],
+                [None, seen(0, 128 * i, (near, 128), length)],
+            )
+
+    def hidden(j):
+        cols = slice(256 * j, 256 * j + 256)
+
+        @pl.loop(0, ROWS // 128)
+        def _(i):
+            at = tile_at(i, 128)
+            pre = nn(second_in[at, :], w_up[:, cols]) + b_up[:, cols]
+            gate = 0.5 * (1.0 + lax.erf(pre * 0.7071067811865476))
+            activated[at, cols] = (pre * gate).astype(BF)
+            slope[at, cols] = (gate + pre * jnp.exp(-0.5 * pre * pre) * 0.3989422804014327).astype(slope.dtype)
+
+    attend_pair(0)
+    attend_pair(1)
+    advance(10)
+    for j in range(4):
+        hidden(j)
+    advance(11)
+    attend_pair(2)
+    attend_pair(3)
+    advance(12)
+    for j in range(4, 8):
+        hidden(j)
+    advance(13)
+    given = pl.ds(pl.multiple_of((1 - c) * 256, 256), 256)
+    swap = net.copy(spread.at[given], swapped.at[pl.ds(64, 256), pl.ds(0, D)], net.core)
+    advance(20)
+    swap.wait_recv()
+    for h in range(8):
+        w_out[pl.ds(pl.multiple_of(h * 64 + c * 32, 32), 32), :] = spread[pl.ds(pl.multiple_of(c * 256 + h * 32, 32), 32), :]
+        w_out[pl.ds(pl.multiple_of(h * 64 + (1 - c) * 32, 32), 32), :] = swapped[64 + h * 32 : 96 + h * 32, :D]
+    net.leave()
+
+
+def forward(tokens, small, qkv, out, up, down):
+    shape = jax.ShapeDtypeStruct
+    return pl.pallas_call(
+        forward_kernel,
+        out_shape=(
+            shape((32, 8, 128), F32), shape((D, 3 * HC), BF), shape((HC, D), BF), shape((D, FF // 2), BF), shape((FF // 2, D), BF),
+            shape((KEYS, D), BF), shape((KEYS, D), BF), shape((ROWS, D), BF), shape((ROWS, HC), BF), shape((KEYS, 2 * HC), BF),
+            shape((ROWS, HC), BF), shape((8, 1, ROWS), F32), shape((ROWS, FF // 2), BF), shape((ROWS, FF // 2), F32),
+        ),
+        in_specs=[VM] * 8,
+        out_specs=(VM,) * 14,
+        scratch_shapes=[
+            pltpu.VMEM((HC, D), BF), pltpu.VMEM((320, FF // 2), BF),
+            pltpu.SemaphoreType.DMA((96,)), pltpu.SemaphoreType.DMA((96,)),
+        ],
+        compiler_params=pltpu.CompilerParams(collective_id=0, has_side_effects=True, vmem_limit_bytes=60 << 20),
+    )(tokens, small, qkv, out, up, down, jnp.asarray(rotary_table(PROMPT + CONT)), jnp.asarray(index_table(128)))
+
+
+HBM = pl.BlockSpec(memory_space=pl.ANY)
+
+
+def scatter_line_kernel(given, total, pair, got, send, recv):
+    net = Net(send, recv)
+    for j in range(4):
+        move_rows(pair.at[j], 0, given.at[j], 0, given.shape[1])
+    net.enter()
+    made = [net.copy(pair.at[(net.z + j) % 4], got.at[j - 1], net.line[j - 1]) for j in (1, 2, 3)]
+    for m in made:
+        m.wait_recv()
+    n = pair.shape[1]
+
+    @pl.loop(0, n // 64)
+    def _(i):
+        rows = pl.ds(pl.multiple_of(i * 64, 64), 64)
+        value = pair[net.z, rows, :].astype(F32)
+        for j in range(3):
+            value = value + got[j, rows, :].astype(F32)
+        total[rows, :] = value
+
+    net.leave()
+
+
+def scatter_line(pair):
+    _, n, w = pair.shape
+    return pl.pallas_call(
+        scatter_line_kernel,
+        out_shape=jax.ShapeDtypeStruct((n, w), F32),
+        in_specs=[VM],
+        out_specs=VM,
+        scratch_shapes=[pltpu.VMEM((4, n, w), pair.dtype), pltpu.VMEM((3, n, w), pair.dtype), pltpu.SemaphoreType.DMA((4,)), pltpu.SemaphoreType.DMA((4,))],
+        compiler_params=pltpu.CompilerParams(collective_id=2, has_side_effects=True, vmem_limit_bytes=32 << 20),
+    )(pair)
+
+
+def scatter_kernel(value, qkv, out, up, down, o_sum, o_qkv, o_out, o_up, o_down, got_s, *scratch):
+    bufs, (send, recv) = scratch[:-2], scratch[-2:]
+    net = Net(send, recv)
+    net.enter()
+    o_sum[...] = value[...]
+    tasks = [sum_steps(net, o_sum, got_s)]
+    plan = ((down, 128, o_down), (up, 64, o_up), (out, 32, o_out), (qkv, 64, o_qkv))
+    for i, (src, rb, total) in enumerate(plan):
+        held = bufs[4 * i]
+        move_rows(held, 0, src, 0, src.shape[0])
+        tasks.append(scatter_steps(net, held, rb, *bufs[4 * i + 1 : 4 * i + 4], total))
+    run_diagonal(tasks)
+    net.leave()
+
+
+def scatter_all(value, qkv, out, up, down):
+    shape = jax.ShapeDtypeStruct
+    n = value.shape[0]
+    bufs = []
+    for src in (down, up, out, qkv):
+        rb, cols = src.shape[0] // 16, src.shape[1]
+        bufs += [pltpu.VMEM(src.shape, BF), pltpu.VMEM((12 * rb, cols // 2), BF), pltpu.VMEM((12 * rb, cols // 2), BF), pltpu.VMEM((3, rb, cols), BF)]
+    return pl.pallas_call(
+        scatter_kernel,
+        out_shape=(
+            shape((n, 128), F32), shape((64, 3 * HC), F32), shape((32, D), F32), shape((64, FF // 2), F32), shape((128, D), F32),
+        ),
+        in_specs=[VM] * 5,
+        out_specs=(VM,) * 5,
+        scratch_shapes=[pltpu.VMEM((7, n, 128), F32)] + bufs
+        + [pltpu.SemaphoreType.DMA((64,)), pltpu.SemaphoreType.DMA((64,))],
+        compiler_params=pltpu.CompilerParams(collective_id=3, has_side_effects=True, vmem_limit_bytes=56 << 20),
+    )(value, qkv, out, up, down)
+
+
+def fast_body(
+    tokens, valid, prompt_of, teacher, cotangent,
+    ln1_gain, ln1_bias, ln2_gain, ln2_bias, qkv_weight, qkv_bias, out_weight, out_bias,
+    up_weight, up_bias, down_weight, down_bias, stop=None,
+):
+    c = lax.axis_index("core")
+    z = lax.axis_index("chip")
+    chips = lax.axis_size("chip")
+    nh = HC // HD
+    rd = down_weight.shape[0]
+    device = lax.axis_index(ALL)
+    pad = lambda v: jnp.pad(v.astype(F32), (0, 128 - v.shape[0]))[None]
+    live_own = (valid > 0).astype(F32)
+    small = jnp.concatenate(
+        [
+            jnp.concatenate([ln1_gain, ln1_bias, ln2_gain, ln2_bias]).astype(F32)[None],
+            pad(jnp.concatenate([out_bias, down_bias])),
+            pad(qkv_bias),
+            pad(up_bias),
+            live_own.reshape(3, 128),
+            jnp.broadcast_to(prompt_of.astype(F32)[:, None], (1, 128)),
+        ]
+    )
+    rows, w_qkv, w_out, w_up, w_down, x_all, first_all, second_in, q, kv, attended, lse, activated, slope = forward(
+        tokens,
+        small,
+        qkv_weight.reshape(32, 3, 2, HC).transpose(2, 0, 1, 3).reshape(2, 32, 3 * HC),
+        out_weight,
+        up_weight.reshape(32, 16, 2, 128).transpose(2, 0, 1, 3).reshape(2, 32, FF // 2),
+        down_weight,
+    )
+    def own_of(a):
+        prompts = lax.dynamic_slice_in_dim(a[: 2 * PROMPT].reshape(2, PROMPT, -1), z * 2 * PSH, 2 * PSH, axis=1)
+        return jnp.concatenate([prompts.reshape(4 * PSH, -1), a[2 * PROMPT :]])
+    x = own_of(x_all).astype(F32)
+    first_in = own_of(first_all)
+    prompt_kv = kv[: 2 * PROMPT].reshape(2, 4, 2 * PSH, 2 * HC).swapaxes(0, 1)
+    kv = own_of(kv)
+    lse = lse[:, 0]
+    normed, rstd = normalize(x)
+    gain1, bias1, gain2, bias2 = (rows[:, 0, 32 * i : 32 * i + 32].reshape(-1) for i in range(4))
+    b_out, b_down = (rows[:, 1, 32 * i : 32 * i + 32].reshape(-1) for i in range(2))
+    count_all = jnp.sum(rows[:, 4:7])
+    places = places_of(z, chips)
+    turn_own = lambda v, d: rotate_heads(v.reshape(-1, nh, HD), places, d).reshape(-1, HC)
+    cont_valid = lax.dynamic_slice_in_dim(rows, (device // 2) * 2, 2)[:, 5:7].reshape(-1)
+    masks = masks_of(z, chips, cont_valid)
+    chosen = prompt_of[0]
+    partial = dot(attended, w_out, (1, 0)) + dot(activated, w_down, (1, 0))
+    halves = split_rows(partial)
+    take = lambda a: lax.dynamic_index_in_dim(a, c, axis=0, keepdims=False)
+    give = lambda a: lax.dynamic_index_in_dim(a, 1 - c, axis=0, keepdims=False)
+    output = tokens.astype(F32) + take(halves) + swap_cores(give(halves)) + b_out + b_down
+    live = (valid > 0).astype(F32)[:, None]
+    missed = output - teacher.astype(F32)
+    squared = jnp.sum(live * missed * missed)
+    out_grad = cotangent.astype(F32) + 2.0 / (count_all * D) * live * missed
+    out_low = pair_rows(out_grad.astype(BF))
+    if stop == "fwd":
+        return output
+    out_bias_grad = jnp.sum(out_grad.astype(BF).astype(F32), axis=0)
+    dw_out = dot(attended, out_low, (0, 0))
+    dw_down = dot(activated, out_low, (0, 0))
+    att_grad = dot(out_low, w_out, (1, 1)).astype(BF)
+    hidden_grad = (dot(out_low, w_down, (1, 1)) * slope).astype(BF)
+    dw_up = dot(second_in, hidden_grad, (0, 0))
+    db_up = jnp.sum(hidden_grad.astype(F32), axis=0)
+    second_grad = dot(hidden_grad, w_up, (1, 1))
+    dq, pair, near = g_attention_back(q, prompt_kv, kv, att_grad, lse, chosen, masks)
+    own_pair = scatter_line(pair.astype(BF).reshape(4, 4 * PSH, 2 * HC))
+    pair = jnp.concatenate([own_pair, near], axis=0)
+    projected_grad = jnp.concatenate([turn_own(dq, -1.0), turn_own(pair[:, :HC], -1.0), pair[:, HC:]], axis=1).astype(BF)
+    dw_qkv = dot(first_in, projected_grad, (0, 0))
+    db_qkv = jnp.sum(projected_grad.astype(F32), axis=0)
+    first_grad = dot(projected_grad, w_qkv, (1, 1))
+    if stop == "bwd":
+        return dw_out, dw_down, dw_up, dw_qkv, second_grad, first_grad, projected_grad, hidden_grad, att_grad
+    joint = first_grad * gain1 + second_grad * gain2
+    halves = split_rows(joint)
+    joint = take(halves) + swap_cores(give(halves))
+    own_normed = take(split_rows(normed))
+    own_rstd = take(split_rows(rstd))
+    input_grad = out_grad + own_rstd * (
+        joint
+        - jnp.mean(joint, axis=-1, keepdims=True)
+        - own_normed * jnp.mean(joint * own_normed, axis=-1, keepdims=True)
+    )
+    wide = lambda v, n: jnp.zeros((v.shape[0], 2, v.shape[1]), F32).at[:, c].set(v).reshape(-1)
+    small = jnp.concatenate(
+        [
+            jnp.sum(first_grad * normed, axis=0),
+            jnp.sum(first_grad, axis=0),
+            jnp.sum(second_grad * normed, axis=0),
+            jnp.sum(second_grad, axis=0),
+            out_bias_grad,
+            wide(db_qkv.reshape(3, HC), 3),
+            wide(db_up.reshape(-1, rd), 16),
+        ]
+    )
+    small = jnp.concatenate([small, jnp.full((128,), squared), jnp.zeros((7 * 128,), F32)]).reshape(-1, 128)
+    pairs = lambda own, other, axis: jnp.where(c == 0, jnp.stack([own, other], axis), jnp.stack([other, own], axis))
+    o = dw_out.astype(BF).reshape(H // 2, 2, 32, D)
+    o_own = lax.dynamic_index_in_dim(o, c, axis=1, keepdims=False)
+    o_other = swap_cores(lax.dynamic_index_in_dim(o, 1 - c, axis=1, keepdims=False))
+    small, s_qkv, s_out, s_up, s_down = scatter_all(
+        small, dw_qkv.astype(BF), pairs(o_own, o_other, 0).reshape(-1, D), dw_up.astype(BF), dw_down.astype(BF)
+    )
+    s_qkv = s_qkv.reshape(2, 32, 3, HC)
+    s_up = s_up.reshape(2, 32, 16, 128)
+    s_qkv = pairs(take(s_qkv), swap_cores(give(s_qkv)), 2).reshape(32, 3 * D)
+    s_up = pairs(take(s_up), swap_cores(give(s_up)), 2).reshape(32, FF)
+    small = small.reshape(-1)
+    shares, at = [], 0
+    for size in (D, D, D, D, D, 3 * D, FF):
+        own = size // lax.axis_size(ALL)
+        shares.append(lax.dynamic_slice_in_dim(small, at + device * own, own))
+        at += size
+    loss_value = small[at] / (count_all * D)
+    return (
+        output.astype(BF), loss_value, input_grad, shares[0], shares[1], shares[2], shares[3],
+        s_qkv, shares[5], s_out, shares[4], s_up, shares[6], s_down, shares[4],
+    )
+
+
 def solution(mesh):
     groups, seats = mesh.shape["grp"], mesh.shape["seq"]
     fine = Mesh(mesh.devices.reshape(groups, seats // 2, 2), ALL)
     rows, row = P(ALL, None), P(ALL)
     in_specs = (rows, row, row, rows, rows) + (row,) * 4 + (rows, row) * 4
     out_specs = (rows, P(), rows) + (row,) * 4 + (rows, row) * 4
-    return jax.shard_map(generic_body, mesh=fine, in_specs=in_specs, out_specs=out_specs, check_vma=False)
+    return jax.shard_map(fast_body if (groups, seats) == (4, 8) else generic_body, mesh=fine, in_specs=in_specs, out_specs=out_specs, check_vma=False)

time: 965 us -> 630 us (0.65)
  waiting for transfers between devices: 522 us -> 0.03 us
  Pallas kernels: 0 us -> 351 us
  blocking collectives: 122 us -> 0 us
  matrix products: 128 us -> 94.3 us
  local copies, waits for them, and re-layouts: 92.5 us -> 117 us
  other arithmetic: 60.3 us -> 36.7 us
    pallas_call x0 -> x3, Pallas kernels: none -> 351 us  [the longest x1 166 us: forward(): pl.pallas_call(forward_kernel, out_shape=(shape((32, 8, 128), F32), shape...]
    reduce_scatter x5 -> x0, waiting for transfers between devices: 314 us -> none  [the longest x4 308 us: generic_body(): lax.psum_scatter(v.astype(BF), CHIPS, scatter_dimension=0, tiled=True)]
    all_gather x5 -> x0, waiting for transfers between devices: 193 us -> none  [the longest x1 55.2 us: g_weights(): down = lax.all_gather(down_weight, CHIPS, axis=0, tiled=True)]
    psum x2 -> x0, blocking collectives: 76.6 us -> none  [generic_body(): lax.psum((jnp.sum(live), jnp.sum(live * missed * missed)), ALL)]
    unnamed x1 -> x0, blocking collectives: 38.4 us -> none
    dot_general x12 -> x10, matrix products: 81.4 us -> 45.3 us  [dot(): lax.dot_general(a, b, ((contract[:1], contract[1:]), ((), ())), preferred...]
    all_gather x2 -> x1, waiting for transfers between devices: 11.7 us -> 0.01 us  [pair_rows(): both = lax.all_gather(own, 'core', axis=0)]
    slice x10 -> x13, local copies, waits for them, and re-layouts: 15.5 us -> 24.7 us  [the longest x2 6.15 us: own_of(): a[:2 * PROMPT].reshape(2, PROMPT, -1)]
  transfers between devices with their start and end apart: 17 -> 6, of which waited for: 12 -> 0; matrix products, arithmetic and copies ran while one was open for 20% -> 16% of each run, Pallas kernels for 0% -> 22%
where the time goes in v2:
time: 630 us; the launch traced here: 621 us
  Pallas kernels  351 us (56%)
  local copies, waits for them, and re-layouts  117 us (19%)
  matrix products  94.3 us (15%)
  other arithmetic  36.7 us (6%)
  between operations  18.9 us (3%)
    pallas_call x1, Pallas kernels, forward(): pl.pallas_call(forward_kernel, out_shape=(shape((32, 8, 128), F32), shape...  166 us
    pallas_call x1, Pallas kernels, scatter_all(): pl.pallas_call(scatter_kernel, out_shape=(shape((n, 128), F32), shape((64...  136 us
    pallas_call x1, Pallas kernels, scatter_line(): pl.pallas_call(scatter_line_kernel, out_shape=jax.ShapeDtypeStruct((n, w)...  48.2 us
    dot_general x10, matrix products, dot(): lax.dot_general(a, b, ((contract[:1], contract[1:]), ((), ())), preferred...  45.3 us
    unnamed x156, local copies, waits for them, and re-layouts  21.2 us
    dot_general x2, matrix products, back(): ein(f'{eq},{ek}->{eq[:-1]}k', query, key) * SCALE  18 us
  transfers between devices with their start and end apart: 6, of which 0 were waited for; matrix products, arithmetic and copies ran while one was open for 16% of the time, Pallas kernels for 22%

profile of v2, /device:TPU:29, one launch (start us, length us, event | category | flops | bytes accessed | tf_op | source)
XLA Modules:
  0.0 620.8 jit_solution(63658420344106048)
XLA Ops:
  13.6 166.2 %shard_map.298 = (f32[32,8,128]{2,1,0:T(8,128)}, bf16[1024,1536]{1,0:T(8,128)(2,1)}, bf16[512,1024]{1,0:T(8,128)(2,1)}, bf16[1024,2048]{1,0:T(8,128)(2,1)}, bf16...) custom-call(bf16[384,1024]{1,0:T(8,128)(2,1)} %tokens.1, ...), custom_call_target="tpu_custom_call" | custom-call | tf_op jit(solution)/shard_map/pallas_call | solution.py:778
  179.8 6.3 %fusion.81 = f32[768,1024]{1,0:T(8,128)S(1)} fusion(bf16[768,2048]{1,0:T(8,128)(2,1)} %get-tuple-element.60, bf16[2048,1024]{1,0:T(8,128)(2,1)} %get-tuple-element.61), kind=kOutput, calls=%fused_computation.198 | convolution fusion | flops 3221225472 | bytes 10485760 | tf_op jit(solution)/shard_map/dot_general | solution.py:79
  192.0 3.1 slice.212
  195.2 3.1 slice.185
  198.4 3.2 copy.75
  201.6 3.2 copy.83
  204.9 4.1 reshape.510
  209.1 3.1 slice.214
  221.2 3.0 fusion.12
  232.7 2.7 copy.74
  235.4 3.1 copy.76
  240.0 3.4 copy.80
  249.3 3.7 fusion.51
  257.8 8.1 %fusion.39 = f32[8,512,1024]{2,1,0:T(8,128)} fusion(bf16[2,8,512,64]{2,3,1,0:T(8,128)(2,1)S(1)} %bitcast.240, bf16[2,8,512,64]{2,3,1,0:T(8,128)(2,1)S(1)} %copy-done.15, bf16[8,768,64]{1,2,0:T(8,128)(2,1)S(1)} %bitcast.265), kind=kOutput, calls=%fused_computation.93 | convolution fusion | flops 538968064 | bytes 19398656 | tf_op jit(solution)/shard_map/hqd,hkd->hqk/dot_general | solution.py:166
  266.0 14.3 %multiply_reduce_fusion = (f32[8,512]{1,0:T(8,128)S(1)}, f32[8,512,1024]{2,1,0:T(8,128)}) fusion(f32[8,512,1024]{2,1,0:T(8,128)} %fusion.39, f32[8,512]{1,0:T(8,128)S(1)} %slice.237, bf16[2,8,512,64]{2,3,1,0:T(8,128)(2,1)S(1)} %copy-done.15, bf16[2,8,512,64]{2,3,1,0:T(8,128)(2,1)S(1)} %bitcast.241, bf16[8,768,64]{1,2,0:T(8,128)(2,1)S(1)} %bitcast.245, ...), kind=kOutput, calls=%fused_computation.1 | convolution fusion | flops 559935488 | bytes 36732928 | tf_op jit(solution)/shard_map/hqd,hkd->hqk/dot_general | solution.py:164
  280.3 7.6 %fusion = f32[8,1024,64]{1,2,0:T(8,128)S(1)} fusion(f32[8,512,1024]{2,1,0:T(8,128)} %get-tuple-element.126, bf16[8,768,64]{1,2,0:T(8,128)(2,1)} %bitcast.266), kind=kOutput, calls=%fused_computation.3 | convolution fusion | flops 541065216 | bytes 19398656 | tf_op jit(solution)/shard_map/hqk,hqd->hkd/dot_general | solution.py:172
  289.2 6.8 %multiply_convert_fusion = bf16[8,512,1024]{2,1,0:T(8,128)(2,1)S(1)} fusion(f32[8,512,1024]{2,1,0:T(8,128)} %get-tuple-element.126, f32[8,512,1024]{2,1,0:T(8,128)S(1)} %bitcast.223, f32[8,512]{1,0:T(8,128)S(1)} %get-tuple-element.125), kind=kLoop, calls=%fused_computation | loop fusion | flops 12582912 | bytes 41959424 | tf_op jit(solution)/shard_map/convert_element_type | solution.py:168
  306.9 3.3 copy.88
  310.2 3.6 multiply_reduce_fusion.1
  318.4 3.0 maximum_bitcast_fusion
  324.1 3.0 copy.89.given
  327.1 48.2 %shard_map.299 = f32[256,1024]{1,0:T(8,128)S(1)} custom-call(bf16[4,256,1024]{2,1,0:T(8,128)(2,1)S(1)} %copy.89.given), custom_call_target="tpu_custom_call" | custom-call | tf_op jit(solution)/shard_map/pallas_call | solution.py:821
  379.9 6.5 %convolution_multiply_fusion.1 = f32[8,512,64]{1,2,0:T(8,128)S(1)} fusion(bf16[8,512,1024]{2,1,0:T(8,128)(2,1)} %copy-done, bf16[2,8,512,64]{2,3,1,0:T(8,128)(2,1)S(1)} %copy-done.16, bf16[2,8,512,64]{2,3,1,0:T(8,128)(2,1)S(1)} %bitcast.242), kind=kOutput, calls=%fused_computation.82 | convolution fusion | flops 539230208 | bytes 11534336 | tf_op jit(solution)/shard_map/hqk,hkd->hqd/dot_general | solution.py:170
  387.8 6.6 %convert_reduce_fusion = (f32[2048]{0:T(1024)S(1)}, bf16[768,2048]{1,0:T(8,128)(2,1)S(1)}) fusion(f32[768,2048]{1,0:T(8,128)S(1)} %bitcast.306, bf16[2048,1024]{1,0:T(8,128)(2,1)} %get-tuple-element.61, bf16[512,1024]{1,0:T(8,128)(2,1)S(1)} %bitcast.276, bf16[256,1024]{1,0:T(8,128)(2,1)S(1)} %bitcast.284), kind=kOutput, calls=%fused_computation.5 | convolution fusion | flops 3230660608 | bytes 15212544 | tf_op jit(solution)/shard_map/dot_general | solution.py:79
  397.8 3.5 fusion.82
  403.2 5.5 fusion.71
  412.0 5.2 convolution_convert_fusion.1.down
  423.9 7.9 %convolution_convert_fusion.2.up = bf16[1024,2048]{1,0:T(8,128)(2,1)} fusion(bf16[768,1024]{1,0:T(8,128)(2,1)} %get-tuple-element.71, bf16[768,2048]{1,0:T(8,128)(2,1)} %copy-done.64), kind=kOutput, calls=%fused_computation.19 | convolution fusion | flops 3223322624 | bytes 8912896 | tf_op jit(solution)/shard_map/dot_general | solution.py:79
  432.5 6.5 %convolution_convert_fusion.qkv = bf16[1024,1536]{1,0:T(8,128)(2,1)} fusion(bf16[512,1024]{1,0:T(8,128)(2,1)} %slice.215, bf16[256,1024]{1,0:T(8,128)(2,1)} %bitcast.288, bf16[768,512]{0,1:T(8,128)(2,1)} %copy-done.33, bf16[768,512]{0,1:T(8,128)(2,1)} %bitcast.261, bf16[768,512]{0,1:T(8,128)(2,1)} %bitcast.264), kind=kOutput, calls=%fused_computation.17 | convolution fusion | flops 2427715584 | bytes 7077888 | tf_op jit(solution)/shard_map/dot_general | solution.py:79
  441.4 136.1 %shard_map.300 = (f32[104,128]{1,0:T(8,128)}, f32[64,1536]{1,0:T(8,128)}, f32[32,1024]{1,0:T(8,128)}, f32[64,2048]{1,0:T(8,128)}, f32[128,1024]{1,0:T(8,128)}) custom-call(f32[104,128]{1,0:T(8,128)} %bitcast.292, bf16[1024,1536]{1,0:T(8,128)(2,1)} %convolution_convert_fusion.qkv, bf16[512,1024]{1,0:T(8,128)(2,1)} %bitcast.251, ...), custom_call_target="tpu_custom_call" | custom-call | tf_op jit(solution)/shard_map/pallas_call | solution.py:853
  585.7 3.2 slice.255
  599.6 2.8 maximum_select_fusion.1
  (294 shorter events, 111.9 us)
Async XLA Ops:
  7.2 5.7 copy-start.55
  7.2 5.6 copy-start.51
  7.2 5.6 copy-start.52
  7.2 5.6 copy-start.53
  7.3 5.6 copy-start.54
  7.3 245.7 %all-gather.3.cloned.1.call-start = ((), (), s32[]{:S(2)}) async-start(), calls=%async_computation | async-start | bytes 2359296 | tf_op jit(solution)/shard_map/all_gather | solution.py:35
  179.8 6.3 %copy-start.40 = (bf16[512,1024]{1,0:T(8,128)(2,1)S(1)}, bf16[512,1024]{1,0:T(8,128)(2,1)}, u32[]{:S(2)}) copy-start(bf16[512,1024]{1,0:T(8,128)(2,1)} %get-tuple-element.59) | copy-start | bytes 3145732
  179.8 6.3 %copy-start.42 = (bf16[768,512]{1,0:T(8,128)(2,1)S(1)}, bf16[768,512]{1,0:T(8,128)(2,1)}, u32[]{:S(2)}) copy-start(bf16[768,512]{1,0:T(8,128)(2,1)} %get-tuple-element.58) | copy-start | bytes 2359300
  191.1 29.1 %collective-permute-start = (f32[384,1024]{1,0:T(8,128)}, f32[384,1024]{1,0:T(8,128)}, u32[]{:S(2)}, u32[]{:S(2)}) collective-permute-start(f32[384,1024]{1,0:T(8,128)} %fusion.22), channel_id=1, source_target_pairs={{0,1},{1,0},{2,3},{3,2},{4,5},{5,4},{6,7},{7,6},{8,9},{9,8},{10,11... | collective-permute-start | bytes 4718600 | tf_op jit(solution)/shard_map/ppermute | solution.py:31
  228.0 20.4 %copy-start.11 = (bf16[512,1024]{1,0:T(8,128)(2,1)}, bf16[512,1024]{1,0:T(8,128)(2,1)S(1)}, u32[]{:S(2)}) copy-start(bf16[512,1024]{1,0:T(8,128)(2,1)S(1)} %slice.213) | copy-start | bytes 3145732
  232.7 33.3 %copy-start.17 = (bf16[512,1024]{0,1:T(8,128)(2,1)}, bf16[512,1024]{0,1:T(8,128)(2,1)S(1)}, u32[]{:S(2)}) copy-start(bf16[512,1024]{0,1:T(8,128)(2,1)S(1)} %copy.84) | copy-start | bytes 3145732
  240.0 9.2 %copy-start.13 = (bf16[8,2,512,64]{2,3,1,0:T(8,128)(2,1)}, bf16[8,2,512,64]{2,3,1,0:T(8,128)(2,1)S(1)}, u32[]{:S(2)}) copy-start(bf16[8,2,512,64]{2,3,1,0:T(8,128)(2,1)S(1)} %squeeze.60) | copy-start | bytes 3145732
  257.8 8.1 %copy-start.19 = (bf16[768,512]{0,1:T(8,128)(2,1)S(1)}, bf16[768,512]{0,1:T(8,128)(2,1)}, u32[]{:S(2)}) copy-start(bf16[768,512]{0,1:T(8,128)(2,1)} %copy.74) | copy-start | bytes 2359300
  266.0 23.2 %slice-start = ((s8[16777216]{0:T(1024)(128)(4,1)}), s8[4194304]{0:T(1024)(128)(4,1)S(1)}, s32[]{:S(2)}) async-start(s8[16777216]{0:T(1024)(128)(4,1)} %bitcast.222), calls=%async_computation.1 | async-start | bytes 8388608
  266.0 23.2 %slice-start.1 = ((s8[16777216]{0:T(1024)(128)(4,1)}), s8[4194304]{0:T(1024)(128)(4,1)S(1)}, s32[]{:S(2)}) async-start(s8[16777216]{0:T(1024)(128)(4,1)} %bitcast.222), calls=%async_computation.2 | async-start | bytes 8388608
  266.0 23.2 %slice-start.2 = ((s8[16777216]{0:T(1024)(128)(4,1)}), s8[4194304]{0:T(1024)(128)(4,1)S(1)}, s32[]{:S(2)}) async-start(s8[16777216]{0:T(1024)(128)(4,1)} %bitcast.222), calls=%async_computation.3 | async-start | bytes 8388608
  280.3 8.9 %slice-start.3 = ((s8[16777216]{0:T(1024)(128)(4,1)}), s8[4194304]{0:T(1024)(128)(4,1)S(1)}, s32[]{:S(2)}) async-start(s8[16777216]{0:T(1024)(128)(4,1)} %bitcast.222), calls=%async_computation.4 | async-start | bytes 8388608
  304.5 5.7 copy-start.25
  378.1 30.9 %copy-start.33 = (bf16[768,512]{0,1:T(8,128)(2,1)}, bf16[768,512]{0,1:T(8,128)(2,1)S(1)}, u32[]{:S(2)}) copy-start(bf16[768,512]{0,1:T(8,128)(2,1)S(1)} %fusion.29) | copy-start | bytes 2359300
  378.1 9.2 %slice-start.4 = ((s8[6291456]{0:T(1024)(128)(4,1)}), s8[4194304]{0:T(1024)(128)(4,1)S(1)}, s32[]{:S(2)}) async-start(s8[6291456]{0:T(1024)(128)(4,1)} %bitcast.305), calls=%async_computation.5 | async-start | bytes 8388608
  379.9 6.5 %copy-start.4 = (bf16[8,2,128,512]{3,2,1,0:T(8,128)(2,1)S(1)}, bf16[8,2,128,512]{3,2,1,0:T(8,128)(2,1)}, u32[]{:S(2)}) copy-start(bf16[8,2,128,512]{3,2,1,0:T(8,128)(2,1)} %copy-done.3) | copy-start | bytes 6291460
  379.9 6.5 %copy-start.14 = (bf16[8,2,512,64]{2,3,1,0:T(8,128)(2,1)S(1)}, bf16[8,2,512,64]{2,3,1,0:T(8,128)(2,1)}, u32[]{:S(2)}) copy-start(bf16[8,2,512,64]{2,3,1,0:T(8,128)(2,1)} %copy-done.13) | copy-start | bytes 3145732
  379.9 7.4 %slice-start.5 = ((s8[6291456]{0:T(1024)(128)(4,1)}), s8[2097152]{0:T(1024)(128)(4,1)S(1)}, s32[]{:S(2)}) async-start(s8[6291456]{0:T(1024)(128)(4,1)} %bitcast.305), calls=%async_computation.6 | async-start | bytes 4194304
  401.4 7.5 %copy-start.31 = (bf16[768,8,64]{0,2,1:T(8,128)(2,1)}, bf16[768,8,64]{0,2,1:T(8,128)(2,1)S(1)}, u32[]{:S(2)}) copy-start(bf16[768,8,64]{0,2,1:T(8,128)(2,1)S(1)} %pad_maximum_fusion.7) | copy-start | bytes 2359300
  401.5 7.5 %copy-start.32 = (bf16[768,8,64]{0,2,1:T(8,128)(2,1)}, bf16[768,8,64]{0,2,1:T(8,128)(2,1)S(1)}, u32[]{:S(2)}) copy-start(bf16[768,8,64]{0,2,1:T(8,128)(2,1)S(1)} %pad_maximum_fusion.6) | copy-start | bytes 2359300
  418.6 186.1 %collective-permute-start.2 = (f32[384,1024]{1,0:T(8,128)}, f32[384,1024]{1,0:T(8,128)}, u32[]{:S(2)}, u32[]{:S(2)}) collective-permute-start(f32[384,1024]{1,0:T(8,128)} %fusion.17), channel_id=1, source_target_pairs={{0,1},{1,0},{2,3},{3,2},{4,5},{5,4},{6,7},{7,6},{8,9},{9,8},{10,11... | collective-permute-start | bytes 4718600 | tf_op jit(solution)/shard_map/ppermute | solution.py:31
  423.9 15.2 %collective-permute-start.1 = (bf16[8,32,1024]{2,1,0:T(8,128)(2,1)}, bf16[8,32,1024]{2,1,0:T(8,128)(2,1)}, u32[]{:S(2)}, u32[]{:S(2)}) collective-permute-start(bf16[8,32,1024]{2,1,0:T(8,128)(2,1)} %get-tuple-element.111), channel_id=1, source_target_pairs={{0,1},{1,0},{2,3},{3,2},{4,5},{5,4},{6,7},{7,6},{8,9},{9,8},{10,11... | collective-permute-start | bytes 1572872 | tf_op jit(solution)/shard_map/ppermute | solution.py:31
  432.5 6.5 %copy-start.49 = (f32[13312]{0:T(1024)}, f32[13312]{0:T(1024)S(1)}, u32[]{:S(2)}) copy-start(f32[13312]{0:T(1024)S(1)} %constant_dynamic-update-slice_fusion) | copy-start | bytes 159748
  432.5 6.5 %copy-start.37 = (bf16[1,8,32,1024]{3,2,1,0:T(8,128)(2,1)S(1)}, bf16[1,8,32,1024]{3,2,1,0:T(8,128)(2,1)}, u32[]{:S(2)}) copy-start(bf16[1,8,32,1024]{3,2,1,0:T(8,128)(2,1)} %get-tuple-element.110) | copy-start | bytes 1572868
  581.4 15.7 %collective-permute-start.3 = (f32[32,3,512]{2,0,1:T(8,128)}, f32[32,3,512]{2,0,1:T(8,128)}, u32[]{:S(2)}, u32[]{:S(2)}) collective-permute-start(f32[32,3,512]{2,0,1:T(8,128)} %bitcast.215), channel_id=1, source_target_pairs={{0,1},{1,0},{2,3},{3,2},{4,5},{5,4},{6,7},{7,6},{8,9},{9,8},{10,11... | collective-permute-start | bytes 589832 | tf_op jit(solution)/shard_map/ppermute | solution.py:31
  585.5 14.1 %collective-permute-start.4 = (f32[32,16,128]{2,1,0:T(8,128)}, f32[32,16,128]{2,1,0:T(8,128)}, u32[]{:S(2)}, u32[]{:S(2)}) collective-permute-start(f32[32,16,128]{2,1,0:T(8,128)} %get-tuple-element.113), channel_id=1, source_target_pairs={{0,1},{1,0},{2,3},{3,2},{4,5},{5,4},{6,7},{7,6},{8,9},{9,8},{10,11... | collective-permute-start | bytes 786440 | tf_op jit(solution)/shard_map/ppermute | solution.py:31
  597.1 13.3 %copy-start.58 = (f32[32]{0:T(128)}, f32[32]{0:T(128)S(1)}, u32[]{:S(2)}) copy-start(f32[32]{0:T(128)S(1)} %get-tuple-element.188) | copy-start | bytes 388
  (45 other events, 122.8 us)
Sparse Core Ops, SparseCore 0:
  226.8 10.3 all-gather.2

commit v3 on v2

--- a/solution.py
+++ b/solution.py
@@ -399,104 +399,6 @@
     return [pair, line, first, second, last]
 
 
-def run_diagonal(tasks):
-    longest = max(len(steps) + t for t, steps in enumerate(tasks))
-    for time in range(longest):
-        for t, steps in enumerate(tasks):
-            if 0 <= time - t < len(steps):
-                steps[time - t]()
-
-
-def add_rows(dst, dst_rows, cols, src, src_rows, count, tile=64):
-    @pl.loop(0, count // tile)
-    def _(i):
-        to = pl.ds(pl.multiple_of(dst_rows + i * tile, tile), tile)
-        total = dst[to, cols].astype(F32) + src[pl.ds(pl.multiple_of(src_rows + i * tile, tile), tile), :].astype(F32)
-        dst[to, cols] = total.astype(dst.dtype)
-
-
-def scatter_steps(net, src, rb, got_a, got_b, got_z, total):
-    cols = src.shape[1]
-    a, b = pl.ds(0, cols // 2), pl.ds(cols // 2, cols // 2)
-    tile = min(64, rb)
-    quad = 4 * rb
-    at = lambda y, x: pl.ds((y * 2 + x) * quad, quad)
-    held = {}
-
-    def first():
-        rows = pl.ds((1 - net.y) * 2 * quad, 2 * quad)
-        held[0] = [net.copy(src.at[rows, a], got_a.at[pl.ds(0, 2 * quad)], net.up)]
-        for y in range(2):
-            held[0].append(net.copy(src.at[at(y, 1 - net.x), b], got_b.at[pl.ds(y * quad, quad)], net.right))
-
-    def second():
-        for made in held[0]:
-            made.wait_recv()
-        add_rows(src, (net.y * 2 + 1 - net.x) * quad, a, got_a, (1 - net.x) * quad, quad, tile)
-        add_rows(src, ((1 - net.y) * 2 + net.x) * quad, b, got_b, (1 - net.y) * quad, quad, tile)
-        held[1] = [
-            net.copy(src.at[at(net.y, 1 - net.x), a], got_a.at[pl.ds(2 * quad, quad)], net.right),
-            net.copy(src.at[at(1 - net.y, net.x), b], got_b.at[pl.ds(2 * quad, quad)], net.up),
-        ]
-        add_rows(src, (net.y * 2 + net.x) * quad, a, got_a, net.x * quad, quad, tile)
-        add_rows(src, (net.y * 2 + net.x) * quad, b, got_b, net.y * quad, quad, tile)
-
-    def third():
-        for made in held[1]:
-            made.wait_recv()
-        line = (net.y * 2 + net.x) * quad
-        add_rows(src, line, a, got_a, 2 * quad, quad, tile)
-        add_rows(src, line, b, got_b, 2 * quad, quad, tile)
-        held[2] = [
-            net.copy(src.at[pl.ds(line + (net.z + j) % 4 * rb, rb)], got_z.at[j - 1], net.line[j - 1])
-            for j in (1, 2, 3)
-        ]
-
-    def last():
-        for made in held[2]:
-            made.wait_recv()
-        line = (net.y * 2 + net.x) * quad + net.z * rb
-
-        @pl.loop(0, rb // tile)
-        def _(i):
-            rows = pl.ds(pl.multiple_of(i * tile, tile), tile)
-            value = src[pl.ds(pl.multiple_of(line + i * tile, tile), tile), :].astype(F32)
-            for j in range(3):
-                value = value + got_z[j, rows, :].astype(F32)
-            total[rows, :] = value
-
-    return [first, second, third, last]
-
-
-def sum_steps(net, value, got):
-    held = {}
-    peers = [net.core, net.right, net.up]
-
-    def make(i):
-        def step():
-            if i > 0:
-                held[i - 1].wait_recv()
-                held[i - 1].wait_send()
-                net.sent = [m for m in net.sent if m is not held[i - 1]]
-                value[...] = value[...] + got[i - 1]
-            if i < 3:
-                held[i] = net.copy(value, got.at[i], peers[i])
-            else:
-                held[3] = [net.copy(value, got.at[3 + net.z], peer) for peer in net.line]
-                got[3 + net.z] = value[...]
-
-        return step
-
-    def last():
-        for made in held[3]:
-            made.wait_recv()
-            made.wait_send()
-            net.sent = [m for m in net.sent if m is not made]
-        value[...] = (got[3] + got[4]) + (got[5] + got[6])
-
-    return [make(i) for i in range(4)] + [last]
-
-
 VM = pl.BlockSpec(memory_space=pltpu.VMEM)
 PROMPT = RANKS * 2 * PSH
 KEYS = 2 * PROMPT + CONT
@@ -606,8 +508,8 @@
 
 def forward_kernel(
     tokens, small, qkv, out, up, down, rotary, index,
-    rows, w_qkv, w_out, w_up, w_down, x_all, first_in, second_in, q, kv, attended, lse, activated, slope,
-    spread, swapped, send, recv,
+    rows, w_qkv, w_out, w_up, w_down, x_own, first_own, second_in, q, kv, attended, lse, activated, slope,
+    x_all, first_in, spread, swapped, send, recv,
 ):
     net = Net(send, recv)
     c, z, chip = net.c, net.z, net.chip
@@ -619,7 +521,6 @@
     pieces = [pl.ds(p * PROMPT + z * 2 * PSH + c * PSH, PSH) for p in range(2)]
     smalls = small_steps(net, rows)
     smalls[0]()
-    own_tokens = [net.same(x_all.at[piece], peer) for peer in net.line for piece in pieces]
     mates = [net.same(x_all.at[piece], net.core) for piece in pieces + [pl.ds(2 * PROMPT + c * HALF, HALF)]]
     half_rows = pl.ds(pl.multiple_of(chip * 64 + c * 32, 32), 32)
     given = pl.ds(0, 32)
@@ -634,15 +535,10 @@
     w_down[pl.ds(pl.multiple_of(chip * 128, 128), 128), :] = down[...]
     spread[pl.ds(pl.multiple_of(chip * 32, 32), 32), :] = out[...]
     none = []
-    tasks = [
-        gather_steps(net, w_qkv, 64, 0, 768, [from_core["qkv"]]),
-        gather_steps(net, w_qkv, 64, 768, 768, none),
-        gather_steps(net, w_up, 64, 0, 1024, [from_core["up"]]),
-        gather_steps(net, w_up, 64, 1024, 1024, none),
-        gather_steps(net, spread, 32, 0, 1024, none),
-        gather_steps(net, w_down, 128, 0, 512, none),
-        gather_steps(net, w_down, 128, 512, 512, none),
-    ]
+    tasks = [gather_steps(net, w_up, 64, 512 * i, 512, [] if i else [from_core["up"]]) for i in range(4)]
+    tasks += [gather_steps(net, w_qkv, 64, 512 * i, 512, [] if i else [from_core["qkv"]]) for i in range(3)]
+    tasks += [gather_steps(net, spread, 32, 0, 1024, [])]
+    tasks += [gather_steps(net, w_down, 128, 256 * i, 256, []) for i in range(4)]
     clock = [0]
 
     def advance(until):
@@ -654,6 +550,33 @@
 
     advance(1)
     smalls[1]()
+    advance(2)
+    smalls[2]()
+    advance(3)
+    smalls[3]()
+    smalls[4]()
+    advance(4)
+    own_tokens = [net.same(x_all.at[piece], peer) for peer in net.line for piece in pieces]
+    places = index.at[c]
+    gain1, bias1, gain2, bias2 = (spread_row(rows, 0, places, 4, 8 + i, D) for i in range(4))
+    b_qkv = spread_row(rows, 2, places, 0, 1, 3 * HC)
+    b_up = spread_row(rows, 3, places, 2, 3, FF // 2)
+    for made in mates:
+        made.wait_recv()
+
+    @pl.loop(0, ROWS // 64)
+    def _(i):
+        prompt = (i // 2) * PROMPT + z * 2 * PSH + (i % 2) * 64
+        here = pl.ds(pl.multiple_of(jnp.where(i < 4, prompt, 2 * PROMPT + (i - 4) * 64), 64), 64)
+        at = tile_at(i, 64)
+        normed = norm_rows(x_all[here, :])
+        x_own[at, :] = x_all[here, :]
+        low = (normed * gain1 + bias1).astype(BF)
+        first_in[here, :] = low
+        first_own[at, :] = low
+        second_in[at, :] = (normed * gain2 + bias2).astype(BF)
+
+    advance(7)
     for made in own_tokens:
         made.wait_recv()
     relays = []
@@ -661,34 +584,38 @@
         for p in range(2):
             piece = pl.ds(p * PROMPT + (z + j) % RANKS * 2 * PSH + c * PSH, PSH)
             relays.append(net.same(x_all.at[piece], net.core))
-    advance(2)
-    smalls[2]()
-    smalls[3]()
-    smalls[4]()
-    advance(3)
-    for made in mates + relays:
+    advance(8)
+    for made in relays:
         made.wait_recv()
-    places = index.at[c]
-    gain1, bias1, gain2, bias2 = (spread_row(rows, 0, places, 4, 8 + i, D) for i in range(4))
-
-    @pl.loop(0, KEYS // 64)
+
+    @pl.loop(0, 12)
     def _(i):
-        at = tile_at(i, 64)
-        first_in[at, :] = (norm_rows(x_all[at, :]) * gain1 + bias1).astype(BF)
-
-    advance(4)
-
-    def own_at(i):
-        prompt = (i // 2) * PROMPT + z * 2 * PSH + (i % 2) * 64
-        return pl.multiple_of(jnp.where(i < 4, prompt, 2 * PROMPT + (i - 4) * 64), 64)
-
-    @pl.loop(0, ROWS // 64)
-    def _(i):
-        second_in[tile_at(i, 64), :] = (norm_rows(x_all[pl.ds(own_at(i), 64), :]) * gain2 + bias2).astype(BF)
-
-    b_qkv = spread_row(rows, 2, places, 0, 1, 3 * HC)
-    b_up = spread_row(rows, 3, places, 2, 3, FF // 2)
-    advance(8)
+        row = (i // 2 % 2) * PROMPT + (z + 1 + i // 4) % RANKS * 2 * PSH + (i % 2) * 64
+        here = pl.ds(pl.multiple_of(row, 64), 64)
+        first_in[here, :] = (norm_rows(x_all[here, :]) * gain1 + bias1).astype(BF)
+
+    def hidden(j):
+        cols = slice(256 * j, 256 * j + 256)
+
+        @pl.loop(0, ROWS // 128)
+        def _(i):
+            at = tile_at(i, 128)
+            pre = nn(second_in[at, :], w_up[:, cols]) + b_up[:, cols]
+            gate = 0.5 * (1.0 + lax.erf(pre * 0.7071067811865476))
+            activated[at, cols] = (pre * gate).astype(BF)
+            slope[at, cols] = (gate + pre * jnp.exp(-0.5 * pre * pre) * 0.3989422804014327).astype(slope.dtype)
+
+    advance(9)
+    for j in range(0, 4):
+        hidden(j)
+    advance(10)
+    for j in range(4, 6):
+        hidden(j)
+    advance(11)
+    for j in range(6, 8):
+        hidden(j)
+    advance(12)
+    advance(13)
 
     @pl.loop(0, KEYS // 256)
     def _(i):
@@ -712,7 +639,7 @@
             cols = slice(256 * j, 256 * j + 256)
             q[tile_at(i, 128), cols] = turn(nn(here, w_qkv[:, cols]) + b_qkv[:, cols], table, 1.0).astype(BF)
 
-    advance(9)
+    advance(14)
     length = jnp.sum(jnp.sum(rows[pl.ds(chip * 2, 2), 5:7, :], axis=0), keepdims=True).astype(jnp.int32)
     second = jnp.broadcast_to(small[7:8, :], (PROMPT, 128)) > 0.5
 
@@ -740,29 +667,13 @@
                 [None, seen(0, 128 * i, (near, 128), length)],
             )
 
-    def hidden(j):
-        cols = slice(256 * j, 256 * j + 256)
-
-        @pl.loop(0, ROWS // 128)
-        def _(i):
-            at = tile_at(i, 128)
-            pre = nn(second_in[at, :], w_up[:, cols]) + b_up[:, cols]
-            gate = 0.5 * (1.0 + lax.erf(pre * 0.7071067811865476))
-            activated[at, cols] = (pre * gate).astype(BF)
-            slope[at, cols] = (gate + pre * jnp.exp(-0.5 * pre * pre) * 0.3989422804014327).astype(slope.dtype)
-
     attend_pair(0)
+    advance(15)
     attend_pair(1)
-    advance(10)
-    for j in range(4):
-        hidden(j)
-    advance(11)
+    advance(16)
     attend_pair(2)
+    advance(17)
     attend_pair(3)
-    advance(12)
-    for j in range(4, 8):
-        hidden(j)
-    advance(13)
     given = pl.ds(pl.multiple_of((1 - c) * 256, 256), 256)
     swap = net.copy(spread.at[given], swapped.at[pl.ds(64, 256), pl.ds(0, D)], net.core)
     advance(20)
@@ -779,94 +690,364 @@
         forward_kernel,
         out_shape=(
             shape((32, 8, 128), F32), shape((D, 3 * HC), BF), shape((HC, D), BF), shape((D, FF // 2), BF), shape((FF // 2, D), BF),
-            shape((KEYS, D), BF), shape((KEYS, D), BF), shape((ROWS, D), BF), shape((ROWS, HC), BF), shape((KEYS, 2 * HC), BF),
+            shape((ROWS, D), BF), shape((ROWS, D), BF), shape((ROWS, D), BF), shape((ROWS, HC), BF), shape((KEYS, 2 * HC), BF),
             shape((ROWS, HC), BF), shape((8, 1, ROWS), F32), shape((ROWS, FF // 2), BF), shape((ROWS, FF // 2), F32),
         ),
         in_specs=[VM] * 8,
         out_specs=(VM,) * 14,
         scratch_shapes=[
-            pltpu.VMEM((HC, D), BF), pltpu.VMEM((320, FF // 2), BF),
-            pltpu.SemaphoreType.DMA((96,)), pltpu.SemaphoreType.DMA((96,)),
+            pltpu.VMEM((KEYS, D), BF), pltpu.VMEM((KEYS, D), BF), pltpu.VMEM((HC, D), BF), pltpu.VMEM((320, FF // 2), BF),
+            pltpu.SemaphoreType.DMA((140,)), pltpu.SemaphoreType.DMA((140,)),
         ],
         compiler_params=pltpu.CompilerParams(collective_id=0, has_side_effects=True, vmem_limit_bytes=60 << 20),
     )(tokens, small, qkv, out, up, down, jnp.asarray(rotary_table(PROMPT + CONT)), jnp.asarray(index_table(128)))
 
 
-HBM = pl.BlockSpec(memory_space=pl.ANY)
-
-
-def scatter_line_kernel(given, total, pair, got, send, recv):
+def add_rows(dst, dst_rows, src, src_rows, count, cols, tile):
+    @pl.loop(0, count // tile)
+    def _(i):
+        to = pl.ds(pl.multiple_of(dst_rows + i * tile, tile), tile)
+        more = src[pl.ds(pl.multiple_of(src_rows + i * tile, tile), tile), cols].astype(F32)
+        dst[to, :] = (dst[to, :].astype(F32) + more).astype(dst.dtype)
+
+
+def scatter_steps(net, src, rb, col, width, before, got_a, got_b, got_z, put):
+    half = width // 2
+    a, b, both = pl.ds(col, half), pl.ds(col + half, half), pl.ds(col, width)
+    quad = 4 * rb
+    tile = min(64, rb)
+    at = lambda y, x: pl.ds((y * 2 + x) * quad, quad)
+    held = {}
+
+    def first():
+        for made in before:
+            made.wait()
+        rows = pl.ds((1 - net.y) * 2 * quad, 2 * quad)
+        held[0] = [net.copy(src.at[rows, a], got_a.at[pl.ds(0, 2 * quad)], net.up)]
+        for y in range(2):
+            held[0].append(net.copy(src.at[at(y, 1 - net.x), b], got_b.at[pl.ds(y * quad, quad)], net.right))
+
+    def second():
+        for made in held[0]:
+            made.wait_recv()
+        add_rows(got_a, (1 - net.x) * quad, src, (net.y * 2 + 1 - net.x) * quad, quad, a, tile)
+        add_rows(got_b, (1 - net.y) * quad, src, ((1 - net.y) * 2 + net.x) * quad, quad, b, tile)
+        held[1] = [
+            net.copy(got_a.at[pl.ds((1 - net.x) * quad, quad)], got_a.at[pl.ds(2 * quad, quad)], net.right),
+            net.copy(got_b.at[pl.ds((1 - net.y) * quad, quad)], got_b.at[pl.ds(2 * quad, quad)], net.up),
+        ]
+        add_rows(got_a, net.x * quad, src, (net.y * 2 + net.x) * quad, quad, a, tile)
+        add_rows(got_b, net.y * quad, src, (net.y * 2 + net.x) * quad, quad, b, tile)
+
+    def third():
+        for made in held[1]:
+            made.wait_recv()
+        add_rows(got_a, net.x * quad, got_a, 2 * quad, quad, slice(None), tile)
+        add_rows(got_b, net.y * quad, got_b, 2 * quad, quad, slice(None), tile)
+        held[2] = []
+        for j in (1, 2, 3):
+            there = (net.z + j) % RANKS * rb
+            peer = net.line[j - 1]
+            held[2].append(net.copy(got_a.at[pl.ds(net.x * quad + there, rb)], got_z.at[j - 1, :, pl.ds(0, half)], peer))
+            held[2].append(net.copy(got_b.at[pl.ds(net.y * quad + there, rb)], got_z.at[j - 1, :, pl.ds(half, half)], peer))
+
+    def last():
+        for made in held[2]:
+            made.wait_recv()
+        for k, (got, way) in enumerate(((got_a, net.x), (got_b, net.y))):
+            cols = slice(k * half, k * half + half)
+
+            @pl.loop(0, rb // tile)
+            def _(i):
+                rows = pl.ds(pl.multiple_of(way * quad + net.z * rb + i * tile, tile), tile)
+                value = got[rows, :].astype(F32)
+                for j in range(3):
+                    value = value + got_z[j, tile_at(i, tile), cols].astype(F32)
+                put(tile_at(i, tile), slice(col + k * half, col + k * half + half), value)
+
+    return [first, second, third, last]
+
+
+def sum_steps(net, value, got):
+    held = {}
+    peers = [net.core, net.right, net.up]
+
+    def make(i):
+        def step():
+            if i > 0:
+                net.settle(held[i - 1])
+                value[...] = value[...] + got[i - 1]
+            if i < 3:
+                held[i] = net.copy(value, got.at[i], peers[i])
+            else:
+                held[3] = [net.copy(value, got.at[3 + net.z], peer) for peer in net.line]
+                got[3 + net.z] = value[...]
+
+        return step
+
+    def last():
+        for made in held[3]:
+            net.settle(made)
+        value[...] = (got[3] + got[4]) + (got[5] + got[6])
+
+    return [make(i) for i in range(4)] + [last]
+
+
+def attend_back(query, grad, keys, values, masks, stat, head):
+    lanes = head_lanes(query.shape[0])
+    lanes = lanes if head == 0 else ~lanes
+    own = jnp.where(lanes, query.astype(F32) * SCALE, 0.0).astype(BF)
+    own_grad = jnp.where(lanes, grad.astype(F32), 0.0).astype(BF)
+    inner, kept = 0.0, []
+    for k, v, m in zip(keys, values, masks):
+        scores = nt(k, own)
+        probs = jnp.exp((scores if m is None else jnp.where(m, scores, NEGATIVE)) - stat)
+        prob_grad = nt(v, own_grad)
+        inner = inner + jnp.sum(probs * prob_grad, axis=0, keepdims=True)
+        kept.append((probs, prob_grad))
+    dq, dks, dvs = 0.0, [], []
+    for k, (probs, prob_grad) in zip(keys, kept):
+        score_grad = (probs * (prob_grad - inner)).astype(BF)
+        dq = dq + tn(k, score_grad)
+        dks.append(nn(score_grad, own))
+        dvs.append(nn(probs.astype(BF), own_grad))
+    return dq[head * HD : head * HD + HD] * SCALE, dks, dvs
+
+
+def backward_kernel(
+    rows, small, value_in, gain, rotary, q, kv, att_grad, lse, first, x, w_qkv, joint_in, dw_out_in, dw_down_in, dw_up_in,
+    value, o_qkv, o_out, o_up, o_down, joint_own,
+    dw_qkv, dw_out, dw_down, dw_up, spread, pairs, got_pairs, far_k, far_v, projected, joint, peer_joint,
+    got_s, s_qkv, s_up, peer_qkv, peer_up, *rest,
+):
+    bufs, (send, recv, local) = rest[:-3], rest[-3:]
     net = Net(send, recv)
-    for j in range(4):
-        move_rows(pair.at[j], 0, given.at[j], 0, given.shape[1])
+    c, z, chip = net.c, net.z, net.chip
+    loads = [pltpu.make_async_copy(src, dst, local.at[i]) for i, (src, dst) in enumerate(
+        ((dw_down_in, dw_down), (dw_up_in, dw_up), (dw_out_in, dw_out)))]
+    for load in loads:
+        load.start()
+    value[...] = value_in[...]
     net.enter()
-    made = [net.copy(pair.at[(net.z + j) % 4], got.at[j - 1], net.line[j - 1]) for j in (1, 2, 3)]
-    for m in made:
-        m.wait_recv()
-    n = pair.shape[1]
-
-    @pl.loop(0, n // 64)
-    def _(i):
-        rows = pl.ds(pl.multiple_of(i * 64, 64), 64)
-        value = pair[net.z, rows, :].astype(F32)
-        for j in range(3):
-            value = value + got[j, rows, :].astype(F32)
-        total[rows, :] = value
-
+    bufs = list(bufs)
+    take3 = lambda: [bufs.pop(0) for _ in range(3)]
+
+    def put_into(ref):
+        def put(at, cols, total):
+            ref[at, cols] = total
+
+        return put
+
+    clock, tasks = [0], []
+
+    def advance(until):
+        while clock[0] < until:
+            for t, steps in tasks:
+                if (clock[0] - t) % 2 == 0 and 0 <= (clock[0] - t) // 2 < len(steps):
+                    steps[(clock[0] - t) // 2]()
+            clock[0] += 1
+
+    loads[0].wait()
+    tasks.append((0, scatter_steps(net, dw_down, 128, 0, 512, [], *take3(), put_into(o_down))))
+    tasks.append((1, scatter_steps(net, dw_down, 128, 512, 512, [], *take3(), put_into(o_down))))
+    tasks.append((2, scatter_steps(net, dw_up, 64, 0, 1024, [loads[1]], *take3(), put_into(s_up))))
+    tasks.append((3, scatter_steps(net, dw_up, 64, 1024, 1024, [], *take3(), put_into(s_up))))
+    advance(2)
+    loads[2].wait()
+    swaps = []
+    for h in range(8):
+        theirs = dw_out.at[pl.ds(h * 64 + (1 - c) * 32, 32)]
+        swaps.append(net.copy(theirs, spread.at[pl.ds((8 * c + h) * 32, 32)], net.core))
+        spread[pl.ds(pl.multiple_of((8 * c + h) * 32, 32), 32), :] = dw_out[pl.ds(pl.multiple_of(h * 64 + c * 32, 32), 32), :]
+    tasks.append((4, scatter_steps(net, spread, 32, 0, 1024, [], *take3(), put_into(o_out))))
+
+    length = jnp.sum(jnp.sum(rows[pl.ds(chip * 2, 2), 5:7, :], axis=0), keepdims=True).astype(jnp.int32)
+    second = jnp.broadcast_to(small[7:8, :], (PROMPT, 128)) > 0.5
+    weight = small[7:8, :]
+    pair_sends = []
+
+    def back_pair(pair):
+        k_at, v_at = pl.ds(128 * pair, 128), pl.ds(HC + 128 * pair, 128)
+        prompts = [(kv[p * PROMPT : (p + 1) * PROMPT, k_at], kv[p * PROMPT : (p + 1) * PROMPT, v_at]) for p in range(2)]
+        chosen = [jnp.where(second, b.astype(F32), a.astype(F32)).astype(BF) for a, b in zip(*prompts)]
+
+        def both_heads(row, size, keys, values, masks, place):
+            dq, dks, dvs = [], None, None
+            for head in range(2):
+                stat = lse[2 * pair + head, :, row : row + size]
+                d, k_parts, v_parts = attend_back(
+                    q[row : row + size, k_at], att_grad[row : row + size, k_at], keys, values, masks, stat, head
+                )
+                dq.append(d)
+                dks = k_parts if dks is None else [a + b for a, b in zip(dks, k_parts)]
+                dvs = v_parts if dvs is None else [a + b for a, b in zip(dvs, v_parts)]
+            dq = jnp.concatenate(dq, axis=0).T
+            projected[row : row + size, k_at] = turn(dq, rotary[pl.ds(place, size), :], -1.0).astype(BF)
+            return dks, dvs
+
+        near_k, near_v = None, None
+        for i in range(2):
+            near = 256 * i + 256
+            masks = [None, seen(0, 256 * i, (near, 256), length)]
+            near_keys = kv[2 * PROMPT : 2 * PROMPT + near, k_at], kv[2 * PROMPT : 2 * PROMPT + near, v_at]
+            dks, dvs = both_heads(
+                256 + 256 * i, 256, [chosen[0], near_keys[0]], [chosen[1], near_keys[1]], masks, PROMPT + 256 * i
+            )
+            if i == 0:
+                far_k[...], far_v[...] = dks[0], dvs[0]
+                near_k, near_v = dks[1], dvs[1]
+            else:
+                far_k[...] = far_k[...] + dks[0]
+                far_v[...] = far_v[...] + dvs[0]
+                near_k = [near_k + dks[1][:256], dks[1][256:]]
+                near_v = [near_v + dvs[1][:256], dvs[1][256:]]
+        for i in range(2):
+            at = slice(256 + 256 * i, 512 + 256 * i)
+            table = rotary[PROMPT + 256 * i : PROMPT + 256 * i + 256, :]
+            projected[at, HC + 128 * pair : HC + 128 * pair + 128] = turn(near_k[i], table, -1.0).astype(BF)
+            projected[at, 2 * HC + 128 * pair : 2 * HC + 128 * pair + 128] = near_v[i].astype(BF)
+        for p in range(2):
+            place = pl.multiple_of(z * 2 * PSH, 128)
+            dks, dvs = both_heads(
+                128 * p, 128, [prompts[p][0]], [prompts[p][1]], [seen(0, z * 2 * PSH, (PROMPT, 128))], place
+            )
+            share = weight if p == 1 else 1.0 - weight
+            at = slice(p * PROMPT, p * PROMPT + PROMPT)
+            pairs[pair, at, :128] = (dks[0] + share * far_k[...]).astype(BF)
+            pairs[pair, at, 128:] = (dvs[0] + share * far_v[...]).astype(BF)
+        for j in (1, 2, 3):
+            for p in range(2):
+                there = pl.ds(p * PROMPT + (z + j) % RANKS * 2 * PSH, 2 * PSH)
+                pair_sends.append(
+                    net.copy(pairs.at[pair, there], got_pairs.at[j - 1, pair, pl.ds(p * 2 * PSH, 2 * PSH)], net.line[j - 1])
+                )
+
+    back_pair(0)
+    advance(3)
+    back_pair(1)
+    advance(4)
+    for made in swaps:
+        made.wait_recv()
+    back_pair(2)
+    advance(5)
+    back_pair(3)
+    advance(6)
+    for made in pair_sends:
+        made.wait_recv()
+    table = rotary[pl.ds(pl.multiple_of(z * 2 * PSH, 128), 128), :]
+    for pair in range(4):
+        for p in range(2):
+            at = slice(p * 128, p * 128 + 128)
+            total = pairs[pair, pl.ds(pl.multiple_of(p * PROMPT + z * 2 * PSH, 128), 128), :].astype(F32)
+            for j in range(3):
+                total = total + got_pairs[j, pair, at, :].astype(F32)
+            projected[at, HC + 128 * pair : HC + 128 * pair + 128] = turn(total[:, :128], table, -1.0).astype(BF)
+            projected[at, 2 * HC + 128 * pair : 2 * HC + 128 * pair + 128] = total[:, 128:].astype(BF)
+
+    def weight_columns(col, width):
+        @pl.loop(0, D // 256)
+        def _(i):
+            part = tn(first[:, tile_at(i, 256)], projected[:, col : col + width])
+            dw_qkv[tile_at(i, 256), col : col + width] = part.astype(BF)
+
+    weight_columns(0, 768)
+    tasks.append((6, scatter_steps(net, dw_qkv, 64, 0, 768, [], *take3(), put_into(s_qkv))))
+    advance(7)
+    weight_columns(768, 768)
+    tasks.append((7, scatter_steps(net, dw_qkv, 64, 768, 768, [], *take3(), put_into(s_qkv))))
+    advance(8)
+    fg_sum, fg_normed = jnp.zeros((1, D), F32), jnp.zeros((1, D), F32)
+    bias = jnp.zeros((1, 3 * HC), F32)
+
+    def first_rows(i, sums):
+        at = tile_at(i, 128)
+        here = projected[at, :]
+        grad = nt(here, w_qkv[...])
+        normed = norm_rows(x[at, :])
+        joint[at, :] = grad * gain[...] + joint_in[at, :]
+        return (
+            sums[0] + jnp.sum(grad, axis=0, keepdims=True),
+            sums[1] + jnp.sum(grad * normed, axis=0, keepdims=True),
+            sums[2] + jnp.sum(here.astype(F32), axis=0, keepdims=True),
+        )
+
+    fg_sum, fg_normed, bias = lax.fori_loop(0, ROWS // 128, first_rows, (fg_sum, fg_normed, bias))
+    ranges = ((0, PSH, lambda o: o * PSH), (PSH, PSH, lambda o: 2 * PSH + o * PSH), (2 * PSH, HALF, lambda o: 4 * PSH + o * HALF))
+    joints = [
+        net.copy(joint.at[pl.ds(there(1 - c), size)], peer_joint.at[pl.ds(at, size)], net.core) for at, size, there in ranges
+    ]
+    for i in range(8):
+        cols = slice(128 * i, 128 * i + 128)
+        value[i : i + 1, :] = value[i : i + 1, :] + fg_normed[:, cols]
+        value[8 + i : 9 + i, :] = value[8 + i : 9 + i, :] + fg_sum[:, cols]
+    for i in range(12):
+        row = pl.ds(40 + i // 4 * 8 + c * 4 + i % 4, 1)
+        value[row, :] = value[row, :] + bias[:, 128 * i : 128 * i + 128]
+    sums = sum_steps(net, value, got_s)
+    sums[0]()
+    advance(9)
+    for made in joints:
+        made.wait_recv()
+    for at, size, there in ranges:
+        mine = pl.ds(pl.multiple_of(there(c), 64), size)
+        joint_own[at : at + size, :] = joint[mine, :] + peer_joint[at : at + size, :]
+    sums[1]()
+    advance(10)
+    sums[2]()
+    ups = []
+
+    def give(total, peer_ref):
+        return net.copy(total.at[pl.ds((1 - c) * 32, 32)], peer_ref, net.core)
+
+    advance(11)
+    ups.append(give(s_up, peer_up))
+    sums[3]()
+    advance(12)
+    sums[4]()
+    advance(16)
+    ups.append(give(s_qkv, peer_qkv))
+    own_rows = pl.ds(pl.multiple_of(c * 32, 32), 32)
+    ups[0].wait_recv()
+    for i in range(16):
+        for who, part in ((c, s_up[own_rows, 128 * i : 128 * i + 128]), (1 - c, peer_up[:, 128 * i : 128 * i + 128])):
+            o_up[:, pl.ds(pl.multiple_of((2 * i + who) * 128, 128), 128)] = part
+    ups[1].wait_recv()
+    for i in range(3):
+        for who, part in ((c, s_qkv[own_rows, HC * i : HC * i + HC]), (1 - c, peer_qkv[:, HC * i : HC * i + HC])):
+            o_qkv[:, pl.ds(pl.multiple_of(i * D + who * HC, 128), HC)] = part
     net.leave()
 
 
-def scatter_line(pair):
-    _, n, w = pair.shape
+def backward(*args):
+    shape = jax.ShapeDtypeStruct
+    bufs = []
+    for rb, width, count in ((128, 512, 2), (64, 1024, 2), (32, 1024, 1), (64, 768, 2)):
+        for _ in range(count):
+            bufs += [pltpu.VMEM((12 * rb, width // 2), BF), pltpu.VMEM((12 * rb, width // 2), BF), pltpu.VMEM((3, rb, width), BF)]
     return pl.pallas_call(
-        scatter_line_kernel,
-        out_shape=jax.ShapeDtypeStruct((n, w), F32),
-        in_specs=[VM],
-        out_specs=VM,
-        scratch_shapes=[pltpu.VMEM((4, n, w), pair.dtype), pltpu.VMEM((3, n, w), pair.dtype), pltpu.SemaphoreType.DMA((4,)), pltpu.SemaphoreType.DMA((4,))],
-        compiler_params=pltpu.CompilerParams(collective_id=2, has_side_effects=True, vmem_limit_bytes=32 << 20),
-    )(pair)
-
-
-def scatter_kernel(value, qkv, out, up, down, o_sum, o_qkv, o_out, o_up, o_down, got_s, *scratch):
-    bufs, (send, recv) = scratch[:-2], scratch[-2:]
-    net = Net(send, recv)
-    net.enter()
-    o_sum[...] = value[...]
-    tasks = [sum_steps(net, o_sum, got_s)]
-    plan = ((down, 128, o_down), (up, 64, o_up), (out, 32, o_out), (qkv, 64, o_qkv))
-    for i, (src, rb, total) in enumerate(plan):
-        held = bufs[4 * i]
-        move_rows(held, 0, src, 0, src.shape[0])
-        tasks.append(scatter_steps(net, held, rb, *bufs[4 * i + 1 : 4 * i + 4], total))
-    run_diagonal(tasks)
-    net.leave()
-
-
-def scatter_all(value, qkv, out, up, down):
-    shape = jax.ShapeDtypeStruct
-    n = value.shape[0]
-    bufs = []
-    for src in (down, up, out, qkv):
-        rb, cols = src.shape[0] // 16, src.shape[1]
-        bufs += [pltpu.VMEM(src.shape, BF), pltpu.VMEM((12 * rb, cols // 2), BF), pltpu.VMEM((12 * rb, cols // 2), BF), pltpu.VMEM((3, rb, cols), BF)]
-    return pl.pallas_call(
-        scatter_kernel,
+        backward_kernel,
         out_shape=(
-            shape((n, 128), F32), shape((64, 3 * HC), F32), shape((32, D), F32), shape((64, FF // 2), F32), shape((128, D), F32),
+            shape((104, 128), F32), shape((32, 3 * D), F32), shape((32, D), F32), shape((32, FF), F32), shape((128, D), F32),
+            shape((384, D), F32),
         ),
-        in_specs=[VM] * 5,
-        out_specs=(VM,) * 5,
-        scratch_shapes=[pltpu.VMEM((7, n, 128), F32)] + bufs
-        + [pltpu.SemaphoreType.DMA((64,)), pltpu.SemaphoreType.DMA((64,))],
-        compiler_params=pltpu.CompilerParams(collective_id=3, has_side_effects=True, vmem_limit_bytes=56 << 20),
-    )(value, qkv, out, up, down)
+        in_specs=[VM] * 13 + [pl.BlockSpec(memory_space=pl.ANY)] * 3,
+        out_specs=(VM,) * 6,
+        scratch_shapes=[
+            pltpu.VMEM((D, 3 * HC), BF), pltpu.VMEM((HC, D), BF), pltpu.VMEM((FF // 2, D), BF), pltpu.VMEM((D, FF // 2), BF),
+            pltpu.VMEM((HC, D), BF), pltpu.VMEM((4, 2 * PROMPT, 256), BF), pltpu.VMEM((3, 4, 4 * PSH, 256), BF),
+            pltpu.VMEM((PROMPT, 128), F32), pltpu.VMEM((PROMPT, 128), F32), pltpu.VMEM((ROWS, 3 * HC), BF),
+            pltpu.VMEM((ROWS, D), F32), pltpu.VMEM((384, D), F32), pltpu.VMEM((7, 104, 128), F32),
+            pltpu.VMEM((64, 3 * HC), F32), pltpu.VMEM((64, FF // 2), F32), pltpu.VMEM((32, 3 * HC), F32), pltpu.VMEM((32, FF // 2), F32),
+        ] + bufs
+        + [pltpu.SemaphoreType.DMA((140,)), pltpu.SemaphoreType.DMA((140,)), pltpu.SemaphoreType.DMA((4,))],
+        compiler_params=pltpu.CompilerParams(collective_id=1, has_side_effects=True, vmem_limit_bytes=63 << 20),
+    )(*args)
 
 
 def fast_body(
     tokens, valid, prompt_of, teacher, cotangent,
     ln1_gain, ln1_bias, ln2_gain, ln2_bias, qkv_weight, qkv_bias, out_weight, out_bias,
-    up_weight, up_bias, down_weight, down_bias, stop=None,
+    up_weight, up_bias, down_weight, down_bias,
 ):
     c = lax.axis_index("core")
     z = lax.axis_index("chip")
@@ -886,7 +1067,7 @@
             jnp.broadcast_to(prompt_of.astype(F32)[:, None], (1, 128)),
         ]
     )
-    rows, w_qkv, w_out, w_up, w_down, x_all, first_all, second_in, q, kv, attended, lse, activated, slope = forward(
+    rows, w_qkv, w_out, w_up, w_down, x_own, first_own, second_in, q, kv, attended, lse, activated, slope = forward(
         tokens,
         small,
         qkv_weight.reshape(32, 3, 2, HC).transpose(2, 0, 1, 3).reshape(2, 32, 3 * HC),
@@ -894,23 +1075,10 @@
         up_weight.reshape(32, 16, 2, 128).transpose(2, 0, 1, 3).reshape(2, 32, FF // 2),
         down_weight,
     )
-    def own_of(a):
-        prompts = lax.dynamic_slice_in_dim(a[: 2 * PROMPT].reshape(2, PROMPT, -1), z * 2 * PSH, 2 * PSH, axis=1)
-        return jnp.concatenate([prompts.reshape(4 * PSH, -1), a[2 * PROMPT :]])
-    x = own_of(x_all).astype(F32)
-    first_in = own_of(first_all)
-    prompt_kv = kv[: 2 * PROMPT].reshape(2, 4, 2 * PSH, 2 * HC).swapaxes(0, 1)
-    kv = own_of(kv)
-    lse = lse[:, 0]
-    normed, rstd = normalize(x)
+    normed, _ = normalize(x_own.astype(F32))
     gain1, bias1, gain2, bias2 = (rows[:, 0, 32 * i : 32 * i + 32].reshape(-1) for i in range(4))
     b_out, b_down = (rows[:, 1, 32 * i : 32 * i + 32].reshape(-1) for i in range(2))
     count_all = jnp.sum(rows[:, 4:7])
-    places = places_of(z, chips)
-    turn_own = lambda v, d: rotate_heads(v.reshape(-1, nh, HD), places, d).reshape(-1, HC)
-    cont_valid = lax.dynamic_slice_in_dim(rows, (device // 2) * 2, 2)[:, 5:7].reshape(-1)
-    masks = masks_of(z, chips, cont_valid)
-    chosen = prompt_of[0]
     partial = dot(attended, w_out, (1, 0)) + dot(activated, w_down, (1, 0))
     halves = split_rows(partial)
     take = lambda a: lax.dynamic_index_in_dim(a, c, axis=0, keepdims=False)
@@ -921,8 +1089,6 @@
     squared = jnp.sum(live * missed * missed)
     out_grad = cotangent.astype(F32) + 2.0 / (count_all * D) * live * missed
     out_low = pair_rows(out_grad.astype(BF))
-    if stop == "fwd":
-        return output
     out_bias_grad = jnp.sum(out_grad.astype(BF).astype(F32), axis=0)
     dw_out = dot(attended, out_low, (0, 0))
     dw_down = dot(activated, out_low, (0, 0))
@@ -931,56 +1097,36 @@
     dw_up = dot(second_in, hidden_grad, (0, 0))
     db_up = jnp.sum(hidden_grad.astype(F32), axis=0)
     second_grad = dot(hidden_grad, w_up, (1, 1))
-    dq, pair, near = g_attention_back(q, prompt_kv, kv, att_grad, lse, chosen, masks)
-    own_pair = scatter_line(pair.astype(BF).reshape(4, 4 * PSH, 2 * HC))
-    pair = jnp.concatenate([own_pair, near], axis=0)
-    projected_grad = jnp.concatenate([turn_own(dq, -1.0), turn_own(pair[:, :HC], -1.0), pair[:, HC:]], axis=1).astype(BF)
-    dw_qkv = dot(first_in, projected_grad, (0, 0))
-    db_qkv = jnp.sum(projected_grad.astype(F32), axis=0)
-    first_grad = dot(projected_grad, w_qkv, (1, 1))
-    if stop == "bwd":
-        return dw_out, dw_down, dw_up, dw_qkv, second_grad, first_grad, projected_grad, hidden_grad, att_grad
-    joint = first_grad * gain1 + second_grad * gain2
-    halves = split_rows(joint)
-    joint = take(halves) + swap_cores(give(halves))
-    own_normed = take(split_rows(normed))
-    own_rstd = take(split_rows(rstd))
+    wide = lambda v: jnp.zeros((v.shape[0], 2, v.shape[1]), F32).at[:, c].set(v).reshape(-1)
+    value = jnp.concatenate(
+        [
+            jnp.zeros((2 * D,), F32),
+            jnp.sum(second_grad * normed, axis=0),
+            jnp.sum(second_grad, axis=0),
+            out_bias_grad,
+            jnp.zeros((3 * D,), F32),
+            wide(db_up.reshape(-1, rd)),
+            jnp.full((128,), squared),
+            jnp.zeros((7 * 128,), F32),
+        ]
+    ).reshape(-1, 128)
+    value, s_qkv, s_out, s_up, s_down, joint = backward(
+        rows, small, value, gain1[None], jnp.asarray(rotary_table(PROMPT + CONT)), q, kv, att_grad, lse, first_own, x_own,
+        w_qkv, second_grad * gain2, dw_out.astype(BF), dw_down.astype(BF), dw_up.astype(BF),
+    )
+    own_normed, own_rstd = normalize(tokens.astype(F32))
     input_grad = out_grad + own_rstd * (
         joint
         - jnp.mean(joint, axis=-1, keepdims=True)
         - own_normed * jnp.mean(joint * own_normed, axis=-1, keepdims=True)
     )
-    wide = lambda v, n: jnp.zeros((v.shape[0], 2, v.shape[1]), F32).at[:, c].set(v).reshape(-1)
-    small = jnp.concatenate(
-        [
-            jnp.sum(first_grad * normed, axis=0),
-            jnp.sum(first_grad, axis=0),
-            jnp.sum(second_grad * normed, axis=0),
-            jnp.sum(second_grad, axis=0),
-            out_bias_grad,
-            wide(db_qkv.reshape(3, HC), 3),
-            wide(db_up.reshape(-1, rd), 16),
-        ]
-    )
-    small = jnp.concatenate([small, jnp.full((128,), squared), jnp.zeros((7 * 128,), F32)]).reshape(-1, 128)
-    pairs = lambda own, other, axis: jnp.where(c == 0, jnp.stack([own, other], axis), jnp.stack([other, own], axis))
-    o = dw_out.astype(BF).reshape(H // 2, 2, 32, D)
-    o_own = lax.dynamic_index_in_dim(o, c, axis=1, keepdims=False)
-    o_other = swap_cores(lax.dynamic_index_in_dim(o, 1 - c, axis=1, keepdims=False))
-    small, s_qkv, s_out, s_up, s_down = scatter_all(
-        small, dw_qkv.astype(BF), pairs(o_own, o_other, 0).reshape(-1, D), dw_up.astype(BF), dw_down.astype(BF)
-    )
-    s_qkv = s_qkv.reshape(2, 32, 3, HC)
-    s_up = s_up.reshape(2, 32, 16, 128)
-    s_qkv = pairs(take(s_qkv), swap_cores(give(s_qkv)), 2).reshape(32, 3 * D)
-    s_up = pairs(take(s_up), swap_cores(give(s_up)), 2).reshape(32, FF)
-    small = small.reshape(-1)
+    value = value.reshape(-1)
     shares, at = [], 0
     for size in (D, D, D, D, D, 3 * D, FF):
         own = size // lax.axis_size(ALL)
-        shares.append(lax.dynamic_slice_in_dim(small, at + device * own, own))
+        shares.append(lax.dynamic_slice_in_dim(value, at + device * own, own))
         at += size
-    loss_value = small[at] / (count_all * D)
+    loss_value = value[at] / (count_all * D)
     return (
         output.astype(BF), loss_value, input_grad, shares[0], shares[1], shares[2], shares[3],
         s_qkv, shares[5], s_out, shares[4], s_up, shares[6], s_down, shares[4],

time: 630 us -> 395 us (0.63)
  local copies, waits for them, and re-layouts: 117 us -> 19.9 us
  matrix products: 94.3 us -> 30.9 us
  Pallas kernels: 351 us -> 294 us
  other arithmetic: 36.7 us -> 16.8 us
  waiting for transfers between devices: 0.03 us -> 10 us
    dot_general x10 -> x0, matrix products: 48.9 us -> none  [the longest x2 18 us: back(): ein(f'{eq},{ek}->{eq[:-1]}k', query, key) * SCALE]
    pallas_call x2 -> x1, Pallas kernels: 184 us -> 141 us  [backward(): pl.pallas_call(backward_kernel, out_shape=(shape((104, 128), F32), shape(...]
    slice x16 -> x1, local copies, waits for them, and re-layouts: 27.3 us -> 1.34 us  [fast_body(): loss_value = value[at] / (count_all * D)]
    unnamed x156 -> x80, local copies, waits for them, and re-layouts: 21.2 us -> 5.62 us
    dot_general x10 -> x8, matrix products: 45.3 us -> 30.9 us  [dot(): lax.dot_general(a, b, ((contract[:1], contract[1:]), ((), ())), preferred...]
    pallas_call x1, Pallas kernels: 166 us -> 152 us  [forward(): pl.pallas_call(forward_kernel, out_shape=(shape((32, 8, 128), F32), shape...]
    convert_element_type x5 -> x0, other arithmetic: 11.1 us -> none  [the longest x2 8.07 us: back(): score_grad = (probs * (prob_grad - inner)).astype(BF)]
    reshape x7 -> x0, local copies, waits for them, and re-layouts: 9.67 us -> none  [the longest x1 4.14 us: g_attention_back(): pk = pk.reshape(2, nh, 2, chips * 2 * PSH, HD)]
  transfers between devices with their start and end apart: 6 -> 2, of which waited for: 0 -> 2; matrix products, arithmetic and copies ran while one was open for 16% -> 1% of each run, Pallas kernels for 22% -> 0%
where the time goes in v3:
time: 395 us; the launch traced here: 390 us
  Pallas kernels  294 us (74%)
  matrix products  30.9 us (8%)
  local copies, waits for them, and re-layouts  19.9 us (5%)
  between operations  17.9 us (5%)
  other arithmetic  16.8 us (4%)
  waiting for transfers between devices  10 us (3%)
    pallas_call x1, Pallas kernels, forward(): pl.pallas_call(forward_kernel, out_shape=(shape((32, 8, 128), F32), shape...  152 us
    pallas_call x1, Pallas kernels, backward(): pl.pallas_call(backward_kernel, out_shape=(shape((104, 128), F32), shape(...  141 us
    dot_general x8, matrix products, dot(): lax.dot_general(a, b, ((contract[:1], contract[1:]), ((), ())), preferred...  30.9 us
    all_gather x1, waiting for transfers between devices, pair_rows(): both = lax.all_gather(own, 'core', axis=0)  8.58 us
  transfers between devices with their start and end apart: 2, of which 2 were waited for; matrix products, arithmetic and copies ran while one was open for 1% of the time, Pallas kernels for 0%

profile of v3, /device:TPU:29, one launch (start us, length us, event | category | flops | bytes accessed | tf_op | source)
XLA Modules:
  0.0 389.7 jit_solution(1455858544331147326)
XLA Ops:
  7.3 0.8 fusion.27
  8.7 1.1 reshape.221
  9.9 0.8 reshape.222.up
  11.0 0.9 reshape.220.qkv
  12.7 152.2 %shard_map.307 = (f32[32,8,128]{2,1,0:T(8,128)}, bf16[1024,1536]{1,0:T(8,128)(2,1)}, bf16[512,1024]{1,0:T(8,128)(2,1)}, bf16[1024,2048]{1,0:T(8,128)(2,1)}, bf16...) custom-call(bf16[384,1024]{1,0:T(8,128)(2,1)} %tokens.1, ...), custom_call_target="tpu_custom_call" | custom-call | tf_op jit(solution)/shard_map/pallas_call | solution.py:689
  165.0 6.3 %fusion.30 = f32[768,1024]{1,0:T(8,128)S(1)} fusion(bf16[768,2048]{1,0:T(8,128)(2,1)} %get-tuple-element.49, bf16[2048,1024]{1,0:T(8,128)(2,1)} %get-tuple-element.50), kind=kOutput, calls=%fused_computation.82 | convolution fusion | flops 3221225472 | bytes 10485760 | tf_op jit(solution)/shard_map/dot_general | solution.py:79
  171.3 1.0 convolution_add_fusion
  172.7 1.0 copy.41
  173.7 2.4 fusion.19
  178.7 1.4 collective-permute-done
  180.1 3.5 fusion.17
  183.7 1.2 convert_reduce_fusion.3
  185.8 0.7 and_reduce_fusion
  187.4 8.6 %all-gather.3.cloned.1.call-done = bf16[768,1024]{1,0:T(8,128)(2,1)} async-done(((bf16[384,1024]{1,0:T(8,128)(2,1)}), bf16[768,1024]{1,0:T(8,128)(2,1)}) %all-gather.3.cloned.1.call-update) | async-done | bytes 1572880 | tf_op jit(solution)/shard_map/all_gather | solution.py:35
  196.0 1.2 slice.61
  197.2 1.4 slice.62
  198.7 5.1 %convolution_convert_fusion.1.dw_down_in = bf16[2048,1024]{1,0:T(8,128)(2,1)} fusion(bf16[768,2048]{1,0:T(8,128)(2,1)S(1)} %copy-done.28, bf16[512,1024]{1,0:T(8,128)(2,1)S(1)} %bitcast.69, bf16[256,1024]{1,0:T(8,128)(2,1)S(1)} %bitcast.74), kind=kOutput, calls=%fused_computation.7 | convolution fusion | flops 3226468352 | bytes 8912896 | tf_op jit(solution)/shard_map/dot_general | solution.py:79
  203.9 2.0 convolution_convert_fusion.2.dw_out_in
  205.9 1.9 convolution_convert_fusion.3.att_grad
  208.4 3.7 convert_reduce_fusion
  212.1 5.5 %convolution_convert_fusion.dw_up_in = bf16[1024,2048]{1,0:T(8,128)(2,1)} fusion(bf16[768,1024]{1,0:T(8,128)(2,1)S(1)} %copy-done.29, bf16[768,2048]{1,0:T(8,128)(2,1)S(1)} %get-tuple-element.91), kind=kOutput, calls=%fused_computation.6 | convolution fusion | flops 3223322624 | bytes 8912896 | tf_op jit(solution)/shard_map/dot_general | solution.py:79
  217.6 5.3 %fusion.24 = (f32[1024]{0:T(1024)S(1)}, f32[1024]{0:T(1024)S(1)}, f32[768,1024]{1,0:T(8,128)}) fusion(f32[768]{0:T(1024)S(1)} %add_rsqrt_fusion, f32[768]{0:T(1024)S(1)} %broadcast_multiply_fusion.1, bf16[768,1024]{1,0:T(8,128)(2,1)S(1)} %copy-done.3, f32[1024]{0:T(1024)S(1)} %mul.117, bf16[768,2048]{1,0:T(8,128)(2,1)S(1)} %get-tuple-element.91, ...), kind=kOutput, calls=%fused_computation.78 | convolution fusion | flops 3226728448 | bytes 12077056 | tf_op jit(solution)/shard_map/dot_general | solution.py:79
  225.0 141.3 %shard_map.308 = (f32[104,128]{1,0:T(8,128)}, f32[32,3072]{1,0:T(8,128)}, f32[32,1024]{1,0:T(8,128)}, f32[32,4096]{1,0:T(8,128)}, f32[128,1024]{1,0:T(8,128)}, /*index=5*/f32[384,1024]{1,0:T(8,128)}) custom-call(f32[32,8,128]{2,1,0:T(8,128)} %get-tuple-element.51.rows, f32[8,128]{1,0:T(8,128)} %concatenate.43.small, f32[104,128]{1,0:T(8,128)} %bitcast.78, ...), custom_call_target="tpu_custom_call" | custom-call | tf_op jit(solution)/shard_map/pallas_call | solution.py:1027
  366.4 1.3 slice.63
  368.4 1.9 fusion.25
  370.3 1.3 fusion.29
  371.6 1.3 dynamic_slice.34
  372.9 1.3 dynamic_slice.36
  374.2 3.8 fusion.12
  378.5 0.7 copy.62
  379.9 0.8 copy.64
  380.7 0.8 copy.65
  (113 shorter events, 8.9 us)
Async XLA Ops:
  7.2 3.5 copy-start.15
  7.2 4.7 %copy-start.23 = (bf16[96]{0:T(256)(128)(2,1)S(1)}, bf16[96]{0:T(256)(128)(2,1)}, u32[]{:S(2)}) copy-start(bf16[96]{0:T(256)(128)(2,1)} %param.32) | copy-start | bytes 580
  7.2 4.7 %copy-start.22 = (bf16[128]{0:T(256)(128)(2,1)S(1)}, bf16[128]{0:T(256)(128)(2,1)}, u32[]{:S(2)}) copy-start(bf16[128]{0:T(256)(128)(2,1)} %param.36) | copy-start | bytes 772
  7.2 4.7 %copy-start.31 = (bf16[32]{0:T(256)(128)(2,1)S(1)}, bf16[32]{0:T(256)(128)(2,1)}, u32[]{:S(2)}) copy-start(bf16[32]{0:T(256)(128)(2,1)} %param.34) | copy-start | bytes 196
  7.2 4.7 %copy-start.30 = (bf16[32]{0:T(256)(128)(2,1)S(1)}, bf16[32]{0:T(256)(128)(2,1)}, u32[]{:S(2)}) copy-start(bf16[32]{0:T(256)(128)(2,1)} %param.38) | copy-start | bytes 196
  7.2 4.8 %copy-start.21 = (bf16[32]{0:T(256)(128)(2,1)S(1)}, bf16[32]{0:T(256)(128)(2,1)}, u32[]{:S(2)}) copy-start(bf16[32]{0:T(256)(128)(2,1)} %param.27) | copy-start | bytes 196
  7.2 4.8 %copy-start.20 = (bf16[32]{0:T(256)(128)(2,1)S(1)}, bf16[32]{0:T(256)(128)(2,1)}, u32[]{:S(2)}) copy-start(bf16[32]{0:T(256)(128)(2,1)} %param.28) | copy-start | bytes 196
  7.3 4.8 %copy-start.19 = (bf16[32]{0:T(256)(128)(2,1)S(1)}, bf16[32]{0:T(256)(128)(2,1)}, u32[]{:S(2)}) copy-start(bf16[32]{0:T(256)(128)(2,1)} %param.29) | copy-start | bytes 196
  7.3 4.8 %copy-start.18 = (bf16[32]{0:T(256)(128)(2,1)S(1)}, bf16[32]{0:T(256)(128)(2,1)}, u32[]{:S(2)}) copy-start(bf16[32]{0:T(256)(128)(2,1)} %param.30) | copy-start | bytes 196
  7.3 188.7 %all-gather.3.cloned.1.call-start = ((), (), s32[]{:S(2)}) async-start(), calls=%async_computation | async-start | bytes 2359296 | tf_op jit(solution)/shard_map/all_gather | solution.py:35
  165.0 6.3 %copy-start.7 = (bf16[512,1024]{1,0:T(8,128)(2,1)S(1)}, bf16[512,1024]{1,0:T(8,128)(2,1)}, u32[]{:S(2)}) copy-start(bf16[512,1024]{1,0:T(8,128)(2,1)} %get-tuple-element.48) | copy-start | bytes 3145732
  165.0 6.3 %copy-start.9 = (bf16[768,512]{1,0:T(8,128)(2,1)S(1)}, bf16[768,512]{1,0:T(8,128)(2,1)}, u32[]{:S(2)}) copy-start(bf16[768,512]{1,0:T(8,128)(2,1)} %get-tuple-element.47) | copy-start | bytes 2359300
  173.7 3.0 copy-start.11
  173.7 4.7 %copy-start = (bf16[384,1024]{1,0:T(8,128)(2,1)S(1)}, bf16[384,1024]{1,0:T(8,128)(2,1)}, u32[]{:S(2)}) copy-start(bf16[384,1024]{1,0:T(8,128)(2,1)} %tokens.1) | copy-start | bytes 2359300
  176.1 4.0 %collective-permute-start = (f32[384,1024]{1,0:T(8,128)}, f32[384,1024]{1,0:T(8,128)}, u32[]{:S(2)}, u32[]{:S(2)}) collective-permute-start(f32[384,1024]{1,0:T(8,128)} %fusion.19), channel_id=1, source_target_pairs={{0,1},{1,0},{2,3},{3,2},{4,5},{5,4},{6,7},{7,6},{8,9},{9,8},{10,11... | collective-permute-start | bytes 4718600 | tf_op jit(solution)/shard_map/ppermute | solution.py:31
  180.1 3.5 copy-start.4
  180.1 3.5 copy-start.6
  183.7 2.9 copy-start.3
  196.0 2.7 copy-start.28
  197.2 10.6 %slice-start = ((s8[6291456]{0:T(1024)(128)(4,1)}), s8[4194304]{0:T(1024)(128)(4,1)S(1)}, s32[]{:S(2)}) async-start(s8[6291456]{0:T(1024)(128)(4,1)} %bitcast.89), calls=%async_computation.1 | async-start | bytes 8388608
  198.7 5.2 %copy-start.10 = (bf16[768,512]{1,0:T(8,128)(2,1)S(1)}, bf16[768,512]{1,0:T(8,128)(2,1)}, u32[]{:S(2)}) copy-start(bf16[768,512]{1,0:T(8,128)(2,1)} %get-tuple-element.47) | copy-start | bytes 2359300
  198.7 9.1 %slice-start.1 = ((s8[6291456]{0:T(1024)(128)(4,1)}), s8[2097152]{0:T(1024)(128)(4,1)S(1)}, s32[]{:S(2)}) async-start(s8[6291456]{0:T(1024)(128)(4,1)} %bitcast.89), calls=%async_computation.2 | async-start | bytes 4194304
  205.9 2.5 copy-start.27
  208.4 3.7 copy-start.29
  212.1 5.5 %copy-start.26 = (bf16[1024,2048]{1,0:T(8,128)(2,1)S(1)}, bf16[1024,2048]{1,0:T(8,128)(2,1)}, u32[]{:S(2)}) copy-start(bf16[1024,2048]{1,0:T(8,128)(2,1)} %get-tuple-element.53) | copy-start | bytes 12582916
  366.4 7.8 %copy-start.2 = (f32[384,1024]{1,0:T(8,128)S(1)}, f32[384,1024]{1,0:T(8,128)}, u32[]{:S(2)}) copy-start(f32[384,1024]{1,0:T(8,128)} %copy-done.1) | copy-start | bytes 4718596
  366.4 7.8 %copy-start.5 = (bf16[384,1024]{1,0:T(8,128)(2,1)S(1)}, bf16[384,1024]{1,0:T(8,128)(2,1)}, u32[]{:S(2)}) copy-start(bf16[384,1024]{1,0:T(8,128)(2,1)} %param.25) | copy-start | bytes 2359300
  371.6 6.4 %copy-start.25 = (f32[32]{0:T(128)}, f32[32]{0:T(128)S(1)}, u32[]{:S(2)}) copy-start(f32[32]{0:T(128)S(1)} %get-tuple-element.149) | copy-start | bytes 388
  374.1 4.4 %copy-start.14 = (f32[32,3072]{1,0:T(8,128)S(1)}, f32[32,3072]{1,0:T(8,128)}, u32[]{:S(2)}) copy-start(f32[32,3072]{1,0:T(8,128)} %get-tuple-element.146) | copy-start | bytes 1179652
  374.2 5.1 %copy-start.16 = (f32[32,1024]{1,0:T(8,128)S(1)}, f32[32,1024]{1,0:T(8,128)}, u32[]{:S(2)}) copy-start(f32[32,1024]{1,0:T(8,128)} %get-tuple-element.148) | copy-start | bytes 393220
  374.2 5.8 %copy-start.13 = (f32[32,4096]{1,0:T(8,128)S(1)}, f32[32,4096]{1,0:T(8,128)}, u32[]{:S(2)}) copy-start(f32[32,4096]{1,0:T(8,128)} %get-tuple-element.150) | copy-start | bytes 1572868
  378.0 2.7 copy-start.12
  (4 other events, 6.2 us)
Sparse Core Ops, SparseCore 0:
  185.2 10.7 all-gather.2

commit v4 on v3

--- a/solution.py
+++ b/solution.py
@@ -507,9 +507,9 @@
 
 
 def forward_kernel(
-    tokens, small, qkv, out, up, down, rotary, index,
-    rows, w_qkv, w_out, w_up, w_down, x_own, first_own, second_in, q, kv, attended, lse, activated, slope,
-    x_all, first_in, spread, swapped, send, recv,
+    tokens, small, qkv, out, up, down, rotary, index, teacher, cotangent,
+    rows, w_qkv, x_own, first_own, q, kv, lse, dw_out, dw_down, dw_up, att_grad, joint, output, out_grad, value,
+    w_out, w_up, w_down, second_in, attended, activated, slope, peer, low, x_all, first_in, spread, swapped, send, recv,
 ):
     net = Net(send, recv)
     c, z, chip = net.c, net.z, net.chip
@@ -681,26 +681,135 @@
     for h in range(8):
         w_out[pl.ds(pl.multiple_of(h * 64 + c * 32, 32), 32), :] = spread[pl.ds(pl.multiple_of(c * 256 + h * 32, 32), 32), :]
         w_out[pl.ds(pl.multiple_of(h * 64 + (1 - c) * 32, 32), 32), :] = swapped[64 + h * 32 : 96 + h * 32, :D]
+
+    def share(at, size):
+        here = pl.ds(pl.multiple_of(at, 128), size)
+        joint[here, :] = nn(attended[here, :], w_out[...]) + nn(activated[here, :], w_down[...])
+
+    def chip_range(i, owner):
+        return ((owner * PSH, PSH, 0), (2 * PSH + owner * PSH, PSH, PSH), (4 * PSH + owner * HALF, HALF, 2 * PSH))[i]
+
+    def pass_share(i):
+        at, size, to = chip_range(i, 1 - c)
+        return net.copy(joint.at[pl.ds(pl.multiple_of(at, 64), size)], peer.at[pl.ds(to, size)], net.core)
+
+    share(4 * PSH + (1 - c) * HALF, HALF)
+    passed = [pass_share(2)]
+    share(0, 256)
+    passed += [pass_share(0), pass_share(1)]
+    share(4 * PSH + c * HALF, HALF)
+    for made in passed:
+        net.settle(made)
+    count = jnp.sum(jnp.sum(rows[:, 4:7, :], axis=0), keepdims=True)
+    pull = 2.0 / (count * D)
+    bias = spread_row(rows, 1, places, 4, 8, D) + spread_row(rows, 1, places, 4, 9, D)
+    value[...] = jnp.zeros_like(value)
+    squared, low_sum = jnp.zeros((1, D), F32), jnp.zeros((1, D), F32)
+    lows = []
+    for i in range(3):
+        at, size, to = chip_range(i, c)
+
+        def rows_out(k, sums, at=at, to=to, i=i):
+            here = pl.ds(pl.multiple_of(at + k * 64, 64), 64)
+            own = pl.ds(pl.multiple_of(to + k * 64, 64), 64)
+            result = tokens[own, :].astype(F32) + joint[here, :] + peer[own, :] + bias
+            missed = result - teacher[own, :].astype(F32)
+            if i == 2:
+                step = lax.broadcasted_iota(jnp.int32, (64, D), 0) + (c * HALF + k * 64)
+                missed = jnp.where(step < length, missed, 0.0)
+            output[own, :] = result.astype(BF)
+            grad = cotangent[own, :].astype(F32) + pull * missed
+            out_grad[own, :] = grad
+            rounded = grad.astype(BF)
+            low[here, :] = rounded
+            return (
+                sums[0] + jnp.sum(missed * missed, axis=0, keepdims=True),
+                sums[1] + jnp.sum(rounded.astype(F32), axis=0, keepdims=True),
+            )
+
+        squared, low_sum = lax.fori_loop(0, size // 64, rows_out, (squared, low_sum))
+        lows.append(net.same(low.at[pl.ds(pl.multiple_of(at, 64), size)], net.core))
+    total = jnp.sum(squared, keepdims=True)
+    value[96:97, :] = jnp.broadcast_to(total, (1, 128))
+
+    def put_row(row, vector):
+        for k in range(vector.shape[1] // 128):
+            value[row + k : row + k + 1, :] = vector[:, 128 * k : 128 * k + 128]
+
+    put_row(32, low_sum)
+    for made in lows:
+        made.wait_recv()
+
+    @pl.loop(0, 8)
+    def _(i):
+        at = tile_at(i, 256)
+        dw_down[at, :] = tn(activated[:, at], low[...]).astype(BF)
+
+    @pl.loop(0, 2)
+    def _(i):
+        at = tile_at(i, 256)
+        dw_out[at, :] = tn(attended[:, at], low[...]).astype(BF)
+
+    @pl.loop(0, ROWS // 128)
+    def _(i):
+        at = tile_at(i, 128)
+        att_grad[at, :] = nt(low[at, :], w_out[...]).astype(BF)
+
+    for j in range(8):
+        cols = slice(256 * j, 256 * j + 256)
+
+        def hidden_rows(i, total, cols=cols):
+            at = tile_at(i, 256)
+            grad = (nt(low[at, :], w_down[cols, :]) * slope[at, cols].astype(F32)).astype(BF)
+            activated[at, cols] = grad
+            return total + jnp.sum(grad.astype(F32), axis=0, keepdims=True)
+
+        total = lax.fori_loop(0, ROWS // 256, hidden_rows, jnp.zeros((1, 256), F32))
+        for k in range(2):
+            value[pl.ds(64 + 4 * j + 2 * k + c, 1), :] = total[:, 128 * k : 128 * k + 128]
+
+    @pl.loop(0, 4)
+    def _(i):
+        at = tile_at(i, 256)
+        for k in range(2):
+            cols = slice(1024 * k, 1024 * k + 1024)
+            dw_up[at, cols] = tn(second_in[:, at], activated[:, cols]).astype(BF)
+
+    def second_rows(i, sums):
+        at = tile_at(i, 128)
+        grad = nt(activated[at, :], w_up[...])
+        joint[at, :] = grad * gain2
+        normed = norm_rows(x_own[at, :])
+        return (
+            sums[0] + jnp.sum(grad * normed, axis=0, keepdims=True),
+            sums[1] + jnp.sum(grad, axis=0, keepdims=True),
+        )
+
+    sums = lax.fori_loop(0, ROWS // 128, second_rows, (jnp.zeros((1, D), F32), jnp.zeros((1, D), F32)))
+    put_row(16, sums[0])
+    put_row(24, sums[1])
     net.leave()
 
 
-def forward(tokens, small, qkv, out, up, down):
+def forward(tokens, small, qkv, out, up, down, teacher, cotangent):
     shape = jax.ShapeDtypeStruct
     return pl.pallas_call(
         forward_kernel,
         out_shape=(
-            shape((32, 8, 128), F32), shape((D, 3 * HC), BF), shape((HC, D), BF), shape((D, FF // 2), BF), shape((FF // 2, D), BF),
-            shape((ROWS, D), BF), shape((ROWS, D), BF), shape((ROWS, D), BF), shape((ROWS, HC), BF), shape((KEYS, 2 * HC), BF),
-            shape((ROWS, HC), BF), shape((8, 1, ROWS), F32), shape((ROWS, FF // 2), BF), shape((ROWS, FF // 2), F32),
+            shape((32, 8, 128), F32), shape((D, 3 * HC), BF), shape((ROWS, D), BF), shape((ROWS, D), BF), shape((ROWS, HC), BF),
+            shape((KEYS, 2 * HC), BF), shape((8, 1, ROWS), F32), shape((HC, D), BF), shape((FF // 2, D), BF), shape((D, FF // 2), BF),
+            shape((ROWS, HC), BF), shape((ROWS, D), F32), shape((384, D), BF), shape((384, D), F32), shape((104, 128), F32),
         ),
-        in_specs=[VM] * 8,
-        out_specs=(VM,) * 14,
+        in_specs=[VM] * 10,
+        out_specs=(VM,) * 15,
         scratch_shapes=[
-            pltpu.VMEM((KEYS, D), BF), pltpu.VMEM((KEYS, D), BF), pltpu.VMEM((HC, D), BF), pltpu.VMEM((320, FF // 2), BF),
-            pltpu.SemaphoreType.DMA((140,)), pltpu.SemaphoreType.DMA((140,)),
+            pltpu.VMEM((HC, D), BF), pltpu.VMEM((D, FF // 2), BF), pltpu.VMEM((FF // 2, D), BF), pltpu.VMEM((ROWS, D), BF),
+            pltpu.VMEM((ROWS, HC), BF), pltpu.VMEM((ROWS, FF // 2), BF), pltpu.VMEM((ROWS, FF // 2), BF), pltpu.VMEM((384, D), F32),
+            pltpu.VMEM((ROWS, D), BF), pltpu.VMEM((KEYS, D), BF), pltpu.VMEM((KEYS, D), BF), pltpu.VMEM((HC, D), BF),
+            pltpu.VMEM((320, FF // 2), BF), pltpu.SemaphoreType.DMA((140,)), pltpu.SemaphoreType.DMA((140,)),
         ],
-        compiler_params=pltpu.CompilerParams(collective_id=0, has_side_effects=True, vmem_limit_bytes=60 << 20),
-    )(tokens, small, qkv, out, up, down, jnp.asarray(rotary_table(PROMPT + CONT)), jnp.asarray(index_table(128)))
+        compiler_params=pltpu.CompilerParams(collective_id=0, has_side_effects=True, vmem_limit_bytes=63 << 20),
+    )(tokens, small, qkv, out, up, down, jnp.asarray(rotary_table(PROMPT + CONT)), jnp.asarray(index_table(128)), teacher, cotangent)
 
 
 def add_rows(dst, dst_rows, src, src_rows, count, cols, tile):
@@ -1067,52 +1176,21 @@
             jnp.broadcast_to(prompt_of.astype(F32)[:, None], (1, 128)),
         ]
     )
-    rows, w_qkv, w_out, w_up, w_down, x_own, first_own, second_in, q, kv, attended, lse, activated, slope = forward(
+    rows, w_qkv, x_own, first_own, q, kv, lse, dw_out, dw_down, dw_up, att_grad, joint, output, out_grad, value = forward(
         tokens,
         small,
         qkv_weight.reshape(32, 3, 2, HC).transpose(2, 0, 1, 3).reshape(2, 32, 3 * HC),
         out_weight,
         up_weight.reshape(32, 16, 2, 128).transpose(2, 0, 1, 3).reshape(2, 32, FF // 2),
         down_weight,
+        teacher,
+        cotangent,
     )
-    normed, _ = normalize(x_own.astype(F32))
-    gain1, bias1, gain2, bias2 = (rows[:, 0, 32 * i : 32 * i + 32].reshape(-1) for i in range(4))
-    b_out, b_down = (rows[:, 1, 32 * i : 32 * i + 32].reshape(-1) for i in range(2))
+    gain1 = rows[:, 0, :32].reshape(-1)
     count_all = jnp.sum(rows[:, 4:7])
-    partial = dot(attended, w_out, (1, 0)) + dot(activated, w_down, (1, 0))
-    halves = split_rows(partial)
-    take = lambda a: lax.dynamic_index_in_dim(a, c, axis=0, keepdims=False)
-    give = lambda a: lax.dynamic_index_in_dim(a, 1 - c, axis=0, keepdims=False)
-    output = tokens.astype(F32) + take(halves) + swap_cores(give(halves)) + b_out + b_down
-    live = (valid > 0).astype(F32)[:, None]
-    missed = output - teacher.astype(F32)
-    squared = jnp.sum(live * missed * missed)
-    out_grad = cotangent.astype(F32) + 2.0 / (count_all * D) * live * missed
-    out_low = pair_rows(out_grad.astype(BF))
-    out_bias_grad = jnp.sum(out_grad.astype(BF).astype(F32), axis=0)
-    dw_out = dot(attended, out_low, (0, 0))
-    dw_down = dot(activated, out_low, (0, 0))
-    att_grad = dot(out_low, w_out, (1, 1)).astype(BF)
-    hidden_grad = (dot(out_low, w_down, (1, 1)) * slope).astype(BF)
-    dw_up = dot(second_in, hidden_grad, (0, 0))
-    db_up = jnp.sum(hidden_grad.astype(F32), axis=0)
-    second_grad = dot(hidden_grad, w_up, (1, 1))
-    wide = lambda v: jnp.zeros((v.shape[0], 2, v.shape[1]), F32).at[:, c].set(v).reshape(-1)
-    value = jnp.concatenate(
-        [
-            jnp.zeros((2 * D,), F32),
-            jnp.sum(second_grad * normed, axis=0),
-            jnp.sum(second_grad, axis=0),
-            out_bias_grad,
-            jnp.zeros((3 * D,), F32),
-            wide(db_up.reshape(-1, rd)),
-            jnp.full((128,), squared),
-            jnp.zeros((7 * 128,), F32),
-        ]
-    ).reshape(-1, 128)
     value, s_qkv, s_out, s_up, s_down, joint = backward(
         rows, small, value, gain1[None], jnp.asarray(rotary_table(PROMPT + CONT)), q, kv, att_grad, lse, first_own, x_own,
-        w_qkv, second_grad * gain2, dw_out.astype(BF), dw_down.astype(BF), dw_up.astype(BF),
+        w_qkv, joint, dw_out, dw_down, dw_up,
     )
     own_normed, own_rstd = normalize(tokens.astype(F32))
     input_grad = out_grad + own_rstd * (
@@ -1128,7 +1206,7 @@
         at += size
     loss_value = value[at] / (count_all * D)
     return (
-        output.astype(BF), loss_value, input_grad, shares[0], shares[1], shares[2], shares[3],
+        output, loss_value, input_grad, shares[0], shares[1], shares[2], shares[3],
         s_qkv, shares[5], s_out, shares[4], s_up, shares[6], s_down, shares[4],
     )
 

time: 395 us -> 361 us (0.914)
  Pallas kernels: 294 us -> 330 us
  matrix products: 30.9 us -> 0 us
  between operations: 17.9 us -> 4.09 us
  other arithmetic: 16.8 us -> 6.31 us
  waiting for transfers between devices: 10 us -> 0 us
  local copies, waits for them, and re-layouts: 19.9 us -> 15.8 us
    pallas_call x1, Pallas kernels: 152 us -> 190 us  [forward(): pl.pallas_call(forward_kernel, out_shape=(shape((32, 8, 128), F32), shape...]
    dot_general x8 -> x0, matrix products: 30.9 us -> none  [dot(): lax.dot_general(a, b, ((contract[:1], contract[1:]), ((), ())), preferred...]
    all_gather x1 -> x0, waiting for transfers between devices: 8.58 us -> none  [pair_rows(): both = lax.all_gather(own, 'core', axis=0)]
    reduce_sum x2 -> x0, other arithmetic: 4.77 us -> none  [the longest x1 3.52 us: fast_body(): squared = jnp.sum(live * missed * missed)]
  transfers between devices with their start and end apart: 2 -> 0, of which waited for: 2 -> 0; matrix products, arithmetic and copies ran while one was open for 1% -> 0% of each run, Pallas kernels for 0% -> 0%
where the time goes in v4:
time: 361 us; the launch traced here: 356 us
  Pallas kernels  330 us (91%)
  local copies, waits for them, and re-layouts  15.8 us (4%)
  other arithmetic  6.31 us (2%)
  between operations  4.09 us (1%)
    pallas_call x1, Pallas kernels, forward(): pl.pallas_call(forward_kernel, out_shape=(shape((32, 8, 128), F32), shape...  190 us
    pallas_call x1, Pallas kernels, backward(): pl.pallas_call(backward_kernel, out_shape=(shape((104, 128), F32), shape(...  139 us

profile of v4, /device:TPU:29, one launch (start us, length us, event | category | flops | bytes accessed | tf_op | source)
XLA Modules:
  0.0 355.8 jit_solution(5993322004824745263)
XLA Ops:
  0.6 0.0 copy-start.8
  0.7 0.7 bitcast_convert_fusion
  1.4 0.7 convert_bitcast_fusion
  2.7 0.7 bitcast_convert_fusion.2
  3.5 0.8 maximum_convert_fusion
  4.2 0.6 concatenate.30.small
  4.9 1.1 reshape.133
  6.0 0.8 reshape.134.up
  6.8 0.1 reshape.131
  7.0 0.1 copy.42
  7.1 0.9 reshape.132.qkv
  8.0 190.2 %shard_map.307 = (f32[32,8,128]{2,1,0:T(8,128)}, bf16[1024,1536]{1,0:T(8,128)(2,1)}, bf16[768,1024]{1,0:T(8,128)(2,1)}, bf16[768,1024]{1,0:T(8,128)(2,1)}, bf16[...) custom-call(bf16[384,1024]{1,0:T(8,128)(2,1)} %tokens.1, ...), custom_call_target="tpu_custom_call" | custom-call | tf_op jit(solution)/shard_map/pallas_call | solution.py:796
  198.3 0.9 slice_reduce_fusion.1
  199.2 0.7 broadcast_in_dim_reshape_squeeze.3.gain
  199.9 139.4 %shard_map.308 = (f32[104,128]{1,0:T(8,128)}, f32[32,3072]{1,0:T(8,128)}, f32[32,1024]{1,0:T(8,128)}, f32[32,4096]{1,0:T(8,128)}, f32[128,1024]{1,0:T(8,128)}, /*index=5*/f32[384,1024]{1,0:T(8,128)}) custom-call(f32[32,8,128]{2,1,0:T(8,128)} %get-tuple-element.37.rows, f32[8,128]{1,0:T(8,128)} %concatenate.30.small, f32[104,128]{1,0:T(8,128)} %get-tuple-element.38.value_in, ...), custom_call_target="tpu_custom_call" | custom-call | tf_op jit(solution)/shard_map/pallas_call | solution.py:1136
  339.3 0.2 convert_reduce_fusion
  339.5 0.3 fusion.8
  339.9 0.8 copy-done.1
  340.7 0.5 fusion.10
  341.3 1.7 fusion.7
  343.0 1.4 fusion.11
  344.4 1.3 dynamic_slice.25
  345.6 1.3 dynamic_slice.27
  346.9 1.2 slice.12
  348.1 0.0 copy-done.7
  348.1 0.6 slice_reduce_fusion
  350.0 0.5 copy.50
  350.6 0.9 copy.51
  351.4 0.7 copy.52
  352.2 0.7 copy.53
  352.8 0.8 copy.54
  353.6 0.8 copy.55
  (25 shorter events, 0.1 us)
Async XLA Ops:
  0.6 6.2 %copy-start.8 = (bf16[32,3072]{1,0:T(8,128)(2,1)S(1)}, bf16[32,3072]{1,0:T(8,128)(2,1)}, u32[]{:S(2)}) copy-start(bf16[32,3072]{1,0:T(8,128)(2,1)} %param.29) | copy-start | bytes 589828
  199.9 139.4 %copy-start = (bf16[384,1024]{1,0:T(8,128)(2,1)S(1)}, bf16[384,1024]{1,0:T(8,128)(2,1)}, u32[]{:S(2)}) copy-start(bf16[384,1024]{1,0:T(8,128)(2,1)} %tokens.1) | copy-start | bytes 2359300
  339.3 1.4 copy-start.1
  339.5 1.8 copy-start.2
  341.3 6.8 %copy-start.7 = (f32[32,8,128]{2,1,0:T(8,128)S(1)}, f32[32,8,128]{2,1,0:T(8,128)}, u32[]{:S(2)}) copy-start(f32[32,8,128]{2,1,0:T(8,128)} %get-tuple-element.37.rows) | copy-start | bytes 393220
  341.3 9.3 %copy-start.3 = (bf16[384,1024]{1,0:T(8,128)(2,1)S(1)}, bf16[384,1024]{1,0:T(8,128)(2,1)}, u32[]{:S(2)}) copy-start(bf16[384,1024]{1,0:T(8,128)(2,1)} %get-tuple-element.111) | copy-start | bytes 2359300
  343.0 8.5 %copy-start.6 = (f32[32,3072]{1,0:T(8,128)S(1)}, f32[32,3072]{1,0:T(8,128)}, u32[]{:S(2)}) copy-start(f32[32,3072]{1,0:T(8,128)} %get-tuple-element.118) | copy-start | bytes 1179652
  343.0 9.2 %copy-start.9 = (f32[32,1024]{1,0:T(8,128)S(1)}, f32[32,1024]{1,0:T(8,128)}, u32[]{:S(2)}) copy-start(f32[32,1024]{1,0:T(8,128)} %get-tuple-element.120) | copy-start | bytes 393220
  343.0 9.9 %copy-start.5 = (f32[32,4096]{1,0:T(8,128)S(1)}, f32[32,4096]{1,0:T(8,128)}, u32[]{:S(2)}) copy-start(f32[32,4096]{1,0:T(8,128)} %get-tuple-element.122) | copy-start | bytes 1572868
  344.4 9.3 %copy-start.10 = (f32[32]{0:T(128)}, f32[32]{0:T(128)S(1)}, u32[]{:S(2)}) copy-start(f32[32]{0:T(128)S(1)} %get-tuple-element.121) | copy-start | bytes 388
  350.6 3.1 copy-start.4

commit v5 on v4

--- a/solution.py
+++ b/solution.py
@@ -400,6 +400,7 @@
 
 
 VM = pl.BlockSpec(memory_space=pltpu.VMEM)
+HBM = pl.BlockSpec(memory_space=pl.ANY)
 PROMPT = RANKS * 2 * PSH
 KEYS = 2 * PROMPT + CONT
 ROWS = 4 * PSH + CONT
@@ -506,10 +507,23 @@
     return out[head * HD : head * HD + HD], top + jnp.log(total)
 
 
+GATHER_ORDER = (
+    (0, 0), (0, 1), (6, 0), (6, 0), (1, 0), (0, 2), (0, 3), (1, 1), (6, 0), (2, 0), (6, 0), (6, 0),
+    (2, 1), (6, 0), (6, 0), (6, 0), (1, 2), (0, 4), (4, 0), (1, 3), (3, 0), (6, 0), (6, 0), (2, 2),
+    (5, 0), (0, 5), (2, 3), (3, 1), (1, 4), (4, 1), (6, 0), (6, 0), (5, 1), (0, 6), (4, 2), (1, 5),
+    (2, 4), (3, 2), (6, 0), (6, 0), (3, 3), (5, 2), (0, 7), (2, 5), (6, 0), (1, 6), (4, 3), (6, 0),
+    (3, 4), (1, 7), (0, 8), (2, 6), (5, 3), (4, 4), (3, 5), (2, 7), (5, 4), (0, 9), (4, 5), (1, 8),
+    (3, 6), (6, 0), (6, 0), (6, 0), (6, 0), (6, 0), (6, 0), (3, 7), (2, 8), (6, 0), (6, 0), (5, 5),
+    (0, 10), (6, 0), (1, 9), (0, 11), (6, 0), (6, 0), (6, 0), (6, 0), (6, 0), (3, 8), (2, 9), (6, 0),
+    (6, 0), (6, 0), (1, 10), (1, 11), (6, 0), (6, 0), (6, 0), (3, 9), (6, 0), (6, 0), (2, 10), (2, 11),
+    (6, 0), (6, 0), (6, 0), (6, 0), (3, 10), (3, 11),
+)
+
+
 def forward_kernel(
     tokens, small, qkv, out, up, down, rotary, index, teacher, cotangent,
-    rows, w_qkv, x_own, first_own, q, kv, lse, dw_out, dw_down, dw_up, att_grad, joint, output, out_grad, value,
-    w_out, w_up, w_down, second_in, attended, activated, slope, peer, low, x_all, first_in, spread, swapped, send, recv,
+    rows, h_w_qkv, h_x, h_first, h_q, h_kv, lse, h_dw_out, h_dw_down, h_dw_up, att_grad, joint, output, out_grad, value,
+    w_qkv, x_own, first_own, q, kv, dw_out, dw_down, dw_up, w_out, w_up, w_down, second_in, attended, activated, slope, peer, low, x_all, first_in, spread, swapped, crossed, send, recv, local,
 ):
     net = Net(send, recv)
     c, z, chip = net.c, net.z, net.chip
@@ -518,10 +532,10 @@
         move_rows(x_all, p * PROMPT + z * 2 * PSH + c * PSH, tokens, p * PSH, PSH)
     move_rows(x_all, 2 * PROMPT + c * HALF, tokens, 2 * PSH, HALF)
     rows[chip * 2 + c] = small[...]
-    pieces = [pl.ds(p * PROMPT + z * 2 * PSH + c * PSH, PSH) for p in range(2)]
+    pieces_at = [pl.ds(p * PROMPT + z * 2 * PSH + c * PSH, PSH) for p in range(2)]
     smalls = small_steps(net, rows)
     smalls[0]()
-    mates = [net.same(x_all.at[piece], net.core) for piece in pieces + [pl.ds(2 * PROMPT + c * HALF, HALF)]]
+    mates = [net.same(x_all.at[piece], net.core) for piece in pieces_at + [pl.ds(2 * PROMPT + c * HALF, HALF)]]
     half_rows = pl.ds(pl.multiple_of(chip * 64 + c * 32, 32), 32)
     given = pl.ds(0, 32)
     w_qkv[half_rows, :] = qkv[c]
@@ -539,63 +553,68 @@
     tasks += [gather_steps(net, w_qkv, 64, 512 * i, 512, [] if i else [from_core["qkv"]]) for i in range(3)]
     tasks += [gather_steps(net, spread, 32, 0, 1024, [])]
     tasks += [gather_steps(net, w_down, 128, 256 * i, 256, []) for i in range(4)]
-    clock = [0]
-
-    def advance(until):
-        while clock[0] < until:
-            for t, steps in enumerate(tasks):
-                if (clock[0] - t) % 2 == 0 and 0 <= (clock[0] - t) // 2 < len(steps):
-                    steps[(clock[0] - t) // 2]()
-            clock[0] += 1
-
-    advance(1)
-    smalls[1]()
-    advance(2)
-    smalls[2]()
-    advance(3)
-    smalls[3]()
-    smalls[4]()
-    advance(4)
-    own_tokens = [net.same(x_all.at[piece], peer) for peer in net.line for piece in pieces]
-    places = index.at[c]
-    gain1, bias1, gain2, bias2 = (spread_row(rows, 0, places, 4, 8 + i, D) for i in range(4))
-    b_qkv = spread_row(rows, 2, places, 0, 1, 3 * HC)
-    b_up = spread_row(rows, 3, places, 2, 3, FF // 2)
-    for made in mates:
-        made.wait_recv()
-
-    @pl.loop(0, ROWS // 64)
-    def _(i):
-        prompt = (i // 2) * PROMPT + z * 2 * PSH + (i % 2) * 64
-        here = pl.ds(pl.multiple_of(jnp.where(i < 4, prompt, 2 * PROMPT + (i - 4) * 64), 64), 64)
-        at = tile_at(i, 64)
-        normed = norm_rows(x_all[here, :])
-        x_own[at, :] = x_all[here, :]
-        low = (normed * gain1 + bias1).astype(BF)
-        first_in[here, :] = low
-        first_own[at, :] = low
-        second_in[at, :] = (normed * gain2 + bias2).astype(BF)
-
-    advance(7)
-    for made in own_tokens:
-        made.wait_recv()
-    relays = []
-    for j in (1, 2, 3):
-        for p in range(2):
-            piece = pl.ds(p * PROMPT + (z + j) % RANKS * 2 * PSH + c * PSH, PSH)
-            relays.append(net.same(x_all.at[piece], net.core))
-    advance(8)
-    for made in relays:
-        made.wait_recv()
-
-    @pl.loop(0, 12)
-    def _(i):
-        row = (i // 2 % 2) * PROMPT + (z + 1 + i // 4) % RANKS * 2 * PSH + (i % 2) * 64
-        here = pl.ds(pl.multiple_of(row, 64), 64)
-        first_in[here, :] = (norm_rows(x_all[here, :]) * gain1 + bias1).astype(BF)
+    pieces, done = [], set()
+
+    def after(needs, work, *args):
+        pieces.append((set(needs), work, args))
+
+    def run_pieces(count):
+        while count and pieces and pieces[0][0] <= done:
+            needs, work, args = pieces.pop(0)
+            work(*args)
+            count -= 1
+
+    held = {}
+
+    def learn():
+        for made in mates:
+            made.wait_recv()
+        places = index.at[c]
+        held["norm"] = [spread_row(rows, 0, places, 4, 8 + i, D) for i in range(4)]
+        held["qkv"] = spread_row(rows, 2, places, 0, 1, 3 * HC)
+        held["length"] = jnp.sum(jnp.sum(rows[pl.ds(chip * 2, 2), 5:7, :], axis=0), keepdims=True).astype(jnp.int32)
+        held["up"] = spread_row(rows, 3, places, 2, 3, FF // 2)
+
+    def own_norms(first_tile, count):
+        gain1, bias1, gain2, bias2 = held["norm"]
+
+        @pl.loop(first_tile, first_tile + count)
+        def _(i):
+            prompt = (i // 2) * PROMPT + z * 2 * PSH + (i % 2) * 64
+            here = pl.ds(pl.multiple_of(jnp.where(i < 4, prompt, 2 * PROMPT + (i - 4) * 64), 64), 64)
+            at = tile_at(i, 64)
+            normed = norm_rows(x_all[here, :])
+            x_own[at, :] = x_all[here, :]
+            narrow = (normed * gain1 + bias1).astype(BF)
+            first_in[here, :] = narrow
+            first_own[at, :] = narrow
+            second_in[at, :] = (normed * gain2 + bias2).astype(BF)
+
+    relays = {}
+    prompt_pieces = [(j, p) for j in (1, 2, 3) for p in range(2)]
+
+    def send_tokens(k):
+        j, p = prompt_pieces[k]
+        held[k] = net.same(x_all.at[pieces_at[p]], net.line[j - 1])
+
+    def relay_tokens(k):
+        j, p = prompt_pieces[k]
+        held[k].wait_recv()
+        relays[k] = net.same(x_all.at[pl.ds(p * PROMPT + (z + RANKS - j) % RANKS * 2 * PSH + c * PSH, PSH)], net.core)
+
+    def other_norms(k):
+        j, p = prompt_pieces[k]
+        relays[k].wait_recv()
+        gain1, bias1 = held["norm"][:2]
+
+        @pl.loop(0, 2)
+        def _(i):
+            here = pl.ds(pl.multiple_of(p * PROMPT + (z + RANKS - j) % RANKS * 2 * PSH + i * 64, 64), 64)
+            first_in[here, :] = (norm_rows(x_all[here, :]) * gain1 + bias1).astype(BF)
 
     def hidden(j):
         cols = slice(256 * j, 256 * j + 256)
+        b_up = held["up"]
 
         @pl.loop(0, ROWS // 128)
         def _(i):
@@ -605,45 +624,30 @@
             activated[at, cols] = (pre * gate).astype(BF)
             slope[at, cols] = (gate + pre * jnp.exp(-0.5 * pre * pre) * 0.3989422804014327).astype(slope.dtype)
 
-    advance(9)
-    for j in range(0, 4):
-        hidden(j)
-    advance(10)
-    for j in range(4, 6):
-        hidden(j)
-    advance(11)
-    for j in range(6, 8):
-        hidden(j)
-    advance(12)
-    advance(13)
-
-    @pl.loop(0, KEYS // 256)
-    def _(i):
-        at = tile_at(i, 256)
+    def key_rows(i):
+        at = slice(256 * i, 256 * i + 256)
         here = first_in[at, :]
-        place = pl.multiple_of(jnp.where(i < 4, (i % 2) * 256, PROMPT + (i - 4) * 256), 256)
-        table = rotary[pl.ds(place, 256), :]
+        place = (i % 2) * 256 if i < 4 else PROMPT + (i - 4) * 256
+        table = rotary[place : place + 256, :]
         for j in range(4):
             cols = slice(HC + 256 * j, HC + 256 * j + 256)
-            value = nn(here, w_qkv[:, cols]) + b_qkv[:, cols]
-            kv[at, 256 * j : 256 * j + 256] = (turn(value, table, 1.0) if j < 2 else value).astype(BF)
-
-    @pl.loop(0, ROWS // 128)
-    def _(i):
-        prompt = i * PROMPT + z * 2 * PSH
-        source = pl.multiple_of(jnp.where(i < 2, prompt, 2 * PROMPT + (i - 2) * 128), 128)
-        place = pl.multiple_of(jnp.where(i < 2, z * 2 * PSH, PROMPT + (i - 2) * 128), 128)
-        here = first_in[pl.ds(source, 128), :]
-        table = rotary[pl.ds(place, 128), :]
-        for j in range(2):
-            cols = slice(256 * j, 256 * j + 256)
-            q[tile_at(i, 128), cols] = turn(nn(here, w_qkv[:, cols]) + b_qkv[:, cols], table, 1.0).astype(BF)
-
-    advance(14)
-    length = jnp.sum(jnp.sum(rows[pl.ds(chip * 2, 2), 5:7, :], axis=0), keepdims=True).astype(jnp.int32)
+            made = nn(here, w_qkv[:, cols]) + held["qkv"][:, cols]
+            kv[at, 256 * j : 256 * j + 256] = (turn(made, table, 1.0) if j < 2 else made).astype(BF)
+
+    def query_rows(first_tile, count):
+        @pl.loop(first_tile, first_tile + count)
+        def _(i):
+            place = pl.multiple_of(jnp.where(i < 2, z * 2 * PSH, PROMPT + (i - 2) * 128), 128)
+            at = tile_at(i, 128)
+            here = first_own[at, :]
+            table = rotary[pl.ds(place, 128), :]
+            for j in range(2):
+                cols = slice(256 * j, 256 * j + 256)
+                q[at, cols] = turn(nn(here, w_qkv[:, cols]) + held["qkv"][:, cols], table, 1.0).astype(BF)
+
     second = jnp.broadcast_to(small[7:8, :], (PROMPT, 128)) > 0.5
 
-    def attend_pair(pair):
+    def attend_pair(pair, part):
         k_at, v_at = pl.ds(128 * pair, 128), pl.ds(HC + 128 * pair, 128)
         prompts = [(kv[p * PROMPT : (p + 1) * PROMPT, k_at], kv[p * PROMPT : (p + 1) * PROMPT, v_at]) for p in range(2)]
 
@@ -655,32 +659,68 @@
                 lse[2 * pair + head, :, row : row + size] = stat
             attended[row : row + size, k_at] = jnp.concatenate(outs, axis=0).T.astype(BF)
 
-        for p in range(2):
+        for p in range(2) if part == 0 else ():
             put(p * 128, 128, [prompts[p][0]], [prompts[p][1]], [seen(0, z * 2 * PSH, (PROMPT, 128))])
         chosen = [jnp.where(second, b.astype(F32), a.astype(F32)).astype(BF) for a, b in zip(*prompts)]
-        for i in range(CONT // 128):
+        for i in ((), (0, 1), (2, 3))[part]:
             near = 128 * i + 128
             put(
                 256 + 128 * i, 128,
                 [chosen[0], kv[2 * PROMPT : 2 * PROMPT + near, k_at]],
                 [chosen[1], kv[2 * PROMPT : 2 * PROMPT + near, v_at]],
-                [None, seen(0, 128 * i, (near, 128), length)],
+                [None, seen(0, 128 * i, (near, 128), held["length"])],
             )
 
-    attend_pair(0)
-    advance(15)
-    attend_pair(1)
-    advance(16)
-    attend_pair(2)
-    advance(17)
-    attend_pair(3)
+    after([], smalls[1])
+    after([(0, 1)], smalls[2])
+    after([(1, 0)], smalls[3])
+    after([(2, 0)], smalls[4])
+    after([(2, 0)], learn)
+    for i in range(3):
+        after([], own_norms, 4 * i, 4)
+    for j in range(8):
+        after([(3, j // 2)], hidden, j)
+    for i in range(2):
+        after([(3, 6)], query_rows, 3 * i, 3)
+    for i in range(2):
+        after([(3, 6)], key_rows, 4 + i)
+    for k in range(6):
+        after([(5, k)], other_norms, k)
+    for i in range(4):
+        after([(5, 5)], key_rows, i)
+    for pair in range(4):
+        for part in range(3):
+            after([], attend_pair, pair, part)
+    for event in GATHER_ORDER:
+        step, t = event
+        if step < 4:
+            tasks[t][step]()
+        elif step == 4:
+            send_tokens(t)
+        elif step == 5:
+            relay_tokens(t)
+        else:
+            run_pieces(1)
+        done.add(event)
+    run_pieces(len(pieces))
+    shipped = []
+
+    def ship(src, dst):
+        made = pltpu.make_async_copy(src, dst, local.at[len(shipped)])
+        made.start()
+        shipped.append(made)
+
+    for src, dst in ((w_qkv, h_w_qkv), (x_own, h_x), (first_own, h_first), (q, h_q), (kv, h_kv)):
+        ship(src, dst)
+    length = held["length"]
+    gain2 = held["norm"][2]
+    places = index.at[c]
     given = pl.ds(pl.multiple_of((1 - c) * 256, 256), 256)
-    swap = net.copy(spread.at[given], swapped.at[pl.ds(64, 256), pl.ds(0, D)], net.core)
-    advance(20)
+    swap = net.copy(spread.at[given], crossed, net.core)
     swap.wait_recv()
     for h in range(8):
         w_out[pl.ds(pl.multiple_of(h * 64 + c * 32, 32), 32), :] = spread[pl.ds(pl.multiple_of(c * 256 + h * 32, 32), 32), :]
-        w_out[pl.ds(pl.multiple_of(h * 64 + (1 - c) * 32, 32), 32), :] = swapped[64 + h * 32 : 96 + h * 32, :D]
+        w_out[pl.ds(pl.multiple_of(h * 64 + (1 - c) * 32, 32), 32), :] = crossed[h * 32 : h * 32 + 32, :]
 
     def share(at, size):
         here = pl.ds(pl.multiple_of(at, 128), size)
@@ -745,10 +785,14 @@
         at = tile_at(i, 256)
         dw_down[at, :] = tn(activated[:, at], low[...]).astype(BF)
 
+    ship(dw_down, h_dw_down)
+
     @pl.loop(0, 2)
     def _(i):
         at = tile_at(i, 256)
         dw_out[at, :] = tn(attended[:, at], low[...]).astype(BF)
+
+    ship(dw_out, h_dw_out)
 
     @pl.loop(0, ROWS // 128)
     def _(i):
@@ -774,6 +818,8 @@
         for k in range(2):
             cols = slice(1024 * k, 1024 * k + 1024)
             dw_up[at, cols] = tn(second_in[:, at], activated[:, cols]).astype(BF)
+
+    ship(dw_up, h_dw_up)
 
     def second_rows(i, sums):
         at = tile_at(i, 128)
@@ -788,6 +834,8 @@
     sums = lax.fori_loop(0, ROWS // 128, second_rows, (jnp.zeros((1, D), F32), jnp.zeros((1, D), F32)))
     put_row(16, sums[0])
     put_row(24, sums[1])
+    for made in shipped:
+        made.wait()
     net.leave()
 
 
@@ -801,12 +849,14 @@
             shape((ROWS, HC), BF), shape((ROWS, D), F32), shape((384, D), BF), shape((384, D), F32), shape((104, 128), F32),
         ),
         in_specs=[VM] * 10,
-        out_specs=(VM,) * 15,
+        out_specs=(VM,) + (HBM,) * 5 + (VM,) + (HBM,) * 3 + (VM,) * 5,
         scratch_shapes=[
+            pltpu.VMEM((D, 3 * HC), BF), pltpu.VMEM((ROWS, D), BF), pltpu.VMEM((ROWS, D), BF), pltpu.VMEM((ROWS, HC), BF),
+            pltpu.VMEM((KEYS, 2 * HC), BF), pltpu.VMEM((HC, D), BF), pltpu.VMEM((FF // 2, D), BF), pltpu.VMEM((D, FF // 2), BF),
             pltpu.VMEM((HC, D), BF), pltpu.VMEM((D, FF // 2), BF), pltpu.VMEM((FF // 2, D), BF), pltpu.VMEM((ROWS, D), BF),
             pltpu.VMEM((ROWS, HC), BF), pltpu.VMEM((ROWS, FF // 2), BF), pltpu.VMEM((ROWS, FF // 2), BF), pltpu.VMEM((384, D), F32),
             pltpu.VMEM((ROWS, D), BF), pltpu.VMEM((KEYS, D), BF), pltpu.VMEM((KEYS, D), BF), pltpu.VMEM((HC, D), BF),
-            pltpu.VMEM((320, FF // 2), BF), pltpu.SemaphoreType.DMA((140,)), pltpu.SemaphoreType.DMA((140,)),
+            pltpu.VMEM((64, FF // 2), BF), pltpu.VMEM((256, D), BF), pltpu.SemaphoreType.DMA((140,)), pltpu.SemaphoreType.DMA((140,)), pltpu.SemaphoreType.DMA((8,)),
         ],
         compiler_params=pltpu.CompilerParams(collective_id=0, has_side_effects=True, vmem_limit_bytes=63 << 20),
     )(tokens, small, qkv, out, up, down, jnp.asarray(rotary_table(PROMPT + CONT)), jnp.asarray(index_table(128)), teacher, cotangent)
@@ -924,16 +974,17 @@
 
 
 def backward_kernel(
-    rows, small, value_in, gain, rotary, q, kv, att_grad, lse, first, x, w_qkv, joint_in, dw_out_in, dw_down_in, dw_up_in,
+    rows, small, value_in, gain, rotary, lse, h_q, h_kv, h_att, h_first, h_x, h_w_qkv, h_joint, dw_out_in, dw_down_in, dw_up_in,
     value, o_qkv, o_out, o_up, o_down, joint_own,
-    dw_qkv, dw_out, dw_down, dw_up, spread, pairs, got_pairs, far_k, far_v, projected, joint, peer_joint,
+    q, kv, att_grad, first, x, w_qkv, joint_in, dw_qkv, dw_out, dw_down, dw_up, spread, pairs, got_pairs, far_k, far_v, projected, joint, peer_joint,
     got_s, s_qkv, s_up, peer_qkv, peer_up, *rest,
 ):
     bufs, (send, recv, local) = rest[:-3], rest[-3:]
     net = Net(send, recv)
     c, z, chip = net.c, net.z, net.chip
     loads = [pltpu.make_async_copy(src, dst, local.at[i]) for i, (src, dst) in enumerate(
-        ((dw_down_in, dw_down), (dw_up_in, dw_up), (dw_out_in, dw_out)))]
+        ((dw_down_in, dw_down), (dw_up_in, dw_up), (dw_out_in, dw_out), (h_q, q), (h_kv, kv), (h_att, att_grad),
+         (h_first, first), (h_w_qkv, w_qkv), (h_x, x), (h_joint, joint_in)))]
     for load in loads:
         load.start()
     value[...] = value_in[...]
@@ -1031,6 +1082,8 @@
                     net.copy(pairs.at[pair, there], got_pairs.at[j - 1, pair, pl.ds(p * 2 * PSH, 2 * PSH)], net.line[j - 1])
                 )
 
+    for load in loads[3:6]:
+        load.wait()
     back_pair(0)
     advance(3)
     back_pair(1)
@@ -1059,6 +1112,8 @@
             part = tn(first[:, tile_at(i, 256)], projected[:, col : col + width])
             dw_qkv[tile_at(i, 256), col : col + width] = part.astype(BF)
 
+    for load in loads[6:]:
+        load.wait()
     weight_columns(0, 768)
     tasks.append((6, scatter_steps(net, dw_qkv, 64, 0, 768, [], *take3(), put_into(s_qkv))))
     advance(7)
@@ -1139,16 +1194,18 @@
             shape((104, 128), F32), shape((32, 3 * D), F32), shape((32, D), F32), shape((32, FF), F32), shape((128, D), F32),
             shape((384, D), F32),
         ),
-        in_specs=[VM] * 13 + [pl.BlockSpec(memory_space=pl.ANY)] * 3,
+        in_specs=[VM] * 6 + [HBM] * 10,
         out_specs=(VM,) * 6,
         scratch_shapes=[
+            pltpu.VMEM((ROWS, HC), BF), pltpu.VMEM((KEYS, 2 * HC), BF), pltpu.VMEM((ROWS, HC), BF), pltpu.VMEM((ROWS, D), BF),
+            pltpu.VMEM((ROWS, D), BF), pltpu.VMEM((D, 3 * HC), BF), pltpu.VMEM((ROWS, D), F32),
             pltpu.VMEM((D, 3 * HC), BF), pltpu.VMEM((HC, D), BF), pltpu.VMEM((FF // 2, D), BF), pltpu.VMEM((D, FF // 2), BF),
             pltpu.VMEM((HC, D), BF), pltpu.VMEM((4, 2 * PROMPT, 256), BF), pltpu.VMEM((3, 4, 4 * PSH, 256), BF),
             pltpu.VMEM((PROMPT, 128), F32), pltpu.VMEM((PROMPT, 128), F32), pltpu.VMEM((ROWS, 3 * HC), BF),
             pltpu.VMEM((ROWS, D), F32), pltpu.VMEM((384, D), F32), pltpu.VMEM((7, 104, 128), F32),
             pltpu.VMEM((64, 3 * HC), F32), pltpu.VMEM((64, FF // 2), F32), pltpu.VMEM((32, 3 * HC), F32), pltpu.VMEM((32, FF // 2), F32),
         ] + bufs
-        + [pltpu.SemaphoreType.DMA((140,)), pltpu.SemaphoreType.DMA((140,)), pltpu.SemaphoreType.DMA((4,))],
+        + [pltpu.SemaphoreType.DMA((140,)), pltpu.SemaphoreType.DMA((140,)), pltpu.SemaphoreType.DMA((10,))],
         compiler_params=pltpu.CompilerParams(collective_id=1, has_side_effects=True, vmem_limit_bytes=63 << 20),
     )(*args)
 
@@ -1189,7 +1246,7 @@
     gain1 = rows[:, 0, :32].reshape(-1)
     count_all = jnp.sum(rows[:, 4:7])
     value, s_qkv, s_out, s_up, s_down, joint = backward(
-        rows, small, value, gain1[None], jnp.asarray(rotary_table(PROMPT + CONT)), q, kv, att_grad, lse, first_own, x_own,
+        rows, small, value, gain1[None], jnp.asarray(rotary_table(PROMPT + CONT)), lse, q, kv, att_grad, first_own, x_own,
         w_qkv, joint, dw_out, dw_down, dw_up,
     )
     own_normed, own_rstd = normalize(tokens.astype(F32))

time: 361 us -> 344 us (0.953)
  Pallas kernels: 330 us -> 312 us
    pallas_call x1, Pallas kernels: 190 us -> 173 us  [forward(): pl.pallas_call(forward_kernel, out_shape=(shape((32, 8, 128), F32), shape...]
where the time goes in v5:
time: 344 us; the launch traced here: 338 us
  Pallas kernels  312 us (91%)
  local copies, waits for them, and re-layouts  15.8 us (5%)
  other arithmetic  6.31 us (2%)
  between operations  4.01 us (1%)
    pallas_call x1, Pallas kernels, forward(): pl.pallas_call(forward_kernel, out_shape=(shape((32, 8, 128), F32), shape...  173 us
    pallas_call x1, Pallas kernels, backward(): pl.pallas_call(backward_kernel, out_shape=(shape((104, 128), F32), shape(...  139 us

profile of v5, /device:TPU:29, one launch (start us, length us, event | category | flops | bytes accessed | tf_op | source)
XLA Modules:
  0.0 338.4 jit_solution(14952191897122408186)
XLA Ops:
  0.7 0.7 bitcast_convert_fusion
  1.4 0.7 convert_bitcast_fusion
  2.7 0.7 bitcast_convert_fusion.2
  3.5 0.8 maximum_convert_fusion
  4.2 0.6 concatenate.30.small
  4.9 1.1 reshape.133
  6.0 0.8 reshape.134.up
  6.8 0.1 reshape.131
  7.0 0.1 copy.42
  7.1 0.9 reshape.132.qkv
  8.0 173.5 %shard_map.307 = (f32[32,8,128]{2,1,0:T(8,128)}, bf16[1024,1536]{1,0:T(8,128)(2,1)}, bf16[768,1024]{1,0:T(8,128)(2,1)}, bf16[768,1024]{1,0:T(8,128)(2,1)}, bf16[...) custom-call(bf16[384,1024]{1,0:T(8,128)(2,1)} %tokens.1, ...), custom_call_target="tpu_custom_call" | custom-call | tf_op jit(solution)/shard_map/pallas_call | solution.py:844
  181.5 0.9 slice_reduce_fusion.1
  182.5 0.7 broadcast_in_dim_reshape_squeeze.3.gain
  183.2 138.8 %shard_map.308 = (f32[104,128]{1,0:T(8,128)}, f32[32,3072]{1,0:T(8,128)}, f32[32,1024]{1,0:T(8,128)}, f32[32,4096]{1,0:T(8,128)}, f32[128,1024]{1,0:T(8,128)}, /*index=5*/f32[384,1024]{1,0:T(8,128)}) custom-call(f32[32,8,128]{2,1,0:T(8,128)} %get-tuple-element.37.rows, f32[8,128]{1,0:T(8,128)} %concatenate.30.small, f32[104,128]{1,0:T(8,128)} %get-tuple-element.38.value_in, ...), custom_call_target="tpu_custom_call" | custom-call | tf_op jit(solution)/shard_map/pallas_call | solution.py:1191
  322.0 0.2 convert_reduce_fusion
  322.2 0.3 fusion.8
  322.5 0.8 copy-done.1
  323.4 0.5 fusion.10
  324.0 1.7 fusion.7
  325.6 1.4 fusion.11
  327.0 1.3 dynamic_slice.25
  328.3 1.3 dynamic_slice.27
  329.6 1.2 slice.12
  330.8 0.6 slice_reduce_fusion
  332.7 0.5 copy.50
  333.2 0.0 copy-done.3
  333.2 0.9 copy.51
  334.1 0.0 copy-done.6
  334.1 0.7 copy.52
  334.8 0.7 copy.53
  335.5 0.8 copy.54
  336.3 0.8 copy.55
  (25 shorter events, 0.1 us)
Async XLA Ops:
  0.6 6.2 %copy-start.8 = (bf16[32,3072]{1,0:T(8,128)(2,1)S(1)}, bf16[32,3072]{1,0:T(8,128)(2,1)}, u32[]{:S(2)}) copy-start(bf16[32,3072]{1,0:T(8,128)(2,1)} %param.29) | copy-start | bytes 589828
  183.2 138.8 %copy-start = (bf16[384,1024]{1,0:T(8,128)(2,1)S(1)}, bf16[384,1024]{1,0:T(8,128)(2,1)}, u32[]{:S(2)}) copy-start(bf16[384,1024]{1,0:T(8,128)(2,1)} %tokens.1) | copy-start | bytes 2359300
  322.0 1.4 copy-start.1
  322.2 1.8 copy-start.2
  323.9 6.8 %copy-start.7 = (f32[32,8,128]{2,1,0:T(8,128)S(1)}, f32[32,8,128]{2,1,0:T(8,128)}, u32[]{:S(2)}) copy-start(f32[32,8,128]{2,1,0:T(8,128)} %get-tuple-element.37.rows) | copy-start | bytes 393220
  324.0 9.3 %copy-start.3 = (bf16[384,1024]{1,0:T(8,128)(2,1)S(1)}, bf16[384,1024]{1,0:T(8,128)(2,1)}, u32[]{:S(2)}) copy-start(bf16[384,1024]{1,0:T(8,128)(2,1)} %get-tuple-element.111) | copy-start | bytes 2359300
  325.6 8.5 %copy-start.6 = (f32[32,3072]{1,0:T(8,128)S(1)}, f32[32,3072]{1,0:T(8,128)}, u32[]{:S(2)}) copy-start(f32[32,3072]{1,0:T(8,128)} %get-tuple-element.118) | copy-start | bytes 1179652
  325.6 9.2 %copy-start.9 = (f32[32,1024]{1,0:T(8,128)S(1)}, f32[32,1024]{1,0:T(8,128)}, u32[]{:S(2)}) copy-start(f32[32,1024]{1,0:T(8,128)} %get-tuple-element.120) | copy-start | bytes 393220
  325.6 9.9 %copy-start.5 = (f32[32,4096]{1,0:T(8,128)S(1)}, f32[32,4096]{1,0:T(8,128)}, u32[]{:S(2)}) copy-start(f32[32,4096]{1,0:T(8,128)} %get-tuple-element.122) | copy-start | bytes 1572868
  327.0 9.3 %copy-start.10 = (f32[32]{0:T(128)}, f32[32]{0:T(128)S(1)}, u32[]{:S(2)}) copy-start(f32[32]{0:T(128)S(1)} %get-tuple-element.121) | copy-start | bytes 388
  333.2 3.1 copy-start.4

commit v6 on v5

--- a/solution.py
+++ b/solution.py
@@ -538,13 +538,17 @@
     mates = [net.same(x_all.at[piece], net.core) for piece in pieces_at + [pl.ds(2 * PROMPT + c * HALF, HALF)]]
     half_rows = pl.ds(pl.multiple_of(chip * 64 + c * 32, 32), 32)
     given = pl.ds(0, 32)
-    w_qkv[half_rows, :] = qkv[c]
-    swapped[given, : 3 * HC] = qkv[1 - c]
+    for i in range(3):
+        cols = slice(HC * i, HC * i + HC)
+        w_qkv[half_rows, cols] = qkv[:, pl.ds(pl.multiple_of(i * D + c * HC, 128), HC)]
+        swapped[given, cols] = qkv[:, pl.ds(pl.multiple_of(i * D + (1 - c) * HC, 128), HC)]
     from_core = {}
     from_core["qkv"] = net.copy(swapped.at[given, pl.ds(0, 3 * HC)], w_qkv.at[half_rows], net.core)
-    w_up[half_rows, :] = up[c]
     given = pl.ds(32, 32)
-    swapped[given, : FF // 2] = up[1 - c]
+    for i in range(16):
+        cols = slice(128 * i, 128 * i + 128)
+        w_up[half_rows, cols] = up[:, pl.ds(pl.multiple_of((2 * i + c) * 128, 128), 128)]
+        swapped[given, cols] = up[:, pl.ds(pl.multiple_of((2 * i + 1 - c) * 128, 128), 128)]
     from_core["up"] = net.copy(swapped.at[given, pl.ds(0, FF // 2)], w_up.at[half_rows], net.core)
     w_down[pl.ds(pl.multiple_of(chip * 128, 128), 128), :] = down[...]
     spread[pl.ds(pl.multiple_of(chip * 32, 32), 32), :] = out[...]
@@ -1236,9 +1240,9 @@
     rows, w_qkv, x_own, first_own, q, kv, lse, dw_out, dw_down, dw_up, att_grad, joint, output, out_grad, value = forward(
         tokens,
         small,
-        qkv_weight.reshape(32, 3, 2, HC).transpose(2, 0, 1, 3).reshape(2, 32, 3 * HC),
+        qkv_weight,
         out_weight,
-        up_weight.reshape(32, 16, 2, 128).transpose(2, 0, 1, 3).reshape(2, 32, FF // 2),
+        up_weight,
         down_weight,
         teacher,
         cotangent,
@@ -1255,13 +1259,10 @@
         - jnp.mean(joint, axis=-1, keepdims=True)
         - own_normed * jnp.mean(joint * own_normed, axis=-1, keepdims=True)
     )
-    value = value.reshape(-1)
-    shares, at = [], 0
-    for size in (D, D, D, D, D, 3 * D, FF):
-        own = size // lax.axis_size(ALL)
-        shares.append(lax.dynamic_slice_in_dim(value, at + device * own, own))
-        at += size
-    loss_value = value[at] / (count_all * D)
+    pick = lambda part, own: lax.dynamic_index_in_dim(part.reshape(-1, own), device, axis=0, keepdims=False)
+    five = lax.dynamic_index_in_dim(value[:40].reshape(5, 32, 32), device, axis=1, keepdims=False)
+    shares = [five[i] for i in range(5)] + [pick(value[40:64], 96), pick(value[64:96], 128)]
+    loss_value = value[96, 0] / (count_all * D)
     return (
         output, loss_value, input_grad, shares[0], shares[1], shares[2], shares[3],
         s_qkv, shares[5], s_out, shares[4], s_up, shares[6], s_down, shares[4],

time: 344 us -> 337 us (0.980)
  local copies, waits for them, and re-layouts: 15.8 us -> 9.74 us
    dynamic_slice x3 -> x0, local copies, waits for them, and re-layouts: 3.93 us -> none  [fast_body(): shares.append(lax.dynamic_slice_in_dim(value, at + device * own, own))]
where the time goes in v6:
time: 337 us; the launch traced here: 332 us
  Pallas kernels  312 us (93%)
  local copies, waits for them, and re-layouts  9.74 us (3%)
  other arithmetic  6.27 us (2%)
  between operations  4 us (1%)
    pallas_call x1, Pallas kernels, forward(): pl.pallas_call(forward_kernel, out_shape=(shape((32, 8, 128), F32), shape...  173 us
    pallas_call x1, Pallas kernels, backward(): pl.pallas_call(backward_kernel, out_shape=(shape((104, 128), F32), shape(...  139 us

profile of v6, /device:TPU:29, one launch (start us, length us, event | category | flops | bytes accessed | tf_op | source)
XLA Modules:
  0.0 332.3 jit_solution(13500702578955198770)
XLA Ops:
  0.6 0.7 bitcast_convert_fusion
  1.3 0.7 convert_bitcast_fusion
  2.7 0.7 bitcast_convert_fusion.2
  3.4 0.8 maximum_convert_fusion
  4.2 0.6 concatenate.30.small
  4.8 173.5 %shard_map.307 = (f32[32,8,128]{2,1,0:T(8,128)}, bf16[1024,1536]{1,0:T(8,128)(2,1)}, bf16[768,1024]{1,0:T(8,128)(2,1)}, bf16[768,1024]{1,0:T(8,128)(2,1)}, bf16[...) custom-call(bf16[384,1024]{1,0:T(8,128)(2,1)} %tokens.1, ...), custom_call_target="tpu_custom_call" | custom-call | tf_op jit(solution)/shard_map/pallas_call | solution.py:848
  178.3 0.9 slice_reduce_fusion.1
  179.3 0.7 broadcast_in_dim_reshape_squeeze.3.gain
  179.9 138.8 %shard_map.308 = (f32[104,128]{1,0:T(8,128)}, f32[32,3072]{1,0:T(8,128)}, f32[32,1024]{1,0:T(8,128)}, f32[32,4096]{1,0:T(8,128)}, f32[128,1024]{1,0:T(8,128)}, /*index=5*/f32[384,1024]{1,0:T(8,128)}) custom-call(f32[32,8,128]{2,1,0:T(8,128)} %get-tuple-element.37.rows, f32[8,128]{1,0:T(8,128)} %concatenate.30.small, f32[104,128]{1,0:T(8,128)} %get-tuple-element.38.value_in, ...), custom_call_target="tpu_custom_call" | custom-call | tf_op jit(solution)/shard_map/pallas_call | solution.py:1195
  318.8 0.0 copy-start.1
  318.8 0.0 copy-done
  318.8 0.2 convert_reduce_fusion
  319.0 0.3 fusion.8
  319.3 0.8 copy-done.1
  320.2 0.5 fusion.17
  320.7 0.0 copy-done.2
  320.7 0.0 copy-start.9
  320.7 0.0 copy-start.7
  320.8 1.7 fusion.7
  322.4 0.1 reshape.132
  322.5 0.5 fusion.10
  323.1 0.1 reshape.133
  323.1 0.5 fusion.11
  323.7 0.5 fusion.12
  324.2 0.5 slice.39
  324.7 0.6 slice_reduce_fusion
  326.6 0.5 copy.42
  327.1 0.9 copy.43
  328.0 0.7 copy.44
  328.8 0.7 copy.45
  329.4 0.8 copy.46
  330.2 0.8 copy.47
  (24 shorter events, 0.1 us)
Async XLA Ops:
  179.9 138.8 %copy-start = (bf16[384,1024]{1,0:T(8,128)(2,1)S(1)}, bf16[384,1024]{1,0:T(8,128)(2,1)}, u32[]{:S(2)}) copy-start(bf16[384,1024]{1,0:T(8,128)(2,1)} %tokens.1) | copy-start | bytes 2359300
  318.8 1.4 copy-start.1
  319.0 1.8 copy-start.2
  320.7 1.7 copy-start.9
  320.7 3.9 %copy-start.7 = (f32[32,8,128]{2,1,0:T(8,128)S(1)}, f32[32,8,128]{2,1,0:T(8,128)}, u32[]{:S(2)}) copy-start(f32[32,8,128]{2,1,0:T(8,128)} %get-tuple-element.37.rows) | copy-start | bytes 393220
  320.8 6.4 %copy-start.3 = (bf16[384,1024]{1,0:T(8,128)(2,1)S(1)}, bf16[384,1024]{1,0:T(8,128)(2,1)}, u32[]{:S(2)}) copy-start(bf16[384,1024]{1,0:T(8,128)(2,1)} %get-tuple-element.111) | copy-start | bytes 2359300
  322.4 5.6 %copy-start.6 = (f32[32,3072]{1,0:T(8,128)S(1)}, f32[32,3072]{1,0:T(8,128)}, u32[]{:S(2)}) copy-start(f32[32,3072]{1,0:T(8,128)} %get-tuple-element.118) | copy-start | bytes 1179652
  322.4 6.4 %copy-start.8 = (f32[32,1024]{1,0:T(8,128)S(1)}, f32[32,1024]{1,0:T(8,128)}, u32[]{:S(2)}) copy-start(f32[32,1024]{1,0:T(8,128)} %get-tuple-element.120) | copy-start | bytes 393220
  322.4 7.0 %copy-start.5 = (f32[32,4096]{1,0:T(8,128)S(1)}, f32[32,4096]{1,0:T(8,128)}, u32[]{:S(2)}) copy-start(f32[32,4096]{1,0:T(8,128)} %get-tuple-element.122) | copy-start | bytes 1572868
  323.1 7.2 %copy-start.10 = (f32[32]{0:T(128)}, f32[32]{0:T(128)S(1)}, u32[]{:S(2)}) copy-start(f32[32]{0:T(128)S(1)} %get-tuple-element.121) | copy-start | bytes 388
  327.1 3.1 copy-start.4

commit v7 on v6

--- a/solution.py
+++ b/solution.py
@@ -521,12 +521,18 @@
 
 
 def forward_kernel(
-    tokens, small, qkv, out, up, down, rotary, index, teacher, cotangent,
-    rows, h_w_qkv, h_x, h_first, h_q, h_kv, lse, h_dw_out, h_dw_down, h_dw_up, att_grad, joint, output, out_grad, value,
-    w_qkv, x_own, first_own, q, kv, dw_out, dw_down, dw_up, w_out, w_up, w_down, second_in, attended, activated, slope, peer, low, x_all, first_in, spread, swapped, crossed, send, recv, local,
+    tokens, small, qkv, out, up, down, h_rotary, index, h_teacher, h_cotangent,
+    rows, h_w_qkv, h_x, h_first, h_q, h_kv, lse, h_dw_out, h_dw_down, h_dw_up, h_att, joint, h_output, h_out_grad, value,
+    rotary, teacher, cotangent, att_grad, output, out_grad, w_qkv, x_own, first_own, q, kv, dw_out, dw_down, dw_up, w_out, w_up, w_down, second_in, attended, activated, slope, peer, low, x_all, first_in, spread, swapped, crossed, send, recv, local,
 ):
     net = Net(send, recv)
     c, z, chip = net.c, net.z, net.chip
+    loads = [
+        pltpu.make_async_copy(src, dst, local.at[11 + i])
+        for i, (src, dst) in enumerate(((h_rotary, rotary), (h_teacher, teacher), (h_cotangent, cotangent)))
+    ]
+    for load in loads:
+        load.start()
     net.enter()
     for p in range(2):
         move_rows(x_all, p * PROMPT + z * 2 * PSH + c * PSH, tokens, p * PSH, PSH)
@@ -571,6 +577,8 @@
     held = {}
 
     def learn():
+        for load in loads:
+            load.wait()
         for made in mates:
             made.wait_recv()
         places = index.at[c]
@@ -780,6 +788,8 @@
         for k in range(vector.shape[1] // 128):
             value[row + k : row + k + 1, :] = vector[:, 128 * k : 128 * k + 128]
 
+    ship(output, h_output)
+    ship(out_grad, h_out_grad)
     put_row(32, low_sum)
     for made in lows:
         made.wait_recv()
@@ -802,6 +812,8 @@
     def _(i):
         at = tile_at(i, 128)
         att_grad[at, :] = nt(low[at, :], w_out[...]).astype(BF)
+
+    ship(att_grad, h_att)
 
     for j in range(8):
         cols = slice(256 * j, 256 * j + 256)
@@ -852,15 +864,17 @@
             shape((KEYS, 2 * HC), BF), shape((8, 1, ROWS), F32), shape((HC, D), BF), shape((FF // 2, D), BF), shape((D, FF // 2), BF),
             shape((ROWS, HC), BF), shape((ROWS, D), F32), shape((384, D), BF), shape((384, D), F32), shape((104, 128), F32),
         ),
-        in_specs=[VM] * 10,
-        out_specs=(VM,) + (HBM,) * 5 + (VM,) + (HBM,) * 3 + (VM,) * 5,
+        in_specs=[VM] * 6 + [HBM, VM, HBM, HBM],
+        out_specs=(VM,) + (HBM,) * 5 + (VM,) + (HBM,) * 4 + (VM,) + (HBM,) * 2 + (VM,),
         scratch_shapes=[
+            pltpu.VMEM((PROMPT + CONT, 384), F32), pltpu.VMEM((384, D), BF), pltpu.VMEM((384, D), BF),
+            pltpu.VMEM((ROWS, HC), BF), pltpu.VMEM((384, D), BF), pltpu.VMEM((384, D), F32),
             pltpu.VMEM((D, 3 * HC), BF), pltpu.VMEM((ROWS, D), BF), pltpu.VMEM((ROWS, D), BF), pltpu.VMEM((ROWS, HC), BF),
             pltpu.VMEM((KEYS, 2 * HC), BF), pltpu.VMEM((HC, D), BF), pltpu.VMEM((FF // 2, D), BF), pltpu.VMEM((D, FF // 2), BF),
             pltpu.VMEM((HC, D), BF), pltpu.VMEM((D, FF // 2), BF), pltpu.VMEM((FF // 2, D), BF), pltpu.VMEM((ROWS, D), BF),
             pltpu.VMEM((ROWS, HC), BF), pltpu.VMEM((ROWS, FF // 2), BF), pltpu.VMEM((ROWS, FF // 2), BF), pltpu.VMEM((384, D), F32),
             pltpu.VMEM((ROWS, D), BF), pltpu.VMEM((KEYS, D), BF), pltpu.VMEM((KEYS, D), BF), pltpu.VMEM((HC, D), BF),
-            pltpu.VMEM((64, FF // 2), BF), pltpu.VMEM((256, D), BF), pltpu.SemaphoreType.DMA((140,)), pltpu.SemaphoreType.DMA((140,)), pltpu.SemaphoreType.DMA((8,)),
+            pltpu.VMEM((64, FF // 2), BF), pltpu.VMEM((256, D), BF), pltpu.SemaphoreType.DMA((140,)), pltpu.SemaphoreType.DMA((140,)), pltpu.SemaphoreType.DMA((14,)),
         ],
         compiler_params=pltpu.CompilerParams(collective_id=0, has_side_effects=True, vmem_limit_bytes=63 << 20),
     )(tokens, small, qkv, out, up, down, jnp.asarray(rotary_table(PROMPT + CONT)), jnp.asarray(index_table(128)), teacher, cotangent)

time: 337 us -> 335 us (level)
  no operation moved by 1% of the time
where the time goes in v7:
time: 335 us; the launch traced here: 330 us
  Pallas kernels  310 us (93%)
  local copies, waits for them, and re-layouts  9.74 us (3%)
  other arithmetic  6.27 us (2%)
  between operations  4 us (1%)
    pallas_call x1, Pallas kernels, forward(): pl.pallas_call(forward_kernel, out_shape=(shape((32, 8, 128), F32), shape...  172 us
    pallas_call x1, Pallas kernels, backward(): pl.pallas_call(backward_kernel, out_shape=(shape((104, 128), F32), shape(...  139 us

profile of v7, /device:TPU:29, one launch (start us, length us, event | category | flops | bytes accessed | tf_op | source)
XLA Modules:
  0.0 330.3 jit_solution(7123315260764647398)
XLA Ops:
  0.6 0.7 bitcast_convert_fusion
  1.3 0.7 convert_bitcast_fusion
  2.7 0.7 bitcast_convert_fusion.2
  3.4 0.8 maximum_convert_fusion
  4.2 0.6 concatenate.30.small
  4.8 171.5 %shard_map.307 = (f32[32,8,128]{2,1,0:T(8,128)}, bf16[1024,1536]{1,0:T(8,128)(2,1)}, bf16[768,1024]{1,0:T(8,128)(2,1)}, bf16[768,1024]{1,0:T(8,128)(2,1)}, bf16[...) custom-call(bf16[384,1024]{1,0:T(8,128)(2,1)} %tokens.1, ...), custom_call_target="tpu_custom_call" | custom-call | tf_op jit(solution)/shard_map/pallas_call | solution.py:860
  176.4 0.9 slice_reduce_fusion.1
  177.3 0.7 broadcast_in_dim_reshape_squeeze.3.gain
  178.0 138.8 %shard_map.308 = (f32[104,128]{1,0:T(8,128)}, f32[32,3072]{1,0:T(8,128)}, f32[32,1024]{1,0:T(8,128)}, f32[32,4096]{1,0:T(8,128)}, f32[128,1024]{1,0:T(8,128)}, /*index=5*/f32[384,1024]{1,0:T(8,128)}) custom-call(f32[32,8,128]{2,1,0:T(8,128)} %get-tuple-element.37.rows, f32[8,128]{1,0:T(8,128)} %concatenate.30.small, f32[104,128]{1,0:T(8,128)} %get-tuple-element.38.value_in, ...), custom_call_target="tpu_custom_call" | custom-call | tf_op jit(solution)/shard_map/pallas_call | solution.py:1209
  316.8 0.0 copy-start.1
  316.8 0.0 copy-done
  316.8 0.2 convert_reduce_fusion
  317.0 0.3 fusion.8
  317.4 0.8 copy-done.1
  318.2 0.5 fusion.17
  318.8 0.0 copy-done.2
  318.8 0.0 copy-start.9
  318.8 0.0 copy-start.7
  318.8 1.7 fusion.7
  320.5 0.1 reshape.132
  320.5 0.5 fusion.10
  321.1 0.1 reshape.133
  321.2 0.5 fusion.11
  321.7 0.5 fusion.12
  322.2 0.5 slice.39
  322.7 0.6 slice_reduce_fusion
  324.7 0.5 copy.42
  325.2 0.9 copy.43
  326.1 0.7 copy.44
  326.8 0.7 copy.45
  327.5 0.8 copy.46
  328.3 0.8 copy.47
  (24 shorter events, 0.1 us)
Async XLA Ops:
  178.0 138.8 %copy-start = (bf16[384,1024]{1,0:T(8,128)(2,1)S(1)}, bf16[384,1024]{1,0:T(8,128)(2,1)}, u32[]{:S(2)}) copy-start(bf16[384,1024]{1,0:T(8,128)(2,1)} %tokens.1) | copy-start | bytes 2359300
  316.8 1.4 copy-start.1
  317.0 1.8 copy-start.2
  318.8 1.7 copy-start.9
  318.8 3.9 %copy-start.7 = (f32[32,8,128]{2,1,0:T(8,128)S(1)}, f32[32,8,128]{2,1,0:T(8,128)}, u32[]{:S(2)}) copy-start(f32[32,8,128]{2,1,0:T(8,128)} %get-tuple-element.37.rows) | copy-start | bytes 393220
  318.8 6.4 %copy-start.3 = (bf16[384,1024]{1,0:T(8,128)(2,1)S(1)}, bf16[384,1024]{1,0:T(8,128)(2,1)}, u32[]{:S(2)}) copy-start(bf16[384,1024]{1,0:T(8,128)(2,1)} %get-tuple-element.111) | copy-start | bytes 2359300
  320.4 5.6 %copy-start.6 = (f32[32,3072]{1,0:T(8,128)S(1)}, f32[32,3072]{1,0:T(8,128)}, u32[]{:S(2)}) copy-start(f32[32,3072]{1,0:T(8,128)} %get-tuple-element.118) | copy-start | bytes 1179652
  320.4 6.4 %copy-start.8 = (f32[32,1024]{1,0:T(8,128)S(1)}, f32[32,1024]{1,0:T(8,128)}, u32[]{:S(2)}) copy-start(f32[32,1024]{1,0:T(8,128)} %get-tuple-element.120) | copy-start | bytes 393220
  320.5 7.0 %copy-start.5 = (f32[32,4096]{1,0:T(8,128)S(1)}, f32[32,4096]{1,0:T(8,128)}, u32[]{:S(2)}) copy-start(f32[32,4096]{1,0:T(8,128)} %get-tuple-element.122) | copy-start | bytes 1572868
  321.1 7.2 %copy-start.10 = (f32[32]{0:T(128)}, f32[32]{0:T(128)S(1)}, u32[]{:S(2)}) copy-start(f32[32]{0:T(128)S(1)} %get-tuple-element.121) | copy-start | bytes 388
  325.2 3.1 copy-start.4
